TPU v7x, 128 devices: a whole 4x4x4 slice. The times are simulated.
128 devices in a mesh: grp: 8 (over x, y_hi), dp: 16 (over z, y_lo, core).
Axes of the slice: x: 4, y: 4 (y_hi: 2, y_lo: 2; y = y_hi * 2 + y_lo), z: 4, core: 2. Of those that a mesh axis runs over, the one named last changes fastest.
Arguments:
- queries: bfloat16 [16, 2048, 1280], P('dp', 'grp'), may hold values from -8 to 8
- keys_in: bfloat16 [16, 2048, 1280], P('dp', 'grp'), may hold values from -8 to 8
- value_rows: bfloat16 [16, 2048, 1280], P('dp', 'grp'), may hold values from -6 to 6
- grad_out: bfloat16 [16, 2048, 1280], P('dp', 'grp'), may hold values from -6 to 6
- out_weight: bfloat16 [1280, 1280], replicated, may hold values from -0.15625 to 0.15625
- image_ids: int32 [16, 16], P('dp'), may hold values from 0 to 3, never falling along the last dimension, each value on 1 to 12 neighbouring positions
Outputs:
- grad_queries: bfloat16 [16, 2048, 1280], P('dp', 'grp')
- grad_keys: bfloat16 [16, 2048, 1280], P('dp', 'grp')
- grad_values: bfloat16 [16, 2048, 1280], P('dp', 'grp')
- grad_weight: float32 [1280, 1280], replicated
Inputs may be any that keep to these rules, and one draw needn't show every extreme that they name: `image_ids`: image numbers never fall along a sequence; each sequence holds 4 images of 1 to 12 blocks, one of exactly that many.
All inputs are finite; a program needn't handle non-finite values.
Results may differ from a plain program's by a relative error of at most 0.011.
Values may be sent and summed in bfloat16 or wider, within the bound.
No kernel may reach another device: no remote copies, remote signals or barrier semaphores. Data moves between devices by JAX's collectives and lax.ppermute only.
A program may use at most 128 MiB of HBM per device.

v0:
```python
import math

import jax
import jax.numpy as jnp
from jax import lax
from jax.sharding import PartitionSpec as P

HEADS = 16
BLK = 128


def inner(left, right):
    return lax.dot_general(
        left, right, (((1,), (1,)), ((), ())), preferred_element_type=jnp.float32
    )


def outer(left, right):
    return lax.dot_general(
        left, right, (((0,), (0,)), ((), ())), preferred_element_type=jnp.float32
    )


def head_grads(query_h, key_h, value_h, attn_h, query_ids, key_ids):
    scaling = 1.0 / math.sqrt(query_h.shape[-1])
    scores = inner(query_h, key_h) * scaling
    same_image = query_ids[:, None] == key_ids[None, :]
    masked = jnp.where(same_image, scores, -1e30)
    row_max = jnp.max(masked, axis=1, keepdims=True)
    weights_raw = jnp.where(same_image, jnp.exp(masked - row_max), 0.0)
    probs = weights_raw / jnp.sum(weights_raw, axis=1, keepdims=True)
    probs_low = probs.astype(jnp.bfloat16)
    attended = jnp.dot(probs_low, value_h, preferred_element_type=jnp.float32).astype(jnp.bfloat16)
    deltas = jnp.sum(
        attn_h.astype(jnp.float32) * attended.astype(jnp.float32), axis=1, keepdims=True
    )
    dprobs = inner(attn_h, value_h)
    dscores = (probs * (dprobs - deltas)).astype(jnp.bfloat16)
    grad_query = jnp.dot(dscores, key_h, preferred_element_type=jnp.float32) * scaling
    grad_key = outer(dscores, query_h) * scaling
    grad_value = outer(probs_low, attn_h)
    return (attended, grad_query, grad_key, grad_value)


def all_heads(query_r, key_r, value_r, attn_r, query_ids, key_ids, heads):

    def split_heads(array):
        return array.reshape(array.shape[0], heads, -1).transpose(1, 0, 2)

    def join_heads(array):
        return array.transpose(1, 0, 2).reshape(array.shape[1], -1)

    def per_head(parts):
        return head_grads(parts[0], parts[1], parts[2], parts[3], query_ids, key_ids)

    results = lax.map(
        per_head,
        (split_heads(query_r), split_heads(key_r), split_heads(value_r), split_heads(attn_r)),
    )
    return tuple((join_heads(item) for item in results))


def per_device(queries, keys_in, value_rows, grad_out, out_weight, image_ids):
    query_own = queries[0]
    key_own = keys_in[0]
    value_own = value_rows[0]
    grads_own = grad_out[0]
    rows = query_own.shape[0]
    groups = lax.axis_size("grp")
    blocks = image_ids.shape[1]
    token_ids = jnp.broadcast_to(image_ids[0][:, None], (blocks, BLK)).reshape(-1)
    grad_attn = inner(grads_own, out_weight).astype(jnp.bfloat16)
    key_all, value_all = (
        lax.all_gather(key_own, "grp", axis=0, tiled=True),
        lax.all_gather(value_own, "grp", axis=0, tiled=True),
    )
    query_ids = lax.dynamic_slice_in_dim(token_ids, lax.axis_index("grp") * rows, rows)
    attended, grad_query, grad_key_part, grad_value_part = all_heads(
        query_own, key_all, value_all, grad_attn, query_ids, token_ids, HEADS
    )
    grad_key, grad_value = (
        lax.psum_scatter(grad_key_part, "grp", scatter_dimension=0, tiled=True),
        lax.psum_scatter(grad_value_part, "grp", scatter_dimension=0, tiled=True),
    )
    grad_query = grad_query.astype(jnp.bfloat16)
    grad_key = grad_key.astype(jnp.bfloat16)
    grad_value = grad_value.astype(jnp.bfloat16)
    weight_term = outer(attended, grads_own)
    total_rows = rows * groups * lax.axis_size("dp")
    grad_weight = lax.psum(weight_term, ("grp", "dp")) * (1.0 / math.sqrt(total_rows))
    return (grad_query[None], grad_key[None], grad_value[None], grad_weight)


def solution(mesh):
    return jax.shard_map(
        per_device,
        mesh=mesh,
        in_specs=(
            P("dp", "grp", None),
            P("dp", "grp", None),
            P("dp", "grp", None),
            P("dp", "grp", None),
            P(),
            P("dp", None),
        ),
        out_specs=(P("dp", "grp", None), P("dp", "grp", None), P("dp", "grp", None), P()),
        check_vma=False,
    )
```

profile of v0, /device:TPU:1, one launch (start us, length us, event | category | flops | bytes accessed | tf_op | source)
XLA Modules:
  0.0 847.6 jit_solution(17497279671785661420)
XLA Ops:
  7.2 2.3 copy.15
  9.6 2.2 copy.16
  11.9 2.2 copy.14
  14.1 3.0 convolution_convert_fusion.1
  17.1 2.2 copy.17
  19.4 82.4 %all-gather.5.cloned.1.call-done = bf16[1,2048,1280]{1,2,0:T(8,128)(2,1)} async-done(((bf16[1,256,1280]{1,2,0:T(8,128)(2,1)}), bf16[1,2048,1280]{1,2,0:T(8,128)(2,1)}) %all-gather.5.cloned.1.call-update) | async-done | bytes 5242896 | tf_op jit(solution)/shard_map/all_gather | solution.py:74
  101.8 89.8 %all-gather.7.cloned.1.call-done = bf16[1,2048,1280]{1,2,0:T(8,128)(2,1)} async-done(((bf16[1,256,1280]{1,2,0:T(8,128)(2,1)}), bf16[1,2048,1280]{1,2,0:T(8,128)(2,1)}) %all-gather.7.cloned.1.call-update) | async-done | bytes 5242896 | tf_op jit(solution)/shard_map/all_gather | solution.py:75
  191.6 210.3 %while.17 = (s32[]{:T(128)}, bf16[16,256,80]{1,2,0:T(8,128)(2,1)}, bf16[16,256,80]{1,2,0:T(8,128)(2,1)}, f32[16,2048,80]{1,2,0:T(8,128)}, f32[16,2048,80]{1,2,0:...) while((s32[]{:T(128)}, bf16[16,256,80]{1,2,0:T(8,128)(2,1)}, ...), condition=%wide.region_4.5_spmd.clone, body=%wide.region_0.4_spmd.clone.sunk | while | flops 512515328 | bytes 20906176 | solution.py:56
  198.8 2.1 fusion.71
  212.0 2.1 fusion.71
  225.1 2.1 fusion.71
  238.2 2.1 fusion.71
  251.3 2.1 fusion.71
  264.5 2.1 fusion.71
  277.7 2.1 fusion.71
  401.9 5.1 fusion.36
  409.8 155.7 %all-reduce.2.cloned.1.call-done = f32[1280,1280]{1,0:T(8,128)} async-done(((f32[1280,1280]{1,0:T(8,128)}), f32[1280,1280]{1,0:T(8,128)}) %all-reduce.2.cloned.1.call-update) | async-done | bytes 6553616 | tf_op jit(solution)/shard_map/psum | solution.py:90
  565.5 6.2 broadcast_multiply_fusion
  571.7 129.2 %reduce-scatter.5.cloned.1.call-done = f32[256,1280]{0,1:T(8,128)} async-done(((f32[2048,1280]{0,1:T(8,128)}), f32[256,1280]{0,1:T(8,128)}) %reduce-scatter.5.cloned.1.call-update) | async-done | bytes 1310736 | tf_op jit(solution)/shard_map/reduce_scatter | solution.py:83
  700.9 2.4 convert_bitcast_fusion
  703.3 2.2 copy.23
  705.4 131.3 %reduce-scatter.3.cloned.1.call-done = f32[256,1280]{0,1:T(8,128)} async-done(((f32[2048,1280]{0,1:T(8,128)}), f32[256,1280]{0,1:T(8,128)}) %reduce-scatter.3.cloned.1.call-update) | async-done | bytes 1310736 | tf_op jit(solution)/shard_map/reduce_scatter | solution.py:82
  836.7 2.2 convert_bitcast_fusion.1
  838.9 2.2 copy.22
  (178 shorter events, 198.8 us)
Async XLA Ops:
  7.2 6.9 copy-start
  7.2 94.7 %all-gather.5.cloned.1.call-start = ((), (), s32[]{:S(2)}) async-start(), calls=%async_computation.5 | async-start | bytes 5898240 | tf_op jit(solution)/shard_map/all_gather | solution.py:74
  9.6 182.0 %all-gather.7.cloned.1.call-start = ((), (), s32[]{:S(2)}) async-start(), calls=%async_computation.6 | async-start | bytes 5898240 | tf_op jit(solution)/shard_map/all_gather | solution.py:75
  11.8 553.7 %all-reduce.2.cloned.1.call-start = ((), (), s32[]{:S(2)}) async-start(), calls=%async_computation.4 | async-start | bytes 13107200 | tf_op jit(solution)/shard_map/psum | solution.py:90
  14.1 5.2 copy-start.3
  407.0 293.9 %reduce-scatter.5.cloned.1.call-start = ((), (), s32[]{:S(2)}) async-start(), calls=%async_computation.3 | async-start | bytes 11796480 | tf_op jit(solution)/shard_map/reduce_scatter | solution.py:83
  407.6 429.1 %reduce-scatter.3.cloned.1.call-start = ((), (), s32[]{:S(2)}) async-start(), calls=%async_computation.2 | async-start | bytes 11796480 | tf_op jit(solution)/shard_map/reduce_scatter | solution.py:82
  407.6 1.1 copy-start.2
  700.9 140.2 %copy-start.1 = (bf16[1280,1280]{1,0:T(8,128)(2,1)S(1)}, bf16[1280,1280]{1,0:T(8,128)(2,1)}, u32[]{:S(2)}) copy-start(bf16[1280,1280]{1,0:T(8,128)(2,1)} %param.12) | copy-start | bytes 9830404
Sparse Core Ops, SparseCore 0:
  10.8 91.0 all-gather.4
  104.0 87.5 all-gather.6
  407.1 158.2 all-reduce.1
  569.2 131.6 reduce-scatter.4
  705.2 131.4 reduce-scatter.2
where the time goes:
time: 853 us; the launch traced here: 848 us
  waiting for transfers between devices  589 us (69%)
  matrix products  185 us (22%)
  other arithmetic  43.2 us (5%)
  local copies, waits for them, and re-layouts  16.1 us (2%)
  between operations  13.8 us (2%)
    psum x1, waiting for transfers between devices, per_device(): lax.psum(weight_term, ('grp', 'dp')) * (1.0 / math.sqrt(total_rows))  156 us
    reduce_scatter x1, waiting for transfers between devices, per_device(): lax.psum_scatter(grad_key_part, 'grp', scatter_dimension=0, tiled=True)  131 us
    reduce_scatter x1, waiting for transfers between devices, per_device(): lax.psum_scatter(grad_value_part, 'grp', scatter_dimension=0, tiled=True)  129 us
    all_gather x1, waiting for transfers between devices, per_device(): lax.all_gather(value_own, 'grp', axis=0, tiled=True)  89.8 us
    all_gather x1, waiting for transfers between devices, per_device(): lax.all_gather(key_own, 'grp', axis=0, tiled=True)  82.4 us
    dot_general x33, matrix products, outer(): lax.dot_general(left, right, (((0,), (0,)), ((), ())), preferred_element_...  67.3 us
    dot_general x33, matrix products, inner(): lax.dot_general(left, right, (((1,), (1,)), ((), ())), preferred_element_...  51.7 us
    dot_general x16, matrix products, head_grads(): jnp.dot(dscores, key_h, preferred_element_type=jnp.float32) * scaling  32.8 us
  transfers between devices with their start and end apart: 5, of which 5 were waited for; matrix products, arithmetic and copies ran while one was open for 3% of the time, Pallas kernels for 0%

commit v1 on v0

v1 whole, which is shorter than its diff:
```python
import math

import jax
import jax.numpy as jnp
from jax import lax
from jax.experimental import pallas as pl
from jax.experimental.pallas import tpu as pltpu
from jax.sharding import PartitionSpec as P

HEADS = 16
BLK = 128
DH = 80
PAIR = 2 * DH
BIG = 12
GBLOCKS = 16
REST = GBLOCKS - BIG
CHUNK = 256
bf16 = jnp.bfloat16
f32 = jnp.float32


def nn(left, right):
    return lax.dot_general(left, right, (((1,), (0,)), ((), ())), preferred_element_type=f32)


def nt(left, right):
    return lax.dot_general(left, right, (((1,), (1,)), ((), ())), preferred_element_type=f32)


def pack_kernel(weight_ref, grads_ref, query_ref, key_ref, value_ref, out_ref):
    arrays = [
        query_ref[...].T,
        key_ref[...].T,
        value_ref[...].T,
        nt(weight_ref[...], grads_ref[...]).astype(bf16),
    ]
    for dest in range(out_ref.shape[0]):
        for block in range(2):
            for which, array in enumerate(arrays):
                out_ref[dest, block, which] = array[
                    dest * PAIR : (dest + 1) * PAIR, block * BLK : (block + 1) * BLK
                ]


def pack(weight, grads, query, key, value):
    rows, width = query.shape
    half = width // 2
    column = pl.BlockSpec((rows, half), lambda i: (0, i))
    return pl.pallas_call(
        pack_kernel,
        grid=(2,),
        in_specs=[
            pl.BlockSpec((half, width), lambda i: (i, 0)),
            pl.BlockSpec((rows, width), lambda i: (0, 0)),
            column,
            column,
            column,
        ],
        out_specs=pl.BlockSpec((4, 2, 4, PAIR, BLK), lambda i: (i, 0, 0, 0, 0)),
        out_shape=jax.ShapeDtypeStruct((8, 2, 4, PAIR, BLK), bf16),
        compiler_params=pltpu.CompilerParams(vmem_limit_bytes=48 * 2**20),
        cost_estimate=pl.CostEstimate(
            flops=2 * rows * width * width, bytes_accessed=9 * 2**20, transcendentals=0
        ),
        name="pack_heads",
    )(weight, grads, query, key, value)


def first_big(ids_ref):
    middle = ids_ref[0, GBLOCKS // 2]
    start = jnp.int32(0)
    for i in range(REST):
        start = start + (ids_ref[0, i] < middle).astype(jnp.int32)
    return start


def three_terms(row):
    high = row.astype(bf16).astype(f32)
    middle = (row - high).astype(bf16).astype(f32)
    low = row - high - middle
    zeros = jnp.zeros((BLK - DH - 3, row.shape[1]), f32)
    return jnp.concatenate([high, middle, low, zeros], axis=0).astype(bf16)


def attention_kernel(ids_ref, in_ref, att_ref, out_ref, rows_ref, kv_ref, acc_ref, mixed_ref):
    scale = 1.0 / math.sqrt(DH)
    log2e = 1.4426950408889634
    start = first_big(ids_ref)
    ones = (lax.broadcasted_iota(jnp.int32, (BLK - DH, BLK * GBLOCKS), 0) < 3).astype(bf16)
    zeros = jnp.zeros((BLK - DH, BLK * GBLOCKS), bf16)

    def place(slot):
        if slot < BIG:
            return start + slot
        other = slot - BIG
        return jnp.where(other < start, other, slot)

    for head in range(2):
        features = slice(head * DH, (head + 1) * DH)
        for which in range(4):
            rows_ref[head, which, DH:, :] = ones if which == 2 else zeros
        for slot in range(GBLOCKS):
            block = place(slot)
            for which in range(4):
                rows_ref[head, which, :DH, slot * BLK : (slot + 1) * BLK] = in_ref[
                    block, which, features, :
                ]
        kv_ref[head, 0] = rows_ref[head, 1].T
        kv_ref[head, 1] = rows_ref[head, 2].T

    def step(head, queries, keys, length, bias):
        span = pl.ds(keys, length)
        query_t = rows_ref[head, 0, :, queries]
        scores = nn(kv_ref[head, 0, span, :], query_t)
        if bias is not None:
            scores = scores + bias
        top = jnp.max(scores, axis=0, keepdims=True)
        weights = jnp.exp2((scores - top) * (scale * log2e))
        weights_low = weights.astype(bf16)
        mixed = nn(rows_ref[head, 2, : DH + 16, span], weights_low)
        inverse = 1.0 / mixed[DH : DH + 1]
        attended = (mixed[:DH] * inverse).astype(bf16)
        grads = (rows_ref[head, 3, :DH, queries].astype(f32) * inverse).astype(bf16)
        delta = -jnp.sum(grads.astype(f32) * attended.astype(f32), axis=0, keepdims=True)
        grads_more = jnp.concatenate(
            [grads, three_terms(delta)], axis=0
        )
        dscores = (weights * nn(kv_ref[head, 1, span, :], grads_more)).astype(bf16)
        mixed_ref[head * DH : (head + 1) * DH, queries] = attended
        grad_query = nn(rows_ref[head, 1, :DH, span], dscores) * scale
        acc_ref[head, 0, :, queries] = grad_query
        acc_ref[head, 1, :, span] += nt(query_t[:DH], dscores)
        acc_ref[head, 2, :, span] += nt(grads, weights_low)

    acc_ref[:, 1:] = jnp.zeros((2, 2, DH, BLK * GBLOCKS), f32)

    def big_step(i, carry):
        for head in range(2):
            step(head, pl.ds(pl.multiple_of(i * CHUNK, CHUNK), CHUNK), 0, BIG * BLK, None)
        return carry

    lax.fori_loop(0, BIG * BLK // CHUNK, big_step, 0)

    numbers = [ids_ref[0, place(BIG + i)] for i in range(REST)]

    def bias_of(first):
        columns = []
        for q in range(first, first + CHUNK // BLK):
            rows = [
                jnp.full((BLK, BLK), jnp.where(numbers[q] == numbers[k], 0.0, -1e30), f32)
                for k in range(REST)
            ]
            columns.append(jnp.concatenate(rows, axis=0))
        return jnp.concatenate(columns, axis=1)

    for part in range(REST * BLK // CHUNK):
        bias = bias_of(part * (CHUNK // BLK))
        for head in range(2):
            step(head, slice(BIG * BLK + part * CHUNK, BIG * BLK + (part + 1) * CHUNK), BIG * BLK, REST * BLK, bias)

    for head in range(2):
        features = slice(head * DH, (head + 1) * DH)
        for slot in range(GBLOCKS):
            block = place(slot)
            columns = slice(slot * BLK, (slot + 1) * BLK)
            out_ref[block, 0, features, :] = acc_ref[head, 0, :, columns].astype(bf16)
            out_ref[block, 1, features, :] = (acc_ref[head, 1, :, columns] * scale).astype(bf16)
            out_ref[block, 2, features, :] = acc_ref[head, 2, :, columns].astype(bf16)
    for slot in range(GBLOCKS):
        target = pl.ds(pl.multiple_of(place(slot) * BLK, BLK), BLK)
        att_ref[:, target] = mixed_ref[:, slot * BLK : (slot + 1) * BLK]


def attention(ids, packed):
    tokens = GBLOCKS * BLK
    return pl.pallas_call(
        attention_kernel,
        in_specs=[
            pl.BlockSpec(memory_space=pltpu.SMEM),
            pl.BlockSpec(memory_space=pltpu.VMEM),
        ],
        out_specs=[
            pl.BlockSpec(memory_space=pltpu.VMEM),
            pl.BlockSpec(memory_space=pltpu.VMEM),
        ],
        out_shape=[
            jax.ShapeDtypeStruct((PAIR, tokens), bf16),
            jax.ShapeDtypeStruct((GBLOCKS, 3, PAIR, BLK), bf16),
        ],
        scratch_shapes=[
            pltpu.VMEM((2, 4, BLK, tokens), bf16),
            pltpu.VMEM((2, 2, tokens, BLK), bf16),
            pltpu.VMEM((2, 3, DH, tokens), f32),
            pltpu.VMEM((PAIR, tokens), bf16),
        ],
        compiler_params=pltpu.CompilerParams(vmem_limit_bytes=56 * 2**20),
        cost_estimate=pl.CostEstimate(
            flops=2 * 6 * 2 * 160 * BLK * BLK * BLK, bytes_accessed=5 * 2**20, transcendentals=2 * 160 * BLK * BLK
        ),
        name="attention_grads",
    )(ids, packed)


def unpack_kernel(in_ref, *out_refs):
    for which, out_ref in enumerate(out_refs):
        for block in range(2):
            columns = jnp.concatenate([in_ref[src, block, which] for src in range(8)], axis=0)
            out_ref[block * BLK : (block + 1) * BLK, :] = columns.T


def unpack(received):
    count = received.shape[2]
    width = 8 * PAIR
    return pl.pallas_call(
        unpack_kernel,
        out_shape=[jax.ShapeDtypeStruct((2 * BLK, width), bf16)] * count,
        compiler_params=pltpu.CompilerParams(vmem_limit_bytes=48 * 2**20),
        cost_estimate=pl.CostEstimate(flops=0, bytes_accessed=4 * 2**20, transcendentals=0),
        name="unpack_heads",
    )(received)


CROWS = 112


def weight_kernel(att_ref, grads_ref, out_ref):
    product = nn(att_ref[...], grads_ref[...])
    columns = product.shape[1] // BLK
    for j in range(columns):
        out_ref[j * PAIR : (j + 1) * PAIR, :] = product[:, j * BLK : (j + 1) * BLK].astype(bf16)
    out_ref[columns * PAIR :, :] = jnp.zeros((out_ref.shape[0] - columns * PAIR, BLK), bf16)


def weight_terms(att, grads):
    return pl.pallas_call(
        weight_kernel,
        out_shape=jax.ShapeDtypeStruct((16 * CROWS, BLK), bf16),
        compiler_params=pltpu.CompilerParams(vmem_limit_bytes=48 * 2**20),
        cost_estimate=pl.CostEstimate(
            flops=2 * att.shape[0] * att.shape[1] * grads.shape[1], bytes_accessed=6 * 2**20, transcendentals=0
        ),
        name="weight_terms",
    )(att, grads)


def finish_kernel(core_ref, own_ref, other_ref, out_ref, rows_ref, *, scale):
    core = core_ref[0]
    for k in range(8):
        rows_ref[2 * k + core] = own_ref[0, k]
        rows_ref[2 * k + 1 - core] = other_ref[0, k]
    rows = rows_ref[...].reshape(16 * CROWS, BLK)
    for j in range(out_ref.shape[1] // BLK):
        block = rows[j * PAIR : (j + 1) * PAIR, :].astype(f32)
        out_ref[:, j * BLK : (j + 1) * BLK] = block * scale


def finish(core, own, other, scale):
    width = 8 * PAIR
    part = pl.BlockSpec((1, 8, CROWS, BLK), lambda i: (i, 0, 0, 0))
    return pl.pallas_call(
        lambda *refs: finish_kernel(*refs, scale=scale),
        grid=(8,),
        in_specs=[pl.BlockSpec(memory_space=pltpu.SMEM), part, part],
        out_specs=pl.BlockSpec((PAIR, width), lambda i: (i, 0)),
        out_shape=jax.ShapeDtypeStruct((width, width), f32),
        scratch_shapes=[pltpu.VMEM((16, CROWS, BLK), bf16)],
        cost_estimate=pl.CostEstimate(flops=0, bytes_accessed=10 * 2**20, transcendentals=0),
        name="finish_weight",
    )(core, own, other)


def per_device(queries, keys_in, value_rows, grad_out, out_weight, image_ids):
    grads_own = grad_out[0]
    packed = pack(out_weight, grads_own, queries[0], keys_in[0], value_rows[0])
    grads_all = lax.all_gather(grads_own, "grp", axis=0, tiled=True)
    received = lax.all_to_all(packed, "grp", 0, 0, tiled=True)
    att, out = attention(image_ids, received.reshape(GBLOCKS, 4, PAIR, BLK))
    back = lax.all_to_all(out.reshape(8, 2, 3, PAIR, BLK), "grp", 0, 0, tiled=True)
    grad_query, grad_key, grad_value = unpack(back)
    terms = weight_terms(att, grads_all).reshape(16, CROWS, BLK)
    parts = lax.all_to_all(terms, "dp", 0, 0, tiled=True)
    part = jnp.sum(parts.astype(f32), axis=0).astype(bf16)
    copies = jnp.broadcast_to(part[None], (64, CROWS, BLK))
    groups = [[i * 2 + core for i in range(64)] for core in range(2)]
    own = lax.all_to_all(copies, ("grp", "dp"), 0, 0, axis_index_groups=groups, tiled=True)
    other = lax.ppermute(own, "dp", [(i, i ^ 1) for i in range(16)])
    core = (lax.axis_index("dp") % 2).astype(jnp.int32).reshape(1)
    shape = (8, 8, CROWS, BLK)
    total = 2 * BLK * 8 * 16
    grad_weight = finish(core, own.reshape(shape), other.reshape(shape), 1.0 / math.sqrt(total))
    return (grad_query[None], grad_key[None], grad_value[None], grad_weight)


def solution(mesh):
    return jax.shard_map(
        per_device,
        mesh=mesh,
        in_specs=(
            P("dp", "grp", None),
            P("dp", "grp", None),
            P("dp", "grp", None),
            P("dp", "grp", None),
            P(),
            P("dp", None),
        ),
        out_specs=(P("dp", "grp", None), P("dp", "grp", None), P("dp", "grp", None), P()),
        check_vma=False,
    )
```

time: 853 us -> 223 us (0.26)
  waiting for transfers between devices: 589 us -> 58 us
  matrix products: 185 us -> 0 us
  blocking collectives: 0 us -> 92.6 us
  Pallas kernels: 0 us -> 45.9 us
  other arithmetic: 43.2 us -> 0.07 us
  local copies, waits for them, and re-layouts: 16.1 us -> 5.66 us
    reduce_scatter x2 -> x0, waiting for transfers between devices: 260 us -> none  [the longest x1 131 us: per_device(): lax.psum_scatter(grad_key_part, 'grp', scatter_dimension=0, tiled=True)]
    dot_general x98 -> x0, matrix products: 185 us -> none  [the longest x33 67.3 us: outer(): lax.dot_general(left, right, (((0,), (0,)), ((), ())), preferred_element_...]
    psum x1 -> x0, waiting for transfers between devices: 156 us -> none  [per_device(): lax.psum(weight_term, ('grp', 'dp')) * (1.0 / math.sqrt(total_rows))]
    all_gather x2 -> x1, waiting for transfers between devices: 172 us -> 27.6 us  [per_device(): grads_all = lax.all_gather(grads_own, 'grp', axis=0, tiled=True)]
    all_to_all x0 -> x3, blocking collectives: none -> 92.6 us  [the longest x1 46.6 us: per_device(): received = lax.all_to_all(packed, 'grp', 0, 0, tiled=True)]
    pallas_call x0 -> x5, Pallas kernels: none -> 45.9 us  [the longest x1 30.6 us: attention(): pl.pallas_call(attention_kernel, in_specs=[pl.BlockSpec(memory_space=pltp...]
    all_to_all x0 -> x1, waiting for transfers between devices: none -> 29.7 us  [per_device(): lax.all_to_all(out.reshape(8, 2, 3, PAIR, BLK), 'grp', 0, 0, tiled=True)]
    reduce_sum x32 -> x1, other arithmetic: 22 us -> 0.07 us  [per_device(): part = jnp.sum(parts.astype(f32), axis=0).astype(bf16)]
  transfers between devices with their start and end apart: 5 -> 3, of which waited for: 5 -> 2; matrix products, arithmetic and copies ran while one was open for 3% -> 0% of each run, Pallas kernels for 0% -> 16%
where the time goes in v1:
time: 223 us; the launch traced here: 222 us
  blocking collectives  92.6 us (42%)
  waiting for transfers between devices  58 us (26%)
  Pallas kernels  45.9 us (21%)
  between operations  14.1 us (6%)
  starting transfers between devices  6.06 us (3%)
  local copies, waits for them, and re-layouts  5.66 us (3%)
    all_to_all x1, blocking collectives, per_device(): received = lax.all_to_all(packed, 'grp', 0, 0, tiled=True)  46.6 us
    all_to_all x1, blocking collectives, per_device(): lax.all_to_all(copies, ('grp', 'dp'), 0, 0, axis_index_groups=groups, til...  31.3 us
    pallas_call x1, Pallas kernels, attention(): pl.pallas_call(attention_kernel, in_specs=[pl.BlockSpec(memory_space=pltp...  30.6 us
    all_to_all x1, waiting for transfers between devices, per_device(): lax.all_to_all(out.reshape(8, 2, 3, PAIR, BLK), 'grp', 0, 0, tiled=True)  29.7 us
    all_gather x1, waiting for transfers between devices, per_device(): grads_all = lax.all_gather(grads_own, 'grp', axis=0, tiled=True)  27.6 us
    all_to_all x1, blocking collectives, per_device(): parts = lax.all_to_all(terms, 'dp', 0, 0, tiled=True)  14.7 us
    pallas_call x1, Pallas kernels, finish(): pl.pallas_call(lambda *refs: finish_kernel(*refs, scale=scale), grid=(8,)...  7.58 us
    unnamed x10, local copies, waits for them, and re-layouts  5.43 us
  transfers between devices with their start and end apart: 3, of which 2 were waited for; matrix products, arithmetic and copies ran while one was open for 0% of the time, Pallas kernels for 16%

profile of v1, /device:TPU:1, one launch (start us, length us, event | category | flops | bytes accessed | tf_op | source)
XLA Modules:
  0.0 222.4 jit_solution(13178074264019665729)
XLA Ops:
  7.2 0.0 all-gather.3.cloned.1.call-start
  7.2 0.7 all-gather.3.cloned.1.call-update
  7.9 0.0 copy-start
  7.9 1.1 copy-done
  9.0 0.0 copy-start.1
  9.0 1.1 copy-done.1
  10.1 1.1 copy-done.2
  11.2 1.1 copy-done.3
  12.3 2.7 %pack_heads.1 = bf16[8,2,4,160,128]{4,3,2,1,0:T(8,128)(2,1)S(1)} custom-call(bf16[1280,1280]{1,0:T(8,128)(2,1)} %weight_ref.1, bf16[256,1280]{1,0:T(8,128)(2,1)S(1)} %bitcast.14, bf16[256,1280]{1,0:T(8,128)(2,1)S(1)} %bitcast.16, bf16[256,1280]{1,0:T(8,128)(2,1)S(1)} %bitcast.17, bf16[256,1280]{1,0:T(8,128)(2,1)S(1)} %bitcast.18), custom_call_target="tpu_custom_call" | custom-call | flops 838860800 | bytes 9437184 | tf_op jit(solution)/shard_map/pack_heads/pallas_call | solution.py:49
  15.0 46.6 %all_to_all.20 = bf16[8,2,4,160,128]{4,3,2,1,0:T(8,128)(2,1)} all-to-all(bf16[8,2,4,160,128]{4,3,2,1,0:T(8,128)(2,1)S(1)} %pack_heads.1), channel_id=1, replica_groups=mesh['grp'=8,'dp'=16] {'grp'}, dimensions={0} | all-to-all | bytes 5242880 | tf_op jit(solution)/shard_map/all_to_all | solution.py:276
  61.6 30.6 %attention_grads.1 = (bf16[160,2048]{1,0:T(8,128)(2,1)}, bf16[16,3,160,128]{3,2,1,0:T(8,128)(2,1)}) custom-call(s32[1,16]{1,0:T(1,128)} %ids_ref.1, bf16[16,4,160,128]{3,2,1,0:T(8,128)(2,1)} %bitcast.20), custom_call_target="tpu_custom_call" | custom-call | flops 8053063680 | bytes 5242880 | tf_op jit(solution)/shard_map/attention_grads/pallas_call | solution.py:176
  92.2 27.6 %all-gather.3.cloned.1.call-done = bf16[1,2048,1280]{2,1,0:T(8,128)(2,1)} async-done(((bf16[1,256,1280]{2,1,0:T(8,128)(2,1)}), bf16[1,2048,1280]{2,1,0:T(8,128)(2,1)}) %all-gather.3.cloned.1.call-update) | async-done | bytes 5242896 | tf_op jit(solution)/shard_map/all_gather | solution.py:275
  119.8 1.1 copy-done.4
  120.9 3.5 %weight_terms.1 = bf16[1792,128]{1,0:T(8,128)(2,1)S(1)} custom-call(bf16[160,2048]{1,0:T(8,128)(2,1)S(1)} %copy-done.4, bf16[2048,1280]{1,0:T(8,128)(2,1)} %bitcast.19), custom_call_target="tpu_custom_call" | custom-call | flops 838860800 | bytes 6291456 | tf_op jit(solution)/shard_map/weight_terms/pallas_call | solution.py:235
  124.4 14.7 %all_to_all.21 = bf16[16,112,128]{2,1,0:T(8,128)(2,1)S(1)} all-to-all(bf16[16,112,128]{2,1,0:T(8,128)(2,1)S(1)} %bitcast.15), channel_id=1, replica_groups=mesh['grp'=8,'dp'=16] {'dp'}, dimensions={0} | all-to-all | bytes 917504 | tf_op jit(solution)/shard_map/all_to_all | solution.py:281
  139.1 0.1 reduce_sum.12
  139.2 0.2 broadcast_in_dim.18
  139.5 31.3 %all_to_all.22 = bf16[64,112,128]{2,1,0:T(8,128)(2,1)} all-to-all(bf16[64,112,128]{2,1,0:T(8,128)(2,1)S(1)} %broadcast_in_dim.18), channel_id=1, replica_groups={{0,2,4,6,8,10,12,14,16,18,20,22,24,26,28,30,32,34,36,38,40,42,44,46,48,..., dimensions={0} | all-to-all | bytes 3670016 | tf_op jit(solution)/shard_map/all_to_all | solution.py:285
  170.8 2.4 %collective-permute-start = (bf16[64,112,128]{2,1,0:T(8,128)(2,1)}, bf16[64,112,128]{2,1,0:T(8,128)(2,1)}, u32[]{:S(2)}, u32[]{:S(2)}) collective-permute-start(bf16[64,112,128]{2,1,0:T(8,128)(2,1)} %all_to_all.22), channel_id=1, source_target_pairs={{0,1},{1,0},{2,3},{3,2},{4,5},{5,4},{6,7},{7,6},{8,9},{9,8},{10,11... | collective-permute-start | bytes 5505032 | tf_op jit(solution)/shard_map/ppermute | solution.py:286
  173.2 3.6 %all-to-all-start.1 = ((bf16[8,2,3,160,128]{4,3,2,1,0:T(8,128)(2,1)}), bf16[8,2,3,160,128]{4,3,2,1,0:T(8,128)(2,1)S(1)}, u32[]{:S(2)}, u32[]{:S(2)}) async-start(bf16[8,2,3,160,128]{4,3,2,1,0:T(8,128)(2,1)} %bitcast.21), calls=%async_computation.1 | async-start | bytes 3932160 | tf_op jit(solution)/shard_map/all_to_all | solution.py:278
  176.8 29.7 %all-to-all-done.1.in_ref = bf16[8,2,3,160,128]{4,3,2,1,0:T(8,128)(2,1)S(1)} async-done(((bf16[8,2,3,160,128]{4,3,2,1,0:T(8,128)(2,1)}), bf16[8,2,3,160,128]{4,3,2,1,0:T(8,128)(2,1)S(1)}, u32[]{:S(2)}, u32[]{:S(2)}) %all-to-all-start.1) | async-done | bytes 1966112 | tf_op jit(solution)/shard_map/all_to_all | solution.py:278
  206.5 1.5 unpack_heads.1
  208.0 0.0 collective-permute-done
  208.0 7.6 %finish_weight.1 = f32[1280,1280]{1,0:T(8,128)} custom-call(s32[1]{0:T(128)} %bitcast.9.refs_0_, bf16[8,8,112,128]{3,2,1,0:T(8,128)(2,1)} %bitcast.12.refs_1_, bf16[8,8,112,128]{3,2,1,0:T(8,128)(2,1)} %bitcast.13.refs_2_), custom_call_target="tpu_custom_call" | custom-call | bytes 10485760 | tf_op jit(solution)/shard_map/finish_weight/pallas_call | solution.py:260
  (3 shorter events, 0.0 us)
Async XLA Ops:
  7.2 112.7 %all-gather.3.cloned.1.call-start = ((), (), s32[]{:S(2)}) async-start(), calls=%async_computation.4 | async-start | bytes 5898240 | tf_op jit(solution)/shard_map/all_gather | solution.py:275
  7.9 1.1 copy-start
  9.0 1.1 copy-start.1
  10.1 1.1 copy-start.2
  11.2 1.1 copy-start.3
  119.8 1.1 copy-start.4
  170.8 37.2 %collective-permute-start = (bf16[64,112,128]{2,1,0:T(8,128)(2,1)}, bf16[64,112,128]{2,1,0:T(8,128)(2,1)}, u32[]{:S(2)}, u32[]{:S(2)}) collective-permute-start(bf16[64,112,128]{2,1,0:T(8,128)(2,1)} %all_to_all.22), channel_id=1, source_target_pairs={{0,1},{1,0},{2,3},{3,2},{4,5},{5,4},{6,7},{7,6},{8,9},{9,8},{10,11... | collective-permute-start | bytes 5505032 | tf_op jit(solution)/shard_map/ppermute | solution.py:286
  173.2 33.3 %all-to-all-start.1 = ((bf16[8,2,3,160,128]{4,3,2,1,0:T(8,128)(2,1)}), bf16[8,2,3,160,128]{4,3,2,1,0:T(8,128)(2,1)S(1)}, u32[]{:S(2)}, u32[]{:S(2)}) async-start(bf16[8,2,3,160,128]{4,3,2,1,0:T(8,128)(2,1)} %bitcast.21), calls=%async_computation.1 | async-start | bytes 3932160 | tf_op jit(solution)/shard_map/all_to_all | solution.py:278
Sparse Core Ops, SparseCore 0:
  10.3 109.4 all-gather.2

commit v2 on v0

v2 whole, which is shorter than its diff:
```python
import math

import jax
import jax.numpy as jnp
from jax import lax
from jax.experimental import pallas as pl
from jax.experimental.pallas import tpu as pltpu
from jax.sharding import PartitionSpec as P

HEADS = 16
BLK = 128
DH = 80
PAIR = 2 * DH
BIG = 12
GBLOCKS = 16
REST = GBLOCKS - BIG
BIG_CHUNK = 768
CHUNK = 512
SCALE = 1.0 / math.sqrt(DH)
LOG2E = 1.4426950408889634
WEIGHT_SCALE = 1.0 / math.sqrt(16 * GBLOCKS * BLK)
bf16 = jnp.bfloat16
f32 = jnp.float32


def nn(left, right):
    return lax.dot_general(left, right, (((1,), (0,)), ((), ())), preferred_element_type=f32)


def nt(left, right):
    return lax.dot_general(left, right, (((1,), (1,)), ((), ())), preferred_element_type=f32)


def whole(shape):
    return pl.BlockSpec(shape, lambda i: (0,) * len(shape))


def first_big(ids_ref):
    middle = ids_ref[0, GBLOCKS // 2]
    start = jnp.int32(0)
    for i in range(REST):
        start = start + (ids_ref[0, i] < middle).astype(jnp.int32)
    return start


def three_terms(row):
    high = row.astype(bf16).astype(f32)
    middle = (row - high).astype(bf16).astype(f32)
    low = row - high - middle
    zeros = jnp.zeros((BLK - DH - 3, row.shape[1]), f32)
    return jnp.concatenate([high, middle, low, zeros], axis=0).astype(bf16)


def place_of(start, slot):
    if slot < BIG:
        return start + slot
    other = slot - BIG
    return jnp.where(other < start, other, slot)


def slot_of(start, block):
    other = jnp.where(block < start, BIG + block, block)
    return jnp.where((block >= start) & (block < start + BIG), block - start, other)


def columns_of(slot):
    return slice(slot * BLK, (slot + 1) * BLK)


def pack_kernel(weight_ref, grads_ref, query_ref, key_ref, value_ref, *refs):
    out_ref, *half_refs = refs[-3:]
    arrays = [
        query_ref[...].T,
        key_ref[...].T,
        value_ref[...].T,
        nt(weight_ref[...], grads_ref[...]).astype(bf16),
    ]
    for dest in range(out_ref.shape[0]):
        for block in range(2):
            for which, array in enumerate(arrays):
                out_ref[dest, block, which] = array[
                    dest * DH : (dest + 1) * DH, columns_of(block)
                ]
    for i, half_ref in enumerate(half_refs):
        half_ref[...] = grads_ref[columns_of(i), :]


def pack(half, weight, grads, query, key, value, *after):
    rows, width = query.shape
    column = pl.BlockSpec((rows, width // 2), lambda i: (0, half))
    shapes = [
        jax.ShapeDtypeStruct((8, 2, 4, DH, BLK), bf16),
        jax.ShapeDtypeStruct((BLK, grads.shape[1]), bf16),
        jax.ShapeDtypeStruct((BLK, grads.shape[1]), bf16),
    ]
    return pl.pallas_call(
        pack_kernel,
        grid=(1,),
        in_specs=[
            pl.BlockSpec((width // 2, width), lambda i: (half, 0)),
            whole(grads.shape),
            column,
            column,
            column,
        ]
        + [pl.BlockSpec(memory_space=pl.ANY)] * len(after),
        out_specs=[whole(shape.shape) for shape in shapes],
        out_shape=shapes,
        compiler_params=pltpu.CompilerParams(vmem_limit_bytes=63 * 2**20),
        cost_estimate=pl.CostEstimate(
            flops=rows * width * width, bytes_accessed=5 * 2**20, transcendentals=0
        ),
        name="pack_heads",
    )(weight, grads, query, key, value, *after)


def attention_kernel(ids_ref, me_ref, in_ref, *refs):
    keep_ref, send_ref, out_ref, rows_ref, kv_ref, acc_ref, mixed_ref = refs[-7:]
    start = first_big(ids_ref)
    width = BLK * GBLOCKS
    ones = (lax.broadcasted_iota(jnp.int32, (BLK - DH, width), 0) < 3).astype(bf16)
    zeros = jnp.zeros((BLK - DH, width), bf16)
    for which in range(4):
        rows_ref[which, DH:, :] = ones if which == 2 else zeros
    for slot in range(GBLOCKS):
        block = place_of(start, slot)
        for which in range(4):
            rows_ref[which, :DH, columns_of(slot)] = in_ref[block, which]
    kv_ref[0] = rows_ref[1].T
    kv_ref[1] = rows_ref[2].T
    acc_ref[1:] = jnp.zeros((2, DH, width), f32)

    def chunk(queries, span, bias):
        query_t = rows_ref[0, :, queries]
        scores = nn(kv_ref[0, span, :], query_t)
        if bias is not None:
            scores = scores + bias
        top = jnp.max(scores, axis=0, keepdims=True)
        weights = jnp.exp2((scores - top) * (SCALE * LOG2E))
        weights_low = weights.astype(bf16)
        mixed = nn(rows_ref[2, : DH + 16, span], weights_low)
        inverse = 1.0 / mixed[DH : DH + 1]
        attended = (mixed[:DH] * inverse).astype(bf16)
        mixed_ref[:, queries] = attended
        grads = (rows_ref[3, :DH, queries].astype(f32) * inverse).astype(bf16)
        delta = -jnp.sum(grads.astype(f32) * attended.astype(f32), axis=0, keepdims=True)
        grads_more = jnp.concatenate([grads, three_terms(delta)], axis=0)
        dscores = (weights * nn(kv_ref[1, span, :], grads_more)).astype(bf16)
        acc_ref[0, :, queries] = nn(rows_ref[1, :DH, span], dscores)
        acc_ref[1, :, span] += nt(query_t[:DH], dscores)
        acc_ref[2, :, span] += nt(grads, weights_low)

    def big_chunk(i, carry):
        chunk(pl.ds(pl.multiple_of(i * BIG_CHUNK, BIG_CHUNK), BIG_CHUNK), slice(0, BIG * BLK), None)
        return carry

    lax.fori_loop(0, BIG * BLK // BIG_CHUNK, big_chunk, 0, unroll=2)

    numbers = [ids_ref[0, place_of(start, BIG + i)] for i in range(REST)]
    for part in range(REST * BLK // CHUNK):
        first = part * (CHUNK // BLK)
        columns = []
        for q in range(first, first + CHUNK // BLK):
            rows = [
                jnp.full((BLK, BLK), jnp.where(numbers[q] == numbers[k], 0.0, -1e30), f32)
                for k in range(REST)
            ]
            columns.append(jnp.concatenate(rows, axis=0))
        queries = slice(BIG * BLK + part * CHUNK, BIG * BLK + (part + 1) * CHUNK)
        chunk(queries, slice(BIG * BLK, GBLOCKS * BLK), jnp.concatenate(columns, axis=1))

    for slot in range(GBLOCKS):
        block = place_of(start, slot)
        own = lax.rem(lax.div(block, 2), 2) == lax.rem(me_ref[0], 2)
        column = lax.div(block, 4) * 2 + lax.rem(block, 2)
        target = pl.ds(pl.multiple_of(column * BLK, BLK), BLK)

        @pl.when(own)
        def _():
            keep_ref[:, target] = mixed_ref[:, columns_of(slot)]

        @pl.when(jnp.logical_not(own))
        def _():
            send_ref[:, target] = mixed_ref[:, columns_of(slot)]

    for slot in range(GBLOCKS):
        block = place_of(start, slot)
        for which in range(3):
            part = acc_ref[which, :, columns_of(slot)]
            if which < 2:
                part = part * SCALE
            out_ref[block, which] = part.astype(bf16)


def attention(head, ids, me, packed, *before):
    tokens = GBLOCKS * BLK
    shapes = [jax.ShapeDtypeStruct((PAIR, tokens // 2), bf16)] * 2
    shapes += [jax.ShapeDtypeStruct((GBLOCKS, 3, PAIR, BLK), bf16)]
    smem = pl.BlockSpec(memory_space=pltpu.SMEM)
    blocks = [pl.BlockSpec((DH, tokens // 2), lambda i: (head, 0))] * 2
    blocks += [pl.BlockSpec((GBLOCKS, 3, DH, BLK), lambda i: (0, 0, head, 0))]
    return pl.pallas_call(
        attention_kernel,
        grid=(1,),
        in_specs=[smem, smem, whole(packed.shape)]
        + [pl.BlockSpec(memory_space=pl.ANY)] * len(before),
        out_specs=blocks,
        out_shape=shapes,
        input_output_aliases={3 + i: i for i in range(len(before))},
        scratch_shapes=[
            pltpu.VMEM((4, BLK, tokens), bf16),
            pltpu.VMEM((2, tokens, BLK), bf16),
            pltpu.VMEM((3, DH, tokens), f32),
            pltpu.VMEM((DH, tokens), bf16),
        ],
        compiler_params=pltpu.CompilerParams(vmem_limit_bytes=63 * 2**20),
        cost_estimate=pl.CostEstimate(
            flops=2 * 6 * 3 * 160 * BLK * BLK * BLK,
            bytes_accessed=4 * 2**20,
            transcendentals=160 * BLK * BLK,
        ),
        name="attention_grads",
    )(ids, me, packed, *before)


def unpack_kernel(in_ref, *out_refs):
    for which, out_ref in enumerate(out_refs):
        for half in range(2):
            rows = [
                in_ref[source, half, which, head * DH : (head + 1) * DH, :]
                for head in range(2)
                for source in range(8)
            ]
            out_ref[half * BLK : (half + 1) * BLK, :] = jnp.concatenate(rows, axis=0).T


def unpack(received):
    count = received.shape[2]
    width = 8 * PAIR
    return pl.pallas_call(
        unpack_kernel,
        out_shape=[jax.ShapeDtypeStruct((2 * BLK, width), bf16)] * count,
        compiler_params=pltpu.CompilerParams(vmem_limit_bytes=63 * 2**20),
        cost_estimate=pl.CostEstimate(flops=0, bytes_accessed=4 * 2**20, transcendentals=0),
        name="unpack_heads",
    )(received)


CROWS = 112


def weight_kernel(me_ref, column_ref, keep_ref, other_ref, *refs):
    grads_refs, out_refs, both_ref, ring_ref, rows_ref = refs[:-5], refs[-5:-3], *refs[-3:-1], refs[-1]
    core = lax.rem(column_ref[0], 2)
    low = lax.rem(lax.div(column_ref[0], 2), 2)
    z = lax.div(column_ref[0], 4)
    both_ref[:PAIR] = keep_ref[...]
    both_ref[PAIR:] = other_ref[...]
    gx = lax.div(me_ref[0], 2)
    offset = gx * (2 * BLK)
    first = 0
    for grads_ref in grads_refs:
        rows = grads_ref.shape[0]
        columns = pl.ds(pl.multiple_of(lax.rem(offset, both_ref.shape[1]), BLK), rows)
        ring_ref[:, first : first + rows] = both_ref[:, columns]
        offset = offset + rows
        first = first + rows
    left = ring_ref[...]
    width = grads_refs[0].shape[1]
    blocks = []
    for j in range(0, width, 2 * BLK):
        right = jnp.concatenate([ref[:, j : j + 2 * BLK] for ref in grads_refs], axis=0)
        blocks.append(nn(left, right).astype(bf16))
    product = jnp.concatenate(blocks, axis=1)
    per_core = product.shape[1] // BLK // 2
    for which in range(2):
        for half in range(2):
            for j in range(per_core):
                rows_ref[j * PAIR : (j + 1) * PAIR, :] = product[
                    which * PAIR : (which + 1) * PAIR, columns_of(half * per_core + j)
                ]
            rows_ref[per_core * PAIR :, :] = jnp.zeros((8 * CROWS - per_core * PAIR, BLK), bf16)

            def store(out_ref):
                for j in range(8):
                    along_z = lax.bitwise_xor(z, j // 2)
                    along_y = which * 2 + lax.bitwise_xor(low, j % 2)
                    out_ref[along_z, along_y] = rows_ref[j * CROWS : (j + 1) * CROWS, :]

            pl.when(core == half)(lambda: store(out_refs[0]))
            pl.when(core != half)(lambda: store(out_refs[1]))


def weight_terms(me, column, keep, other, grads):
    vmem = pl.BlockSpec(memory_space=pltpu.VMEM)
    return pl.pallas_call(
        weight_kernel,
        in_specs=[pl.BlockSpec(memory_space=pltpu.SMEM)] * 2 + [vmem] * (2 + len(grads)),
        out_specs=[vmem] * 2,
        out_shape=[jax.ShapeDtypeStruct((4, 4, CROWS, BLK), bf16)] * 2,
        scratch_shapes=[
            pltpu.VMEM((2 * PAIR, keep.shape[1]), bf16),
            pltpu.VMEM((2 * PAIR, keep.shape[1]), bf16),
            pltpu.VMEM((8 * CROWS, BLK), bf16),
        ],
        compiler_params=pltpu.CompilerParams(vmem_limit_bytes=63 * 2**20),
        cost_estimate=pl.CostEstimate(
            flops=2 * 2 * PAIR * 4 * grads[0].size, bytes_accessed=6 * 2**20, transcendentals=0
        ),
        name="weight_terms",
    )(me, column, keep, other, *grads)


def add_kernel(*refs):
    count = len(refs) - 4
    for i in range(4):
        total = refs[0][i].astype(f32)
        for ref in refs[1:count]:
            total = total + ref[i].astype(f32)
        refs[count + i][...] = total.astype(bf16)


def add_up(*arrays):
    shape = arrays[0].shape[1:]
    return pl.pallas_call(
        add_kernel,
        out_shape=[jax.ShapeDtypeStruct(shape, bf16)] * 4,
        compiler_params=pltpu.CompilerParams(vmem_limit_bytes=63 * 2**20),
        cost_estimate=pl.CostEstimate(
            flops=len(arrays) * arrays[0].size, bytes_accessed=2**20, transcendentals=0
        ),
        name="add_up",
    )(*arrays)


def nothing_kernel(*refs):
    pass


def once(array, *after):
    anywhere = pl.BlockSpec(memory_space=pl.ANY)
    return pl.pallas_call(
        nothing_kernel,
        in_specs=[anywhere] * (1 + len(after)),
        out_specs=anywhere,
        out_shape=jax.ShapeDtypeStruct(array.shape, array.dtype),
        input_output_aliases={0: 0},
        compiler_params=pltpu.CompilerParams(vmem_limit_bytes=63 * 2**20),
        name="once",
    )(array, *after)


def add_kernel(*refs):
    count = len(refs) - 4
    for i in range(4):
        total = refs[0][i].astype(f32)
        for ref in refs[1:count]:
            total = total + ref[i].astype(f32)
        refs[count + i][...] = total.astype(bf16)


def add_up(*arrays):
    shape = arrays[0].shape[1:]
    return pl.pallas_call(
        add_kernel,
        out_shape=[jax.ShapeDtypeStruct(shape, bf16)] * 4,
        compiler_params=pltpu.CompilerParams(vmem_limit_bytes=63 * 2**20),
        cost_estimate=pl.CostEstimate(
            flops=len(arrays) * arrays[0].size, bytes_accessed=2**20, transcendentals=0
        ),
        name="add_up",
    )(*arrays)


def nothing_kernel(*refs):
    pass


def once(array, *after):
    anywhere = pl.BlockSpec(memory_space=pl.ANY)
    return pl.pallas_call(
        nothing_kernel,
        in_specs=[anywhere] * (1 + len(after)),
        out_specs=anywhere,
        out_shape=jax.ShapeDtypeStruct(array.shape, array.dtype),
        input_output_aliases={0: 0},
        compiler_params=pltpu.CompilerParams(vmem_limit_bytes=63 * 2**20),
        name="once",
    )(array, *after)


def finish_kernel(core_ref, in_ref, *refs):
    out_ref = refs[-1]
    for pair in range(in_ref.shape[0]):
        for j in range(out_ref.shape[3] // BLK):
            block = in_ref[pair, j * PAIR : (j + 1) * PAIR, :].astype(f32) * WEIGHT_SCALE
            for head in range(2):
                out_ref[head, pair, :, columns_of(j)] = block[head * DH : (head + 1) * DH]


def finish(core, rows, *before):
    width = 8 * PAIR
    return pl.pallas_call(
        finish_kernel,
        grid_spec=pltpu.PrefetchScalarGridSpec(
            num_scalar_prefetch=1,
            grid=(2,),
            in_specs=[pl.BlockSpec((4, 8 * CROWS, BLK), lambda i, core: (i, 0, 0))]
            + [pl.BlockSpec(memory_space=pl.ANY)] * len(before),
            out_specs=pl.BlockSpec((2, 4, DH, width // 2), lambda i, core: (0, i, 0, core[0])),
        ),
        out_shape=jax.ShapeDtypeStruct((2, 8, DH, width), f32),
        input_output_aliases={2: 0} if before else {},
        compiler_params=pltpu.CompilerParams(vmem_limit_bytes=63 * 2**20),
        cost_estimate=pl.CostEstimate(flops=0, bytes_accessed=5 * 2**20, transcendentals=0),
        name="finish_weight",
    )(core, rows, *before)


def scalar(value):
    return value.astype(jnp.int32).reshape(1)


def per_device(queries, keys_in, value_rows, grad_out, out_weight, image_ids):
    grads_own = grad_out[0]
    both = ("grp", "dp")
    me = scalar(lax.axis_index("grp"))
    core = lax.axis_index("dp") % 2
    operands = (out_weight, grads_own, queries[0], keys_in[0], value_rows[0])
    packed_first, _, _ = pack(0, *operands)
    packed_second, *grads_late = pack(1, *operands, packed_first)
    shape = (GBLOCKS, 4, DH, BLK)
    first = lax.all_to_all(packed_first, "grp", 0, 0, tiled=True).reshape(shape)
    packed_second = once(packed_second, first)
    second = lax.all_to_all(packed_second, "grp", 0, 0, tiled=True).reshape(shape)
    results = attention(0, image_ids, me, first)
    up = [(i, (i + 2) % 8) for i in range(8)]
    down = [(i, (i + 6) % 8) for i in range(8)]
    grads_late = [once(half, first) for half in grads_late]
    grads_left = [lax.ppermute(half, "grp", up) for half in grads_late]
    grads_right = [lax.ppermute(half, "grp", down) for half in grads_late]
    keep, send, out = attention(1, image_ids, me, second, *results)
    grads_right[0] = once(grads_right[0], send)
    grads_left[1] = once(grads_left[1], send)
    grads_far = [lax.ppermute(grads_right[0], "grp", down), lax.ppermute(grads_left[1], "grp", up)]
    send = once(send, *grads_left, *grads_right)
    other = lax.ppermute(send, "grp", [(i, i ^ 1) for i in range(8)])
    out = once(out, other, *grads_far)
    back = lax.all_to_all(out.reshape(8, 2, 3, PAIR, BLK), "grp", 0, 0, tiled=True)
    grads_line = (grads_own, *grads_right, *grads_far, *grads_left)
    column = scalar(lax.axis_index("dp"))
    kept, sent = weight_terms(me, column, keep, other, grads_line)
    cores = [(i, i ^ 1) for i in range(16)]
    sent = lax.ppermute(sent, "dp", cores)
    parts = [(kept[k].astype(f32) + sent[k].astype(f32)).astype(bf16) for k in range(4)]
    parts = [parts[0]] + [
        lax.ppermute(parts[k], "dp", [(i, i ^ (4 * k)) for i in range(16)]) for k in range(1, 4)
    ]
    parts = [sum(item[k].astype(f32) for item in parts).astype(bf16) for k in range(4)]
    parts = [parts[0]] + [
        lax.ppermute(parts[k], both, [(i, i ^ (16 * (k // 2) + 2 * (k % 2))) for i in range(128)])
        for k in range(1, 4)
    ]
    part = sum(item.astype(f32) for item in parts).astype(bf16)
    copies = jnp.broadcast_to(part[None], (64,) + part.shape)
    same_core = [[i * 2 + c for i in range(64)] for c in range(2)]
    own = lax.all_to_all(copies, both, 0, 0, axis_index_groups=same_core, tiled=True)
    grad_query, grad_key, grad_value = unpack(back)
    own = once(own, grad_query).reshape(8, 8 * CROWS, BLK)
    swapped = lax.ppermute(own, "dp", cores)
    grad_weight = finish(scalar(1 - core), swapped, finish(scalar(core), own))
    grad_weight = grad_weight.reshape(out_weight.shape)
    return (grad_query[None], grad_key[None], grad_value[None], grad_weight)


def solution(mesh):
    return jax.shard_map(
        per_device,
        mesh=mesh,
        in_specs=(
            P("dp", "grp", None),
            P("dp", "grp", None),
            P("dp", "grp", None),
            P("dp", "grp", None),
            P(),
            P("dp", None),
        ),
        out_specs=(P("dp", "grp", None), P("dp", "grp", None), P("dp", "grp", None), P()),
        check_vma=False,
    )
```

time: 853 us -> 157 us (0.18)
  waiting for transfers between devices: 589 us -> 55.4 us
  matrix products: 185 us -> 0 us
  starting transfers between devices: 0.2 us -> 50.4 us
  Pallas kernels: 0 us -> 44.1 us
  other arithmetic: 43.2 us -> 1.27 us
  between operations: 13.8 us -> 0.73 us
  local copies, waits for them, and re-layouts: 16.1 us -> 4.37 us
    reduce_scatter x2 -> x0, waiting for transfers between devices: 260 us -> none  [the longest x1 131 us: per_device(): lax.psum_scatter(grad_key_part, 'grp', scatter_dimension=0, tiled=True)]
    dot_general x98 -> x0, matrix products: 185 us -> none  [the longest x33 67.3 us: outer(): lax.dot_general(left, right, (((0,), (0,)), ((), ())), preferred_element_...]
    all_gather x2 -> x0, waiting for transfers between devices: 172 us -> none  [the longest x1 89.8 us: per_device(): lax.all_gather(value_own, 'grp', axis=0, tiled=True)]
    psum x1 -> x0, waiting for transfers between devices: 156 us -> none  [per_device(): lax.psum(weight_term, ('grp', 'dp')) * (1.0 / math.sqrt(total_rows))]
    pallas_call x0 -> x16, Pallas kernels: none -> 44.1 us  [the longest x2 23.5 us: attention(): pl.pallas_call(attention_kernel, grid=(1,), in_specs=[smem, smem, whole(p...]
    all_to_all x0 -> x4, waiting for transfers between devices: none -> 38 us  [the longest x1 21.4 us: per_device(): lax.all_to_all(copies, both, 0, 0, axis_index_groups=same_core, tiled=True)]
    ppermute x0 -> x15, starting transfers between devices: none -> 26.7 us  [the longest x2 5.24 us: per_device(): grads_right = [lax.ppermute(half, 'grp', down) for half in grads_late]]
    all_to_all x0 -> x4, starting transfers between devices: none -> 23.7 us  [the longest x1 7.6 us: per_device(): lax.all_to_all(copies, both, 0, 0, axis_index_groups=same_core, tiled=True)]
  transfers between devices with their start and end apart: 5 -> 19, of which waited for: 5 -> 13; matrix products, arithmetic and copies ran while one was open for 3% -> 1% of each run, Pallas kernels for 0% -> 24%
where the time goes in v2:
time: 157 us; the launch traced here: 156 us
  waiting for transfers between devices  55.4 us (35%)
  starting transfers between devices  50.4 us (32%)
  Pallas kernels  44.1 us (28%)
  local copies, waits for them, and re-layouts  4.37 us (3%)
    pallas_call x2, Pallas kernels, attention(): pl.pallas_call(attention_kernel, grid=(1,), in_specs=[smem, smem, whole(p...  23.5 us
    all_to_all x1, waiting for transfers between devices, per_device(): lax.all_to_all(copies, both, 0, 0, axis_index_groups=same_core, tiled=True)  21.4 us
    all_to_all x1, waiting for transfers between devices, per_device(): first = lax.all_to_all(packed_first, 'grp', 0, 0, tiled=True).reshape(shape)  15.6 us
    all_to_all x1, starting transfers between devices, per_device(): lax.all_to_all(copies, both, 0, 0, axis_index_groups=same_core, tiled=True)  7.6 us
    all_to_all x1, starting transfers between devices, per_device(): first = lax.all_to_all(packed_first, 'grp', 0, 0, tiled=True).reshape(shape)  7.47 us
    pallas_call x2, Pallas kernels, pack(): pl.pallas_call(pack_kernel, grid=(1,), in_specs=[pl.BlockSpec((width // 2...  7.45 us
    pallas_call x2, Pallas kernels, finish(): pl.pallas_call(finish_kernel, grid_spec=pltpu.PrefetchScalarGridSpec(num_...  6.02 us
    ppermute x3, waiting for transfers between devices, per_device(): lax.ppermute(parts[k], 'dp', [(i, i ^ 4 * k) for i in range(16)])  5.5 us
  transfers between devices with their start and end apart: 19, of which 13 were waited for; matrix products, arithmetic and copies ran while one was open for 1% of the time, Pallas kernels for 24%

profile of v2, /device:TPU:1, one launch (start us, length us, event | category | flops | bytes accessed | tf_op | source)
XLA Modules:
  0.0 156.3 jit_solution(8770137427331937739)
XLA Ops:
  0.6 3.7 %pack_heads.2 = (bf16[8,2,4,80,128]{4,3,2,1,0:T(8,128)(2,1)}, bf16[128,1280]{1,0:T(8,128)(2,1)}, bf16[128,1280]{1,0:T(8,128)(2,1)}) custom-call(bf16[1280,1280]{1,0:T(8,128)(2,1)} %weight_ref.3, bf16[256,1280]{1,0:T(8,128)(2,1)} %bitcast.55, bf16[256,1280]{1,0:T(8,128)(2,1)} %bitcast.58, bf16[256,1280]{1,0:T(8,128)(2,1)} %bitcast.60, bf16[256,1280]{1,0:T(8,128)(2,1)} %bitcast.62), custom_call_target="tpu_custom_call" | custom-call | flops 419430400 | bytes 5242880 | tf_op jit(solution)/shard_map/pack_heads/pallas_call | solution.py:96
  4.4 7.5 %all-to-all-start = ((bf16[8,2,4,80,128]{4,3,2,1,0:T(8,128)(2,1)}), bf16[8,2,4,80,128]{4,3,2,1,0:T(8,128)(2,1)}, u32[]{:S(2)}, u32[]{:S(2)}) async-start(bf16[8,2,4,80,128]{4,3,2,1,0:T(8,128)(2,1)} %get-tuple-element.19.refs_0_), calls=%async_computation | async-start | bytes 2621440 | tf_op jit(solution)/shard_map/all_to_all | solution.py:433
  11.8 3.7 %pack_heads.3 = (bf16[8,2,4,80,128]{4,3,2,1,0:T(8,128)(2,1)}, bf16[128,1280]{1,0:T(8,128)(2,1)}, bf16[128,1280]{1,0:T(8,128)(2,1)}) custom-call(bf16[1280,1280]{1,0:T(8,128)(2,1)} %weight_ref.3, bf16[256,1280]{1,0:T(8,128)(2,1)} %bitcast.56, bf16[256,1280]{1,0:T(8,128)(2,1)} %bitcast.59, bf16[256,1280]{1,0:T(8,128)(2,1)} %bitcast.61, ...), custom_call_target="tpu_custom_call" | custom-call | flops 419430400 | bytes 5242880 | tf_op jit(solution)/shard_map/pack_heads/pallas_call | solution.py:96
  15.5 15.6 %all-to-all-done = bf16[8,2,4,80,128]{4,3,2,1,0:T(8,128)(2,1)} async-done(((bf16[8,2,4,80,128]{4,3,2,1,0:T(8,128)(2,1)}), bf16[8,2,4,80,128]{4,3,2,1,0:T(8,128)(2,1)}, u32[]{:S(2)}, u32[]{:S(2)}) %all-to-all-start) | async-done | bytes 1310752 | tf_op jit(solution)/shard_map/all_to_all | solution.py:433
  31.1 4.3 %all-to-all-start.1 = ((bf16[8,2,4,80,128]{4,3,2,1,0:T(8,128)(2,1)}), bf16[8,2,4,80,128]{4,3,2,1,0:T(8,128)(2,1)}, u32[]{:S(2)}, u32[]{:S(2)}) async-start(bf16[8,2,4,80,128]{4,3,2,1,0:T(8,128)(2,1)} %once.8), calls=%async_computation.1 | async-start | bytes 2621440 | tf_op jit(solution)/shard_map/all_to_all | solution.py:435
  35.4 2.6 %collective-permute-start.3 = (bf16[128,1280]{1,0:T(8,128)(2,1)}, bf16[128,1280]{1,0:T(8,128)(2,1)S(1)}, u32[]{:S(2)}, u32[]{:S(2)}) collective-permute-start(bf16[128,1280]{1,0:T(8,128)(2,1)} %once.10), channel_id=1, source_target_pairs={{0,96},{16,112},{32,0},{48,16},{64,32},{80,48},{96,64},{112,80},{1... | collective-permute-start | bytes 983048 | tf_op jit(solution)/shard_map/ppermute | solution.py:441
  38.0 2.7 %collective-permute-start.2 = (bf16[128,1280]{1,0:T(8,128)(2,1)}, bf16[128,1280]{1,0:T(8,128)(2,1)S(1)}, u32[]{:S(2)}, u32[]{:S(2)}) collective-permute-start(bf16[128,1280]{1,0:T(8,128)(2,1)} %once.9), channel_id=1, source_target_pairs={{0,96},{16,112},{32,0},{48,16},{64,32},{80,48},{96,64},{112,80},{1... | collective-permute-start | bytes 983048 | tf_op jit(solution)/shard_map/ppermute | solution.py:441
  40.7 11.8 %attention_grads.2 = (bf16[160,1024]{1,0:T(8,128)(2,1)}, bf16[160,1024]{1,0:T(8,128)(2,1)}, bf16[16,3,160,128]{3,2,1,0:T(8,128)(2,1)}) custom-call(s32[1,16]{1,0:T(1,128)} %ids_ref.3, s32[1]{0:T(128)} %bitcast.me_ref, bf16[16,4,80,128]{3,2,1,0:T(8,128)(2,1)} %bitcast.5.refs_1_.in_ref), custom_call_target="tpu_custom_call" | custom-call | flops 12079595520 | bytes 4194304 | tf_op jit(solution)/shard_map/attention_grads/pallas_call | solution.py:202
  53.5 11.7 %attention_grads.3 = (bf16[160,1024]{1,0:T(8,128)(2,1)}, bf16[160,1024]{1,0:T(8,128)(2,1)}, bf16[16,3,160,128]{3,2,1,0:T(8,128)(2,1)}) custom-call(s32[1,16]{1,0:T(1,128)} %ids_ref.3, s32[1]{0:T(128)} %bitcast.me_ref, bf16[16,4,80,128]{3,2,1,0:T(8,128)(2,1)} %bitcast.6.in_ref, ...), custom_call_target="tpu_custom_call", output_to_operand_aliasing={{0}: (3, {}), {1}: (4, {}), {2}: (5, {})} | custom-call | flops 12079595520 | bytes 4194304 | tf_op jit(solution)/shard_map/attention_grads/pallas_call | solution.py:202
  67.4 2.5 %collective-permute-start.4 = (bf16[160,1024]{1,0:T(8,128)(2,1)}, bf16[160,1024]{1,0:T(8,128)(2,1)S(1)}, u32[]{:S(2)}, u32[]{:S(2)}) collective-permute-start(bf16[160,1024]{1,0:T(8,128)(2,1)} %once.13), channel_id=1, source_target_pairs={{0,16},{16,0},{32,48},{48,32},{64,80},{80,64},{96,112},{112,96},{1... | collective-permute-start | bytes 983048 | tf_op jit(solution)/shard_map/ppermute | solution.py:447
  72.6 2.5 %collective-permute-done.4.refs_1_.other_ref = bf16[160,1024]{1,0:T(8,128)(2,1)S(1)} collective-permute-done((bf16[160,1024]{1,0:T(8,128)(2,1)}, bf16[160,1024]{1,0:T(8,128)(2,1)S(1)}, u32[]{:S(2)}, u32[]{:S(2)}) %collective-permute-start.4) | collective-permute-done | bytes 327712 | tf_op jit(solution)/shard_map/ppermute | solution.py:447
  79.3 4.3 %all-to-all-start.2 = ((bf16[8,2,3,160,128]{4,3,2,1,0:T(8,128)(2,1)}), bf16[8,2,3,160,128]{4,3,2,1,0:T(8,128)(2,1)}, u32[]{:S(2)}, u32[]{:S(2)}) async-start(bf16[8,2,3,160,128]{4,3,2,1,0:T(8,128)(2,1)} %bitcast.54), calls=%async_computation.2 | async-start | bytes 3932160 | tf_op jit(solution)/shard_map/all_to_all | solution.py:449
  83.6 4.0 %weight_terms.1 = (bf16[4,4,112,128]{3,2,1,0:T(8,128)(2,1)}, bf16[4,4,112,128]{3,2,1,0:T(8,128)(2,1)}) custom-call(s32[1]{0:T(128)} %bitcast.me_ref, s32[1]{0:T(128)} %bitcast.12.column_ref, bf16[160,1024]{1,0:T(8,128)(2,1)} %get-tuple-element.31.keep_ref, bf16[160,1024]{1,0:T(8,128)(2,1)} %copy-done.4, bf16[256,1280]{1,0:T(8,128)(2,1)} %bitcast.57, ...), custom_call_target="tpu_custom_call" | custom-call | flops 838860800 | bytes 6291456 | tf_op jit(solution)/shard_map/weight_terms/pallas_call | solution.py:296
  87.7 3.8 %collective-permute-start.7 = (bf16[4,4,112,128]{3,2,1,0:T(8,128)(2,1)}, bf16[4,4,112,128]{3,2,1,0:T(8,128)(2,1)S(1)}, u32[]{:S(2)}, u32[]{:S(2)}) collective-permute-start(bf16[4,4,112,128]{3,2,1,0:T(8,128)(2,1)} %get-tuple-element.33), channel_id=1, source_target_pairs={{0,1},{1,0},{2,3},{3,2},{4,5},{5,4},{6,7},{7,6},{8,9},{9,8},{10,11... | collective-permute-start | bytes 1376264 | tf_op jit(solution)/shard_map/ppermute | solution.py:454
  94.3 3.9 %collective-permute-start.10 = (bf16[4,112,128]{2,1,0:T(8,128)(2,1)S(1)}, bf16[4,112,128]{2,1,0:T(8,128)(2,1)S(1)}, u32[]{:S(2)}, u32[]{:S(2)}) collective-permute-start(bf16[4,112,128]{2,1,0:T(8,128)(2,1)S(1)} %get-tuple-element.35), channel_id=1, source_target_pairs={{0,12},{1,13},{2,14},{3,15},{4,8},{5,9},{6,10},{7,11},{8,4},{9,5},... | collective-permute-start | bytes 344072 | tf_op jit(solution)/shard_map/ppermute | solution.py:457
  98.9 4.1 %collective-permute-done.10 = bf16[4,112,128]{2,1,0:T(8,128)(2,1)S(1)} collective-permute-done((bf16[4,112,128]{2,1,0:T(8,128)(2,1)S(1)}, bf16[4,112,128]{2,1,0:T(8,128)(2,1)S(1)}, u32[]{:S(2)}, u32[]{:S(2)}) %collective-permute-start.10) | collective-permute-done | bytes 114720 | tf_op jit(solution)/shard_map/ppermute | solution.py:457
  104.9 3.1 %collective-permute-start.13 = (bf16[112,128]{1,0:T(8,128)(2,1)S(1)}, bf16[112,128]{1,0:T(8,128)(2,1)S(1)}, u32[]{:S(2)}, u32[]{:S(2)}) collective-permute-start(bf16[112,128]{1,0:T(8,128)(2,1)S(1)} %get-tuple-element.39), channel_id=1, source_target_pairs={{0,18},{1,19},{2,16},{3,17},{4,22},{5,23},{6,20},{7,21},{8,26},{9,... | collective-permute-start | bytes 86024 | tf_op jit(solution)/shard_map/ppermute | solution.py:461
  109.9 2.5 %collective-permute-done.12 = bf16[112,128]{1,0:T(8,128)(2,1)S(1)} collective-permute-done((bf16[112,128]{1,0:T(8,128)(2,1)S(1)}, bf16[112,128]{1,0:T(8,128)(2,1)S(1)}, u32[]{:S(2)}, u32[]{:S(2)}) %collective-permute-start.12) | collective-permute-done | bytes 28704 | tf_op jit(solution)/shard_map/ppermute | solution.py:461
  113.9 7.6 %all-to-all-start.3 = ((bf16[64,112,128]{2,1,0:T(8,128)(2,1)}), bf16[64,112,128]{2,1,0:T(8,128)(2,1)}, u32[]{:S(2)}, u32[]{:S(2)}) async-start(bf16[64,112,128]{2,1,0:T(8,128)(2,1)} %broadcast_in_dim.18), calls=%async_computation.3 | async-start | bytes 3670016 | tf_op jit(solution)/shard_map/all_to_all | solution.py:467
  121.5 3.0 %unpack_heads.1 = (bf16[256,1280]{1,0:T(8,128)(2,1)}, bf16[256,1280]{1,0:T(8,128)(2,1)}, bf16[256,1280]{1,0:T(8,128)(2,1)}) custom-call(bf16[8,2,3,160,128]{4,3,2,1,0:T(8,128)(2,1)} %all-to-all-done.2.in_ref), custom_call_target="tpu_custom_call" | custom-call | bytes 4194304 | tf_op jit(solution)/shard_map/unpack_heads/pallas_call | solution.py:240
  124.5 21.4 %all-to-all-done.3.refs_0_ = bf16[64,112,128]{2,1,0:T(8,128)(2,1)} async-done(((bf16[64,112,128]{2,1,0:T(8,128)(2,1)}), bf16[64,112,128]{2,1,0:T(8,128)(2,1)}, u32[]{:S(2)}, u32[]{:S(2)}) %all-to-all-start.3) | async-done | bytes 1835040 | tf_op jit(solution)/shard_map/all_to_all | solution.py:467
  145.9 3.6 %collective-permute-start.14 = (bf16[8,896,128]{2,1,0:T(8,128)(2,1)}, bf16[8,896,128]{2,1,0:T(8,128)(2,1)}, u32[]{:S(2)}, u32[]{:S(2)}) collective-permute-start(bf16[8,896,128]{2,1,0:T(8,128)(2,1)} %bitcast.24.in_ref), channel_id=1, source_target_pairs={{0,1},{1,0},{2,3},{3,2},{4,5},{5,4},{6,7},{7,6},{8,9},{9,8},{10,11... | collective-permute-start | bytes 5505032 | tf_op jit(solution)/shard_map/ppermute | solution.py:470
  149.5 3.0 %finish_weight.2.refs_0_ = f32[2,8,80,1280]{3,2,1,0:T(8,128)} custom-call(s32[1]{0:T(128)} %bitcast.25.core_ref, bf16[8,896,128]{2,1,0:T(8,128)(2,1)} %bitcast.24.in_ref), custom_call_target="tpu_custom_call" | custom-call | bytes 5242880 | tf_op jit(solution)/shard_map/finish_weight/pallas_call | solution.py:403
  153.3 3.0 %finish_weight.3 = f32[2,8,80,1280]{3,2,1,0:T(8,128)} custom-call(s32[1]{0:T(128)} %bitcast.11.core_ref, bf16[8,896,128]{2,1,0:T(8,128)(2,1)} %collective-permute-done.14.in_ref, f32[2,8,80,1280]{3,2,1,0:T(8,128)} %finish_weight.2.refs_0_), custom_call_target="tpu_custom_call", output_to_operand_aliasing={{}: (2, {})} | custom-call | bytes 5242880 | tf_op jit(solution)/shard_map/finish_weight/pallas_call | solution.py:403
  (50 shorter events, 19.6 us)
Async XLA Ops:
  4.4 26.8 %all-to-all-start = ((bf16[8,2,4,80,128]{4,3,2,1,0:T(8,128)(2,1)}), bf16[8,2,4,80,128]{4,3,2,1,0:T(8,128)(2,1)}, u32[]{:S(2)}, u32[]{:S(2)}) async-start(bf16[8,2,4,80,128]{4,3,2,1,0:T(8,128)(2,1)} %get-tuple-element.19.refs_0_), calls=%async_computation | async-start | bytes 2621440 | tf_op jit(solution)/shard_map/all_to_all | solution.py:433
  31.1 22.4 %all-to-all-start.1 = ((bf16[8,2,4,80,128]{4,3,2,1,0:T(8,128)(2,1)}), bf16[8,2,4,80,128]{4,3,2,1,0:T(8,128)(2,1)}, u32[]{:S(2)}, u32[]{:S(2)}) async-start(bf16[8,2,4,80,128]{4,3,2,1,0:T(8,128)(2,1)} %once.8), calls=%async_computation.1 | async-start | bytes 2621440 | tf_op jit(solution)/shard_map/all_to_all | solution.py:435
  35.4 31.2 %collective-permute-start.3 = (bf16[128,1280]{1,0:T(8,128)(2,1)}, bf16[128,1280]{1,0:T(8,128)(2,1)S(1)}, u32[]{:S(2)}, u32[]{:S(2)}) collective-permute-start(bf16[128,1280]{1,0:T(8,128)(2,1)} %once.10), channel_id=1, source_target_pairs={{0,96},{16,112},{32,0},{48,16},{64,32},{80,48},{96,64},{112,80},{1... | collective-permute-start | bytes 983048 | tf_op jit(solution)/shard_map/ppermute | solution.py:441
  38.0 27.9 %collective-permute-start.1 = (bf16[128,1280]{1,0:T(8,128)(2,1)}, bf16[128,1280]{1,0:T(8,128)(2,1)S(1)}, u32[]{:S(2)}, u32[]{:S(2)}) collective-permute-start(bf16[128,1280]{1,0:T(8,128)(2,1)} %once.10), channel_id=1, source_target_pairs={{0,32},{16,48},{32,64},{48,80},{64,96},{80,112},{96,0},{112,16},{1... | collective-permute-start | bytes 983048 | tf_op jit(solution)/shard_map/ppermute | solution.py:440
  38.0 27.2 %collective-permute-start.2 = (bf16[128,1280]{1,0:T(8,128)(2,1)}, bf16[128,1280]{1,0:T(8,128)(2,1)S(1)}, u32[]{:S(2)}, u32[]{:S(2)}) collective-permute-start(bf16[128,1280]{1,0:T(8,128)(2,1)} %once.9), channel_id=1, source_target_pairs={{0,96},{16,112},{32,0},{48,16},{64,32},{80,48},{96,64},{112,80},{1... | collective-permute-start | bytes 983048 | tf_op jit(solution)/shard_map/ppermute | solution.py:441
  40.7 26.0 %collective-permute-start = (bf16[128,1280]{1,0:T(8,128)(2,1)}, bf16[128,1280]{1,0:T(8,128)(2,1)}, u32[]{:S(2)}, u32[]{:S(2)}) collective-permute-start(bf16[128,1280]{1,0:T(8,128)(2,1)} %once.9), channel_id=1, source_target_pairs={{0,32},{16,48},{32,64},{48,80},{64,96},{80,112},{96,0},{112,16},{1... | collective-permute-start | bytes 983048 | tf_op jit(solution)/shard_map/ppermute | solution.py:440
  65.9 5.7 %copy-start.3 = (bf16[128,1280]{1,0:T(8,128)(2,1)S(1)}, bf16[128,1280]{1,0:T(8,128)(2,1)}, u32[]{:S(2)}) copy-start(bf16[128,1280]{1,0:T(8,128)(2,1)} %once.12.refs_3_.refs_1_) | copy-start | bytes 983044
  65.9 0.7 copy-start
  66.7 3.2 %copy-start.1 = (bf16[128,1280]{1,0:T(8,128)(2,1)S(1)}, bf16[128,1280]{1,0:T(8,128)(2,1)}, u32[]{:S(2)}) copy-start(bf16[128,1280]{1,0:T(8,128)(2,1)} %once.11.refs_2_.refs_6_) | copy-start | bytes 983044
  67.4 7.6 %collective-permute-start.4 = (bf16[160,1024]{1,0:T(8,128)(2,1)}, bf16[160,1024]{1,0:T(8,128)(2,1)S(1)}, u32[]{:S(2)}, u32[]{:S(2)}) collective-permute-start(bf16[160,1024]{1,0:T(8,128)(2,1)} %once.13), channel_id=1, source_target_pairs={{0,16},{16,0},{32,48},{48,32},{64,80},{80,64},{96,112},{112,96},{1... | collective-permute-start | bytes 983048 | tf_op jit(solution)/shard_map/ppermute | solution.py:447
  69.9 7.4 %collective-permute-start.6 = (bf16[128,1280]{1,0:T(8,128)(2,1)S(1)}, bf16[128,1280]{1,0:T(8,128)(2,1)S(1)}, u32[]{:S(2)}, u32[]{:S(2)}) collective-permute-start(bf16[128,1280]{1,0:T(8,128)(2,1)S(1)} %copy-done.1), channel_id=1, source_target_pairs={{0,32},{16,48},{32,64},{48,80},{64,96},{80,112},{96,0},{112,16},{1... | collective-permute-start | bytes 983048 | tf_op jit(solution)/shard_map/ppermute | solution.py:445
  71.6 6.9 %collective-permute-start.5 = (bf16[128,1280]{1,0:T(8,128)(2,1)S(1)}, bf16[128,1280]{1,0:T(8,128)(2,1)S(1)}, u32[]{:S(2)}, u32[]{:S(2)}) collective-permute-start(bf16[128,1280]{1,0:T(8,128)(2,1)S(1)} %copy-done.3), channel_id=1, source_target_pairs={{0,96},{16,112},{32,0},{48,16},{64,32},{80,48},{96,64},{112,80},{1... | collective-permute-start | bytes 983048 | tf_op jit(solution)/shard_map/ppermute | solution.py:445
  75.0 4.2 %copy-start.4 = (bf16[160,1024]{1,0:T(8,128)(2,1)}, bf16[160,1024]{1,0:T(8,128)(2,1)S(1)}, u32[]{:S(2)}) copy-start(bf16[160,1024]{1,0:T(8,128)(2,1)S(1)} %collective-permute-done.4.refs_1_.other_ref) | copy-start | bytes 983044
  77.3 1.2 copy-start.5
  79.3 33.1 %all-to-all-start.2 = ((bf16[8,2,3,160,128]{4,3,2,1,0:T(8,128)(2,1)}), bf16[8,2,3,160,128]{4,3,2,1,0:T(8,128)(2,1)}, u32[]{:S(2)}, u32[]{:S(2)}) async-start(bf16[8,2,3,160,128]{4,3,2,1,0:T(8,128)(2,1)} %bitcast.54), calls=%async_computation.2 | async-start | bytes 3932160 | tf_op jit(solution)/shard_map/all_to_all | solution.py:449
  87.7 5.5 %collective-permute-start.7 = (bf16[4,4,112,128]{3,2,1,0:T(8,128)(2,1)}, bf16[4,4,112,128]{3,2,1,0:T(8,128)(2,1)S(1)}, u32[]{:S(2)}, u32[]{:S(2)}) collective-permute-start(bf16[4,4,112,128]{3,2,1,0:T(8,128)(2,1)} %get-tuple-element.33), channel_id=1, source_target_pairs={{0,1},{1,0},{2,3},{3,2},{4,5},{5,4},{6,7},{7,6},{8,9},{9,8},{10,11... | collective-permute-start | bytes 1376264 | tf_op jit(solution)/shard_map/ppermute | solution.py:454
  94.3 8.7 %collective-permute-start.10 = (bf16[4,112,128]{2,1,0:T(8,128)(2,1)S(1)}, bf16[4,112,128]{2,1,0:T(8,128)(2,1)S(1)}, u32[]{:S(2)}, u32[]{:S(2)}) collective-permute-start(bf16[4,112,128]{2,1,0:T(8,128)(2,1)S(1)} %get-tuple-element.35), channel_id=1, source_target_pairs={{0,12},{1,13},{2,14},{3,15},{4,8},{5,9},{6,10},{7,11},{8,4},{9,5},... | collective-permute-start | bytes 344072 | tf_op jit(solution)/shard_map/ppermute | solution.py:457
  98.2 5.6 %collective-permute-start.9 = (bf16[4,112,128]{2,1,0:T(8,128)(2,1)S(1)}, bf16[4,112,128]{2,1,0:T(8,128)(2,1)S(1)}, u32[]{:S(2)}, u32[]{:S(2)}) collective-permute-start(bf16[4,112,128]{2,1,0:T(8,128)(2,1)S(1)} %get-tuple-element.36), channel_id=1, source_target_pairs={{0,8},{1,9},{2,10},{3,11},{4,12},{5,13},{6,14},{7,15},{8,0},{9,1},... | collective-permute-start | bytes 344072 | tf_op jit(solution)/shard_map/ppermute | solution.py:457
  98.2 6.2 %collective-permute-start.8 = (bf16[4,112,128]{2,1,0:T(8,128)(2,1)S(1)}, bf16[4,112,128]{2,1,0:T(8,128)(2,1)S(1)}, u32[]{:S(2)}, u32[]{:S(2)}) collective-permute-start(bf16[4,112,128]{2,1,0:T(8,128)(2,1)S(1)} %get-tuple-element.37), channel_id=1, source_target_pairs={{0,4},{1,5},{2,6},{3,7},{4,0},{5,1},{6,2},{7,3},{8,12},{9,13},{10,... | collective-permute-start | bytes 344072 | tf_op jit(solution)/shard_map/ppermute | solution.py:457
  104.5 4.3 %collective-permute-start.11 = (bf16[112,128]{1,0:T(8,128)(2,1)S(1)}, bf16[112,128]{1,0:T(8,128)(2,1)S(1)}, u32[]{:S(2)}, u32[]{:S(2)}) collective-permute-start(bf16[112,128]{1,0:T(8,128)(2,1)S(1)} %get-tuple-element.38), channel_id=1, source_target_pairs={{0,2},{1,3},{2,0},{3,1},{4,6},{5,7},{6,4},{7,5},{8,10},{9,11},{10,... | collective-permute-start | bytes 86024 | tf_op jit(solution)/shard_map/ppermute | solution.py:461
  104.9 5.0 %collective-permute-start.13 = (bf16[112,128]{1,0:T(8,128)(2,1)S(1)}, bf16[112,128]{1,0:T(8,128)(2,1)S(1)}, u32[]{:S(2)}, u32[]{:S(2)}) collective-permute-start(bf16[112,128]{1,0:T(8,128)(2,1)S(1)} %get-tuple-element.39), channel_id=1, source_target_pairs={{0,18},{1,19},{2,16},{3,17},{4,22},{5,23},{6,20},{7,21},{8,26},{9,... | collective-permute-start | bytes 86024 | tf_op jit(solution)/shard_map/ppermute | solution.py:461
  108.1 4.3 %collective-permute-start.12 = (bf16[112,128]{1,0:T(8,128)(2,1)S(1)}, bf16[112,128]{1,0:T(8,128)(2,1)S(1)}, u32[]{:S(2)}, u32[]{:S(2)}) collective-permute-start(bf16[112,128]{1,0:T(8,128)(2,1)S(1)} %get-tuple-element.40), channel_id=1, source_target_pairs={{0,16},{1,17},{2,18},{3,19},{4,20},{5,21},{6,22},{7,23},{8,24},{9,... | collective-permute-start | bytes 86024 | tf_op jit(solution)/shard_map/ppermute | solution.py:461
  113.9 32.0 %all-to-all-start.3 = ((bf16[64,112,128]{2,1,0:T(8,128)(2,1)}), bf16[64,112,128]{2,1,0:T(8,128)(2,1)}, u32[]{:S(2)}, u32[]{:S(2)}) async-start(bf16[64,112,128]{2,1,0:T(8,128)(2,1)} %broadcast_in_dim.18), calls=%async_computation.3 | async-start | bytes 3670016 | tf_op jit(solution)/shard_map/all_to_all | solution.py:467
  145.9 7.4 %collective-permute-start.14 = (bf16[8,896,128]{2,1,0:T(8,128)(2,1)}, bf16[8,896,128]{2,1,0:T(8,128)(2,1)}, u32[]{:S(2)}, u32[]{:S(2)}) collective-permute-start(bf16[8,896,128]{2,1,0:T(8,128)(2,1)} %bitcast.24.in_ref), channel_id=1, source_target_pairs={{0,1},{1,0},{2,3},{3,2},{4,5},{5,4},{6,7},{7,6},{8,9},{9,8},{10,11... | collective-permute-start | bytes 5505032 | tf_op jit(solution)/shard_map/ppermute | solution.py:470
  (3 other events, 2.2 us)

commit v3 on v2

--- a/solution.py
+++ b/solution.py
@@ -103,10 +103,10 @@
             column,
             column,
         ]
-        + [pl.BlockSpec(memory_space=pl.ANY)] * len(after),
+        + [pl.BlockSpec(memory_space=pltpu.HBM)] * len(after),
         out_specs=[whole(shape.shape) for shape in shapes],
         out_shape=shapes,
-        compiler_params=pltpu.CompilerParams(vmem_limit_bytes=63 * 2**20),
+        compiler_params=pltpu.CompilerParams(vmem_limit_bytes=65408 * 2**10),
         cost_estimate=pl.CostEstimate(
             flops=rows * width * width, bytes_accessed=5 * 2**20, transcendentals=0
         ),
@@ -194,26 +194,26 @@
 
 def attention(head, ids, me, packed, *before):
     tokens = GBLOCKS * BLK
-    shapes = [jax.ShapeDtypeStruct((PAIR, tokens // 2), bf16)] * 2
+    shapes = [jax.ShapeDtypeStruct((DH, tokens // 2), bf16)] * 2
     shapes += [jax.ShapeDtypeStruct((GBLOCKS, 3, PAIR, BLK), bf16)]
     smem = pl.BlockSpec(memory_space=pltpu.SMEM)
-    blocks = [pl.BlockSpec((DH, tokens // 2), lambda i: (head, 0))] * 2
+    blocks = [whole(shapes[0].shape)] * 2
     blocks += [pl.BlockSpec((GBLOCKS, 3, DH, BLK), lambda i: (0, 0, head, 0))]
     return pl.pallas_call(
         attention_kernel,
         grid=(1,),
         in_specs=[smem, smem, whole(packed.shape)]
-        + [pl.BlockSpec(memory_space=pl.ANY)] * len(before),
+        + [pl.BlockSpec(memory_space=pltpu.HBM)] * len(before),
         out_specs=blocks,
         out_shape=shapes,
-        input_output_aliases={3 + i: i for i in range(len(before))},
+        input_output_aliases={3: 2} if before else {},
         scratch_shapes=[
             pltpu.VMEM((4, BLK, tokens), bf16),
             pltpu.VMEM((2, tokens, BLK), bf16),
             pltpu.VMEM((3, DH, tokens), f32),
             pltpu.VMEM((DH, tokens), bf16),
         ],
-        compiler_params=pltpu.CompilerParams(vmem_limit_bytes=63 * 2**20),
+        compiler_params=pltpu.CompilerParams(vmem_limit_bytes=65408 * 2**10),
         cost_estimate=pl.CostEstimate(
             flops=2 * 6 * 3 * 160 * BLK * BLK * BLK,
             bytes_accessed=4 * 2**20,
@@ -240,7 +240,7 @@
     return pl.pallas_call(
         unpack_kernel,
         out_shape=[jax.ShapeDtypeStruct((2 * BLK, width), bf16)] * count,
-        compiler_params=pltpu.CompilerParams(vmem_limit_bytes=63 * 2**20),
+        compiler_params=pltpu.CompilerParams(vmem_limit_bytes=24 * 2**20),
         cost_estimate=pl.CostEstimate(flops=0, bytes_accessed=4 * 2**20, transcendentals=0),
         name="unpack_heads",
     )(received)
@@ -249,13 +249,13 @@
 CROWS = 112
 
 
-def weight_kernel(me_ref, column_ref, keep_ref, other_ref, *refs):
-    grads_refs, out_refs, both_ref, ring_ref, rows_ref = refs[:-5], refs[-5:-3], *refs[-3:-1], refs[-1]
+def weight_kernel(me_ref, column_ref, *refs):
+    grads_refs, out_refs, both_ref, ring_ref, rows_ref = refs[4:-5], refs[-5:-3], *refs[-3:-1], refs[-1]
     core = lax.rem(column_ref[0], 2)
     low = lax.rem(lax.div(column_ref[0], 2), 2)
     z = lax.div(column_ref[0], 4)
-    both_ref[:PAIR] = keep_ref[...]
-    both_ref[PAIR:] = other_ref[...]
+    for i in range(4):
+        both_ref[i * DH : (i + 1) * DH] = refs[i][...]
     gx = lax.div(me_ref[0], 2)
     offset = gx * (2 * BLK)
     first = 0
@@ -291,24 +291,24 @@
             pl.when(core != half)(lambda: store(out_refs[1]))
 
 
-def weight_terms(me, column, keep, other, grads):
+def weight_terms(me, column, atts, grads):
     vmem = pl.BlockSpec(memory_space=pltpu.VMEM)
     return pl.pallas_call(
         weight_kernel,
-        in_specs=[pl.BlockSpec(memory_space=pltpu.SMEM)] * 2 + [vmem] * (2 + len(grads)),
+        in_specs=[pl.BlockSpec(memory_space=pltpu.SMEM)] * 2 + [vmem] * (4 + len(grads)),
         out_specs=[vmem] * 2,
         out_shape=[jax.ShapeDtypeStruct((4, 4, CROWS, BLK), bf16)] * 2,
         scratch_shapes=[
-            pltpu.VMEM((2 * PAIR, keep.shape[1]), bf16),
-            pltpu.VMEM((2 * PAIR, keep.shape[1]), bf16),
+            pltpu.VMEM((2 * PAIR, atts[0].shape[1]), bf16),
+            pltpu.VMEM((2 * PAIR, atts[0].shape[1]), bf16),
             pltpu.VMEM((8 * CROWS, BLK), bf16),
         ],
-        compiler_params=pltpu.CompilerParams(vmem_limit_bytes=63 * 2**20),
+        compiler_params=pltpu.CompilerParams(vmem_limit_bytes=65408 * 2**10),
         cost_estimate=pl.CostEstimate(
             flops=2 * 2 * PAIR * 4 * grads[0].size, bytes_accessed=6 * 2**20, transcendentals=0
         ),
         name="weight_terms",
-    )(me, column, keep, other, *grads)
+    )(me, column, *atts, *grads)
 
 
 def add_kernel(*refs):
@@ -325,7 +325,7 @@
     return pl.pallas_call(
         add_kernel,
         out_shape=[jax.ShapeDtypeStruct(shape, bf16)] * 4,
-        compiler_params=pltpu.CompilerParams(vmem_limit_bytes=63 * 2**20),
+        compiler_params=pltpu.CompilerParams(vmem_limit_bytes=65408 * 2**10),
         cost_estimate=pl.CostEstimate(
             flops=len(arrays) * arrays[0].size, bytes_accessed=2**20, transcendentals=0
         ),
@@ -338,14 +338,15 @@
 
 
 def once(array, *after):
-    anywhere = pl.BlockSpec(memory_space=pl.ANY)
+    anywhere = pl.BlockSpec(memory_space=pltpu.HBM)
     return pl.pallas_call(
         nothing_kernel,
         in_specs=[anywhere] * (1 + len(after)),
         out_specs=anywhere,
         out_shape=jax.ShapeDtypeStruct(array.shape, array.dtype),
         input_output_aliases={0: 0},
-        compiler_params=pltpu.CompilerParams(vmem_limit_bytes=63 * 2**20),
+        compiler_params=pltpu.CompilerParams(vmem_limit_bytes=65408 * 2**10),
+        cost_estimate=pl.CostEstimate(flops=0, bytes_accessed=0, transcendentals=0),
         name="once",
     )(array, *after)
 
@@ -364,7 +365,7 @@
     return pl.pallas_call(
         add_kernel,
         out_shape=[jax.ShapeDtypeStruct(shape, bf16)] * 4,
-        compiler_params=pltpu.CompilerParams(vmem_limit_bytes=63 * 2**20),
+        compiler_params=pltpu.CompilerParams(vmem_limit_bytes=65408 * 2**10),
         cost_estimate=pl.CostEstimate(
             flops=len(arrays) * arrays[0].size, bytes_accessed=2**20, transcendentals=0
         ),
@@ -377,16 +378,32 @@
 
 
 def once(array, *after):
-    anywhere = pl.BlockSpec(memory_space=pl.ANY)
+    anywhere = pl.BlockSpec(memory_space=pltpu.HBM)
     return pl.pallas_call(
         nothing_kernel,
         in_specs=[anywhere] * (1 + len(after)),
         out_specs=anywhere,
         out_shape=jax.ShapeDtypeStruct(array.shape, array.dtype),
         input_output_aliases={0: 0},
-        compiler_params=pltpu.CompilerParams(vmem_limit_bytes=63 * 2**20),
+        compiler_params=pltpu.CompilerParams(vmem_limit_bytes=65408 * 2**10),
+        cost_estimate=pl.CostEstimate(flops=0, bytes_accessed=0, transcendentals=0),
         name="once",
     )(array, *after)
+
+
+def one_kernel(*refs):
+    refs[-1][0, 0] = 1.0
+
+
+def one_after(*after):
+    return pl.pallas_call(
+        one_kernel,
+        in_specs=[pl.BlockSpec(memory_space=pltpu.HBM)] * len(after),
+        out_specs=pl.BlockSpec(memory_space=pltpu.SMEM),
+        out_shape=jax.ShapeDtypeStruct((1, 1), f32),
+        cost_estimate=pl.CostEstimate(flops=0, bytes_accessed=0, transcendentals=0),
+        name="one_after",
+    )(*after)
 
 
 def finish_kernel(core_ref, in_ref, *refs):
@@ -406,12 +423,12 @@
             num_scalar_prefetch=1,
             grid=(2,),
             in_specs=[pl.BlockSpec((4, 8 * CROWS, BLK), lambda i, core: (i, 0, 0))]
-            + [pl.BlockSpec(memory_space=pl.ANY)] * len(before),
+            + [pl.BlockSpec(memory_space=pltpu.HBM)] * len(before),
             out_specs=pl.BlockSpec((2, 4, DH, width // 2), lambda i, core: (0, i, 0, core[0])),
         ),
         out_shape=jax.ShapeDtypeStruct((2, 8, DH, width), f32),
         input_output_aliases={2: 0} if before else {},
-        compiler_params=pltpu.CompilerParams(vmem_limit_bytes=63 * 2**20),
+        compiler_params=pltpu.CompilerParams(vmem_limit_bytes=16 * 2**20),
         cost_estimate=pl.CostEstimate(flops=0, bytes_accessed=5 * 2**20, transcendentals=0),
         name="finish_weight",
     )(core, rows, *before)
@@ -433,23 +450,26 @@
     first = lax.all_to_all(packed_first, "grp", 0, 0, tiled=True).reshape(shape)
     packed_second = once(packed_second, first)
     second = lax.all_to_all(packed_second, "grp", 0, 0, tiled=True).reshape(shape)
-    results = attention(0, image_ids, me, first)
+    keep_first, send_first, out = attention(0, image_ids, me, first)
     up = [(i, (i + 2) % 8) for i in range(8)]
     down = [(i, (i + 6) % 8) for i in range(8)]
-    grads_late = [once(half, first) for half in grads_late]
+    grads_late = [once(half, send_first) for half in grads_late]
     grads_left = [lax.ppermute(half, "grp", up) for half in grads_late]
     grads_right = [lax.ppermute(half, "grp", down) for half in grads_late]
-    keep, send, out = attention(1, image_ids, me, second, *results)
+    keep, send, out = attention(1, image_ids, me, second, out)
+    side = [(i, i ^ 1) for i in range(8)]
+    other_first = lax.ppermute(send_first, "grp", side)
     grads_right[0] = once(grads_right[0], send)
     grads_left[1] = once(grads_left[1], send)
     grads_far = [lax.ppermute(grads_right[0], "grp", down), lax.ppermute(grads_left[1], "grp", up)]
     send = once(send, *grads_left, *grads_right)
-    other = lax.ppermute(send, "grp", [(i, i ^ 1) for i in range(8)])
+    send = once(send, other_first)
+    other = lax.ppermute(send, "grp", side)
     out = once(out, other, *grads_far)
     back = lax.all_to_all(out.reshape(8, 2, 3, PAIR, BLK), "grp", 0, 0, tiled=True)
     grads_line = (grads_own, *grads_right, *grads_far, *grads_left)
     column = scalar(lax.axis_index("dp"))
-    kept, sent = weight_terms(me, column, keep, other, grads_line)
+    kept, sent = weight_terms(me, column, (keep_first, keep, other_first, other), grads_line)
     cores = [(i, i ^ 1) for i in range(16)]
     sent = lax.ppermute(sent, "dp", cores)
     parts = [(kept[k].astype(f32) + sent[k].astype(f32)).astype(bf16) for k in range(4)]
@@ -461,7 +481,7 @@
         lax.ppermute(parts[k], both, [(i, i ^ (16 * (k // 2) + 2 * (k % 2))) for i in range(128)])
         for k in range(1, 4)
     ]
-    part = sum(item.astype(f32) for item in parts).astype(bf16)
+    part = (sum(item.astype(f32) for item in parts) * one_after(back)).astype(bf16)
     copies = jnp.broadcast_to(part[None], (64,) + part.shape)
     same_core = [[i * 2 + c for i in range(64)] for c in range(2)]
     own = lax.all_to_all(copies, both, 0, 0, axis_index_groups=same_core, tiled=True)

time: 157 us -> 155 us (0.987)
  local copies, waits for them, and re-layouts: 4.37 us -> 1.47 us
    ppermute x1 -> x2, waiting for transfers between devices: 2.46 us -> 5.71 us  [the longest x1 5.71 us: per_device(): other = lax.ppermute(send, 'grp', side)]
    unnamed x16 -> x0, local copies, waits for them, and re-layouts: 2.9 us -> none
    ppermute x1, starting transfers between devices: 0.97 us -> 2.67 us  [per_device(): lax.ppermute(grads_right[0], 'grp', down)]
    ppermute x1, starting transfers between devices: 1.71 us -> 0.01 us  [per_device(): lax.ppermute(grads_left[1], 'grp', up)]
    ppermute x1 -> x2, starting transfers between devices: 2.5 us -> 3.19 us  [the longest x1 2.83 us: per_device(): other_first = lax.ppermute(send_first, 'grp', side)]
  transfers between devices with their start and end apart: 19 -> 20, of which waited for: 13 -> 11; matrix products, arithmetic and copies ran while one was open for 1% -> 1% of each run, Pallas kernels for 24% -> 25%
where the time goes in v3:
time: 155 us; the launch traced here: 154 us
  waiting for transfers between devices  54.8 us (35%)
  starting transfers between devices  51.8 us (33%)
  Pallas kernels  43.3 us (28%)
  other arithmetic  1.92 us (1%)
    pallas_call x2, Pallas kernels, attention(): pl.pallas_call(attention_kernel, grid=(1,), in_specs=[smem, smem, whole(p...  23.3 us
    all_to_all x1, waiting for transfers between devices, per_device(): lax.all_to_all(copies, both, 0, 0, axis_index_groups=same_core, tiled=True)  21.4 us
    all_to_all x1, waiting for transfers between devices, per_device(): first = lax.all_to_all(packed_first, 'grp', 0, 0, tiled=True).reshape(shape)  15.6 us
    all_to_all x1, starting transfers between devices, per_device(): lax.all_to_all(copies, both, 0, 0, axis_index_groups=same_core, tiled=True)  7.64 us
    all_to_all x1, starting transfers between devices, per_device(): first = lax.all_to_all(packed_first, 'grp', 0, 0, tiled=True).reshape(shape)  7.47 us
    pallas_call x2, Pallas kernels, pack(): pl.pallas_call(pack_kernel, grid=(1,), in_specs=[pl.BlockSpec((width // 2...  7.46 us
    ppermute x1, waiting for transfers between devices, per_device(): other = lax.ppermute(send, 'grp', side)  5.71 us
    ppermute x3, waiting for transfers between devices, per_device(): lax.ppermute(parts[k], 'dp', [(i, i ^ 4 * k) for i in range(16)])  5.5 us
  transfers between devices with their start and end apart: 20, of which 11 were waited for; matrix products, arithmetic and copies ran while one was open for 1% of the time, Pallas kernels for 25%

profile of v3, /device:TPU:1, one launch (start us, length us, event | category | flops | bytes accessed | tf_op | source)
XLA Modules:
  0.0 154.1 jit_solution(7772224042870140231)
XLA Ops:
  0.6 3.7 %pack_heads.2 = (bf16[8,2,4,80,128]{4,3,2,1,0:T(8,128)(2,1)}, bf16[128,1280]{1,0:T(8,128)(2,1)}, bf16[128,1280]{1,0:T(8,128)(2,1)}) custom-call(bf16[1280,1280]{1,0:T(8,128)(2,1)} %weight_ref.3, bf16[256,1280]{1,0:T(8,128)(2,1)} %bitcast.56, bf16[256,1280]{1,0:T(8,128)(2,1)} %bitcast.59, bf16[256,1280]{1,0:T(8,128)(2,1)} %bitcast.61, bf16[256,1280]{1,0:T(8,128)(2,1)} %bitcast.63), custom_call_target="tpu_custom_call" | custom-call | flops 419430400 | bytes 5242880 | tf_op jit(solution)/shard_map/pack_heads/pallas_call | solution.py:96
  4.4 7.5 %all-to-all-start = ((bf16[8,2,4,80,128]{4,3,2,1,0:T(8,128)(2,1)}), bf16[8,2,4,80,128]{4,3,2,1,0:T(8,128)(2,1)}, u32[]{:S(2)}, u32[]{:S(2)}) async-start(bf16[8,2,4,80,128]{4,3,2,1,0:T(8,128)(2,1)} %get-tuple-element.19.refs_0_), calls=%async_computation | async-start | bytes 2621440 | tf_op jit(solution)/shard_map/all_to_all | solution.py:450
  11.8 3.7 %pack_heads.3 = (bf16[8,2,4,80,128]{4,3,2,1,0:T(8,128)(2,1)}, bf16[128,1280]{1,0:T(8,128)(2,1)}, bf16[128,1280]{1,0:T(8,128)(2,1)}) custom-call(bf16[1280,1280]{1,0:T(8,128)(2,1)} %weight_ref.3, bf16[256,1280]{1,0:T(8,128)(2,1)} %bitcast.57, bf16[256,1280]{1,0:T(8,128)(2,1)} %bitcast.60, bf16[256,1280]{1,0:T(8,128)(2,1)} %bitcast.62, ...), custom_call_target="tpu_custom_call" | custom-call | flops 419430400 | bytes 5242880 | tf_op jit(solution)/shard_map/pack_heads/pallas_call | solution.py:96
  15.6 15.6 %all-to-all-done = bf16[8,2,4,80,128]{4,3,2,1,0:T(8,128)(2,1)} async-done(((bf16[8,2,4,80,128]{4,3,2,1,0:T(8,128)(2,1)}), bf16[8,2,4,80,128]{4,3,2,1,0:T(8,128)(2,1)}, u32[]{:S(2)}, u32[]{:S(2)}) %all-to-all-start) | async-done | bytes 1310752 | tf_op jit(solution)/shard_map/all_to_all | solution.py:450
  31.1 4.3 %all-to-all-start.1 = ((bf16[8,2,4,80,128]{4,3,2,1,0:T(8,128)(2,1)}), bf16[8,2,4,80,128]{4,3,2,1,0:T(8,128)(2,1)}, u32[]{:S(2)}, u32[]{:S(2)}) async-start(bf16[8,2,4,80,128]{4,3,2,1,0:T(8,128)(2,1)} %once.9), calls=%async_computation.1 | async-start | bytes 2621440 | tf_op jit(solution)/shard_map/all_to_all | solution.py:452
  35.4 11.7 %attention_grads.2 = (bf16[80,1024]{1,0:T(8,128)(2,1)}, bf16[80,1024]{1,0:T(8,128)(2,1)}, bf16[16,3,160,128]{3,2,1,0:T(8,128)(2,1)}) custom-call(s32[1,16]{1,0:T(1,128)} %ids_ref.3, s32[1]{0:T(128)} %bitcast.me_ref, bf16[16,4,80,128]{3,2,1,0:T(8,128)(2,1)} %bitcast.5.refs_1_.in_ref), custom_call_target="tpu_custom_call" | custom-call | flops 12079595520 | bytes 4194304 | tf_op jit(solution)/shard_map/attention_grads/pallas_call | solution.py:202
  47.1 2.8 %collective-permute-start.4 = (bf16[80,1024]{1,0:T(8,128)(2,1)}, bf16[80,1024]{1,0:T(8,128)(2,1)}, u32[]{:S(2)}, u32[]{:S(2)}) collective-permute-start(bf16[80,1024]{1,0:T(8,128)(2,1)} %get-tuple-element.25.refs_1_), channel_id=1, source_target_pairs={{0,16},{16,0},{32,48},{48,32},{64,80},{80,64},{96,112},{112,96},{1... | collective-permute-start | bytes 491528 | tf_op jit(solution)/shard_map/ppermute | solution.py:461
  49.9 2.4 %collective-permute-start.2 = (bf16[128,1280]{1,0:T(8,128)(2,1)}, bf16[128,1280]{1,0:T(8,128)(2,1)}, u32[]{:S(2)}, u32[]{:S(2)}) collective-permute-start(bf16[128,1280]{1,0:T(8,128)(2,1)} %once.10), channel_id=1, source_target_pairs={{0,96},{16,112},{32,0},{48,16},{64,32},{80,48},{96,64},{112,80},{1... | collective-permute-start | bytes 983048 | tf_op jit(solution)/shard_map/ppermute | solution.py:458
  52.4 2.7 %collective-permute-start.3 = (bf16[128,1280]{1,0:T(8,128)(2,1)}, bf16[128,1280]{1,0:T(8,128)(2,1)}, u32[]{:S(2)}, u32[]{:S(2)}) collective-permute-start(bf16[128,1280]{1,0:T(8,128)(2,1)} %once.11), channel_id=1, source_target_pairs={{0,96},{16,112},{32,0},{48,16},{64,32},{80,48},{96,64},{112,80},{1... | collective-permute-start | bytes 983048 | tf_op jit(solution)/shard_map/ppermute | solution.py:458
  55.1 11.7 %attention_grads.3 = (bf16[80,1024]{1,0:T(8,128)(2,1)}, bf16[80,1024]{1,0:T(8,128)(2,1)}, bf16[16,3,160,128]{3,2,1,0:T(8,128)(2,1)}) custom-call(s32[1,16]{1,0:T(1,128)} %ids_ref.3, s32[1]{0:T(128)} %bitcast.me_ref, bf16[16,4,80,128]{3,2,1,0:T(8,128)(2,1)} %bitcast.6.in_ref, ...), custom_call_target="tpu_custom_call", output_to_operand_aliasing={{2}: (3, {})} | custom-call | flops 12079595520 | bytes 4194304 | tf_op jit(solution)/shard_map/attention_grads/pallas_call | solution.py:202
  66.7 2.7 %collective-permute-start.6 = (bf16[128,1280]{1,0:T(8,128)(2,1)}, bf16[128,1280]{1,0:T(8,128)(2,1)}, u32[]{:S(2)}, u32[]{:S(2)}) collective-permute-start(bf16[128,1280]{1,0:T(8,128)(2,1)} %once.13.refs_3_.refs_5_), channel_id=1, source_target_pairs={{0,96},{16,112},{32,0},{48,16},{64,32},{80,48},{96,64},{112,80},{1... | collective-permute-start | bytes 983048 | tf_op jit(solution)/shard_map/ppermute | solution.py:464
  69.8 5.7 %collective-permute-done.5.refs_1_.refs_3_ = bf16[80,1024]{1,0:T(8,128)(2,1)} collective-permute-done((bf16[80,1024]{1,0:T(8,128)(2,1)}, bf16[80,1024]{1,0:T(8,128)(2,1)}, u32[]{:S(2)}, u32[]{:S(2)}) %collective-permute-start.5) | collective-permute-done | bytes 163872 | tf_op jit(solution)/shard_map/ppermute | solution.py:467
  76.9 4.3 %all-to-all-start.2 = ((bf16[8,2,3,160,128]{4,3,2,1,0:T(8,128)(2,1)}), bf16[8,2,3,160,128]{4,3,2,1,0:T(8,128)(2,1)}, u32[]{:S(2)}, u32[]{:S(2)}) async-start(bf16[8,2,3,160,128]{4,3,2,1,0:T(8,128)(2,1)} %bitcast.55), calls=%async_computation.2 | async-start | bytes 3932160 | tf_op jit(solution)/shard_map/all_to_all | solution.py:469
  81.2 4.1 %weight_terms.1 = (bf16[4,4,112,128]{3,2,1,0:T(8,128)(2,1)}, bf16[4,4,112,128]{3,2,1,0:T(8,128)(2,1)}) custom-call(s32[1]{0:T(128)} %bitcast.me_ref, s32[1]{0:T(128)} %bitcast.12.column_ref, bf16[80,1024]{1,0:T(8,128)(2,1)} %get-tuple-element.30.refs_0_, bf16[80,1024]{1,0:T(8,128)(2,1)} %get-tuple-element.31.refs_1_, ...), custom_call_target="tpu_custom_call" | custom-call | flops 838860800 | bytes 6291456 | tf_op jit(solution)/shard_map/weight_terms/pallas_call | solution.py:296
  85.3 4.7 %collective-permute-start.8 = (bf16[4,4,112,128]{3,2,1,0:T(8,128)(2,1)}, bf16[4,4,112,128]{3,2,1,0:T(8,128)(2,1)S(1)}, u32[]{:S(2)}, u32[]{:S(2)}) collective-permute-start(bf16[4,4,112,128]{3,2,1,0:T(8,128)(2,1)} %get-tuple-element.33), channel_id=1, source_target_pairs={{0,1},{1,0},{2,3},{3,2},{4,5},{5,4},{6,7},{7,6},{8,9},{9,8},{10,11... | collective-permute-start | bytes 1376264 | tf_op jit(solution)/shard_map/ppermute | solution.py:474
  92.9 3.9 %collective-permute-start.11 = (bf16[4,112,128]{2,1,0:T(8,128)(2,1)S(1)}, bf16[4,112,128]{2,1,0:T(8,128)(2,1)S(1)}, u32[]{:S(2)}, u32[]{:S(2)}) collective-permute-start(bf16[4,112,128]{2,1,0:T(8,128)(2,1)S(1)} %get-tuple-element.35), channel_id=1, source_target_pairs={{0,12},{1,13},{2,14},{3,15},{4,8},{5,9},{6,10},{7,11},{8,4},{9,5},... | collective-permute-start | bytes 344072 | tf_op jit(solution)/shard_map/ppermute | solution.py:477
  97.5 4.1 %collective-permute-done.11 = bf16[4,112,128]{2,1,0:T(8,128)(2,1)S(1)} collective-permute-done((bf16[4,112,128]{2,1,0:T(8,128)(2,1)S(1)}, bf16[4,112,128]{2,1,0:T(8,128)(2,1)S(1)}, u32[]{:S(2)}, u32[]{:S(2)}) %collective-permute-start.11) | collective-permute-done | bytes 114720 | tf_op jit(solution)/shard_map/ppermute | solution.py:477
  103.5 3.0 %collective-permute-start.14 = (bf16[112,128]{1,0:T(8,128)(2,1)S(1)}, bf16[112,128]{1,0:T(8,128)(2,1)S(1)}, u32[]{:S(2)}, u32[]{:S(2)}) collective-permute-start(bf16[112,128]{1,0:T(8,128)(2,1)S(1)} %get-tuple-element.39), channel_id=1, source_target_pairs={{0,18},{1,19},{2,16},{3,17},{4,22},{5,23},{6,20},{7,21},{8,26},{9,... | collective-permute-start | bytes 86024 | tf_op jit(solution)/shard_map/ppermute | solution.py:481
  108.2 2.6 %collective-permute-done.13 = bf16[112,128]{1,0:T(8,128)(2,1)S(1)} collective-permute-done((bf16[112,128]{1,0:T(8,128)(2,1)S(1)}, bf16[112,128]{1,0:T(8,128)(2,1)S(1)}, u32[]{:S(2)}, u32[]{:S(2)}) %collective-permute-start.13) | collective-permute-done | bytes 28704 | tf_op jit(solution)/shard_map/ppermute | solution.py:481
  112.9 7.6 %all-to-all-start.3 = ((bf16[64,112,128]{2,1,0:T(8,128)(2,1)}), bf16[64,112,128]{2,1,0:T(8,128)(2,1)}, u32[]{:S(2)}, u32[]{:S(2)}) async-start(bf16[64,112,128]{2,1,0:T(8,128)(2,1)} %broadcast_in_dim.18), calls=%async_computation.3 | async-start | bytes 3670016 | tf_op jit(solution)/shard_map/all_to_all | solution.py:487
  120.6 3.0 %unpack_heads.1 = (bf16[256,1280]{1,0:T(8,128)(2,1)}, bf16[256,1280]{1,0:T(8,128)(2,1)}, bf16[256,1280]{1,0:T(8,128)(2,1)}) custom-call(bf16[8,2,3,160,128]{4,3,2,1,0:T(8,128)(2,1)} %all-to-all-done.2.in_ref.refs_0_), custom_call_target="tpu_custom_call" | custom-call | bytes 4194304 | tf_op jit(solution)/shard_map/unpack_heads/pallas_call | solution.py:240
  123.6 21.4 %all-to-all-done.3.refs_0_ = bf16[64,112,128]{2,1,0:T(8,128)(2,1)} async-done(((bf16[64,112,128]{2,1,0:T(8,128)(2,1)}), bf16[64,112,128]{2,1,0:T(8,128)(2,1)}, u32[]{:S(2)}, u32[]{:S(2)}) %all-to-all-start.3) | async-done | bytes 1835040 | tf_op jit(solution)/shard_map/all_to_all | solution.py:487
  145.0 3.6 %collective-permute-start.15 = (bf16[8,896,128]{2,1,0:T(8,128)(2,1)}, bf16[8,896,128]{2,1,0:T(8,128)(2,1)S(1)}, u32[]{:S(2)}, u32[]{:S(2)}) collective-permute-start(bf16[8,896,128]{2,1,0:T(8,128)(2,1)} %bitcast.25.in_ref), channel_id=1, source_target_pairs={{0,1},{1,0},{2,3},{3,2},{4,5},{5,4},{6,7},{7,6},{8,9},{9,8},{10,11... | collective-permute-start | bytes 5505032 | tf_op jit(solution)/shard_map/ppermute | solution.py:490
  148.6 3.0 %finish_weight.2.refs_0_ = f32[2,8,80,1280]{3,2,1,0:T(8,128)} custom-call(s32[1]{0:T(128)} %bitcast.26.core_ref, bf16[8,896,128]{2,1,0:T(8,128)(2,1)} %bitcast.25.in_ref), custom_call_target="tpu_custom_call" | custom-call | bytes 5242880 | tf_op jit(solution)/shard_map/finish_weight/pallas_call | solution.py:420
  (38 shorter events, 13.3 us)
Async XLA Ops:
  4.4 26.8 %all-to-all-start = ((bf16[8,2,4,80,128]{4,3,2,1,0:T(8,128)(2,1)}), bf16[8,2,4,80,128]{4,3,2,1,0:T(8,128)(2,1)}, u32[]{:S(2)}, u32[]{:S(2)}) async-start(bf16[8,2,4,80,128]{4,3,2,1,0:T(8,128)(2,1)} %get-tuple-element.19.refs_0_), calls=%async_computation | async-start | bytes 2621440 | tf_op jit(solution)/shard_map/all_to_all | solution.py:450
  31.1 23.9 %all-to-all-start.1 = ((bf16[8,2,4,80,128]{4,3,2,1,0:T(8,128)(2,1)}), bf16[8,2,4,80,128]{4,3,2,1,0:T(8,128)(2,1)}, u32[]{:S(2)}, u32[]{:S(2)}) async-start(bf16[8,2,4,80,128]{4,3,2,1,0:T(8,128)(2,1)} %once.9), calls=%async_computation.1 | async-start | bytes 2621440 | tf_op jit(solution)/shard_map/all_to_all | solution.py:452
  47.1 22.3 %collective-permute-start.4 = (bf16[80,1024]{1,0:T(8,128)(2,1)}, bf16[80,1024]{1,0:T(8,128)(2,1)}, u32[]{:S(2)}, u32[]{:S(2)}) collective-permute-start(bf16[80,1024]{1,0:T(8,128)(2,1)} %get-tuple-element.25.refs_1_), channel_id=1, source_target_pairs={{0,16},{16,0},{32,48},{48,32},{64,80},{80,64},{96,112},{112,96},{1... | collective-permute-start | bytes 491528 | tf_op jit(solution)/shard_map/ppermute | solution.py:461
  49.9 16.8 %collective-permute-start.2 = (bf16[128,1280]{1,0:T(8,128)(2,1)}, bf16[128,1280]{1,0:T(8,128)(2,1)}, u32[]{:S(2)}, u32[]{:S(2)}) collective-permute-start(bf16[128,1280]{1,0:T(8,128)(2,1)} %once.10), channel_id=1, source_target_pairs={{0,96},{16,112},{32,0},{48,16},{64,32},{80,48},{96,64},{112,80},{1... | collective-permute-start | bytes 983048 | tf_op jit(solution)/shard_map/ppermute | solution.py:458
  52.4 17.0 %collective-permute-start = (bf16[128,1280]{1,0:T(8,128)(2,1)}, bf16[128,1280]{1,0:T(8,128)(2,1)}, u32[]{:S(2)}, u32[]{:S(2)}) collective-permute-start(bf16[128,1280]{1,0:T(8,128)(2,1)} %once.10), channel_id=1, source_target_pairs={{0,32},{16,48},{32,64},{48,80},{64,96},{80,112},{96,0},{112,16},{1... | collective-permute-start | bytes 983048 | tf_op jit(solution)/shard_map/ppermute | solution.py:457
  52.4 17.0 %collective-permute-start.3 = (bf16[128,1280]{1,0:T(8,128)(2,1)}, bf16[128,1280]{1,0:T(8,128)(2,1)}, u32[]{:S(2)}, u32[]{:S(2)}) collective-permute-start(bf16[128,1280]{1,0:T(8,128)(2,1)} %once.11), channel_id=1, source_target_pairs={{0,96},{16,112},{32,0},{48,16},{64,32},{80,48},{96,64},{112,80},{1... | collective-permute-start | bytes 983048 | tf_op jit(solution)/shard_map/ppermute | solution.py:458
  55.0 14.4 %collective-permute-start.1 = (bf16[128,1280]{1,0:T(8,128)(2,1)}, bf16[128,1280]{1,0:T(8,128)(2,1)}, u32[]{:S(2)}, u32[]{:S(2)}) collective-permute-start(bf16[128,1280]{1,0:T(8,128)(2,1)} %once.11), channel_id=1, source_target_pairs={{0,32},{16,48},{32,64},{48,80},{64,96},{80,112},{96,0},{112,16},{1... | collective-permute-start | bytes 983048 | tf_op jit(solution)/shard_map/ppermute | solution.py:457
  66.7 8.8 %collective-permute-start.6 = (bf16[128,1280]{1,0:T(8,128)(2,1)}, bf16[128,1280]{1,0:T(8,128)(2,1)}, u32[]{:S(2)}, u32[]{:S(2)}) collective-permute-start(bf16[128,1280]{1,0:T(8,128)(2,1)} %once.13.refs_3_.refs_5_), channel_id=1, source_target_pairs={{0,96},{16,112},{32,0},{48,16},{64,32},{80,48},{96,64},{112,80},{1... | collective-permute-start | bytes 983048 | tf_op jit(solution)/shard_map/ppermute | solution.py:464
  69.4 7.5 %collective-permute-start.7 = (bf16[128,1280]{1,0:T(8,128)(2,1)}, bf16[128,1280]{1,0:T(8,128)(2,1)}, u32[]{:S(2)}, u32[]{:S(2)}) collective-permute-start(bf16[128,1280]{1,0:T(8,128)(2,1)} %once.12.refs_2_.refs_10_), channel_id=1, source_target_pairs={{0,32},{16,48},{32,64},{48,80},{64,96},{80,112},{96,0},{112,16},{1... | collective-permute-start | bytes 983048 | tf_op jit(solution)/shard_map/ppermute | solution.py:464
  69.5 6.1 %collective-permute-start.5 = (bf16[80,1024]{1,0:T(8,128)(2,1)}, bf16[80,1024]{1,0:T(8,128)(2,1)}, u32[]{:S(2)}, u32[]{:S(2)}) collective-permute-start(bf16[80,1024]{1,0:T(8,128)(2,1)} %once.15), channel_id=1, source_target_pairs={{0,16},{16,0},{32,48},{48,32},{64,80},{80,64},{96,112},{112,96},{1... | collective-permute-start | bytes 491528 | tf_op jit(solution)/shard_map/ppermute | solution.py:467
  76.9 30.4 %all-to-all-start.2 = ((bf16[8,2,3,160,128]{4,3,2,1,0:T(8,128)(2,1)}), bf16[8,2,3,160,128]{4,3,2,1,0:T(8,128)(2,1)}, u32[]{:S(2)}, u32[]{:S(2)}) async-start(bf16[8,2,3,160,128]{4,3,2,1,0:T(8,128)(2,1)} %bitcast.55), calls=%async_computation.2 | async-start | bytes 3932160 | tf_op jit(solution)/shard_map/all_to_all | solution.py:469
  85.3 6.4 %collective-permute-start.8 = (bf16[4,4,112,128]{3,2,1,0:T(8,128)(2,1)}, bf16[4,4,112,128]{3,2,1,0:T(8,128)(2,1)S(1)}, u32[]{:S(2)}, u32[]{:S(2)}) collective-permute-start(bf16[4,4,112,128]{3,2,1,0:T(8,128)(2,1)} %get-tuple-element.33), channel_id=1, source_target_pairs={{0,1},{1,0},{2,3},{3,2},{4,5},{5,4},{6,7},{7,6},{8,9},{9,8},{10,11... | collective-permute-start | bytes 1376264 | tf_op jit(solution)/shard_map/ppermute | solution.py:474
  92.9 8.7 %collective-permute-start.11 = (bf16[4,112,128]{2,1,0:T(8,128)(2,1)S(1)}, bf16[4,112,128]{2,1,0:T(8,128)(2,1)S(1)}, u32[]{:S(2)}, u32[]{:S(2)}) collective-permute-start(bf16[4,112,128]{2,1,0:T(8,128)(2,1)S(1)} %get-tuple-element.35), channel_id=1, source_target_pairs={{0,12},{1,13},{2,14},{3,15},{4,8},{5,9},{6,10},{7,11},{8,4},{9,5},... | collective-permute-start | bytes 344072 | tf_op jit(solution)/shard_map/ppermute | solution.py:477
  96.8 5.6 %collective-permute-start.10 = (bf16[4,112,128]{2,1,0:T(8,128)(2,1)S(1)}, bf16[4,112,128]{2,1,0:T(8,128)(2,1)S(1)}, u32[]{:S(2)}, u32[]{:S(2)}) collective-permute-start(bf16[4,112,128]{2,1,0:T(8,128)(2,1)S(1)} %get-tuple-element.36), channel_id=1, source_target_pairs={{0,8},{1,9},{2,10},{3,11},{4,12},{5,13},{6,14},{7,15},{8,0},{9,1},... | collective-permute-start | bytes 344072 | tf_op jit(solution)/shard_map/ppermute | solution.py:477
  96.8 6.2 %collective-permute-start.9 = (bf16[4,112,128]{2,1,0:T(8,128)(2,1)S(1)}, bf16[4,112,128]{2,1,0:T(8,128)(2,1)S(1)}, u32[]{:S(2)}, u32[]{:S(2)}) collective-permute-start(bf16[4,112,128]{2,1,0:T(8,128)(2,1)S(1)} %get-tuple-element.37), channel_id=1, source_target_pairs={{0,4},{1,5},{2,6},{3,7},{4,0},{5,1},{6,2},{7,3},{8,12},{9,13},{10,... | collective-permute-start | bytes 344072 | tf_op jit(solution)/shard_map/ppermute | solution.py:477
  103.0 4.7 %collective-permute-start.12 = (bf16[112,128]{1,0:T(8,128)(2,1)S(1)}, bf16[112,128]{1,0:T(8,128)(2,1)S(1)}, u32[]{:S(2)}, u32[]{:S(2)}) collective-permute-start(bf16[112,128]{1,0:T(8,128)(2,1)S(1)} %get-tuple-element.38), channel_id=1, source_target_pairs={{0,2},{1,3},{2,0},{3,1},{4,6},{5,7},{6,4},{7,5},{8,10},{9,11},{10,... | collective-permute-start | bytes 86024 | tf_op jit(solution)/shard_map/ppermute | solution.py:481
  103.5 4.7 %collective-permute-start.14 = (bf16[112,128]{1,0:T(8,128)(2,1)S(1)}, bf16[112,128]{1,0:T(8,128)(2,1)S(1)}, u32[]{:S(2)}, u32[]{:S(2)}) collective-permute-start(bf16[112,128]{1,0:T(8,128)(2,1)S(1)} %get-tuple-element.39), channel_id=1, source_target_pairs={{0,18},{1,19},{2,16},{3,17},{4,22},{5,23},{6,20},{7,21},{8,26},{9,... | collective-permute-start | bytes 86024 | tf_op jit(solution)/shard_map/ppermute | solution.py:481
  106.5 4.3 %collective-permute-start.13 = (bf16[112,128]{1,0:T(8,128)(2,1)S(1)}, bf16[112,128]{1,0:T(8,128)(2,1)S(1)}, u32[]{:S(2)}, u32[]{:S(2)}) collective-permute-start(bf16[112,128]{1,0:T(8,128)(2,1)S(1)} %get-tuple-element.40), channel_id=1, source_target_pairs={{0,16},{1,17},{2,18},{3,19},{4,20},{5,21},{6,22},{7,23},{8,24},{9,... | collective-permute-start | bytes 86024 | tf_op jit(solution)/shard_map/ppermute | solution.py:481
  112.9 32.1 %all-to-all-start.3 = ((bf16[64,112,128]{2,1,0:T(8,128)(2,1)}), bf16[64,112,128]{2,1,0:T(8,128)(2,1)}, u32[]{:S(2)}, u32[]{:S(2)}) async-start(bf16[64,112,128]{2,1,0:T(8,128)(2,1)} %broadcast_in_dim.18), calls=%async_computation.3 | async-start | bytes 3670016 | tf_op jit(solution)/shard_map/all_to_all | solution.py:487
  145.0 7.2 %collective-permute-start.15 = (bf16[8,896,128]{2,1,0:T(8,128)(2,1)}, bf16[8,896,128]{2,1,0:T(8,128)(2,1)S(1)}, u32[]{:S(2)}, u32[]{:S(2)}) collective-permute-start(bf16[8,896,128]{2,1,0:T(8,128)(2,1)} %bitcast.25.in_ref), channel_id=1, source_target_pairs={{0,1},{1,0},{2,3},{3,2},{4,5},{5,4},{6,7},{7,6},{8,9},{9,8},{10,11... | collective-permute-start | bytes 5505032 | tf_op jit(solution)/shard_map/ppermute | solution.py:490

commit v4 on v3

--- a/solution.py
+++ b/solution.py
@@ -1,3 +1,4 @@
+import functools
 import math
 
 import jax
@@ -58,17 +59,12 @@
     return jnp.where(other < start, other, slot)
 
 
-def slot_of(start, block):
-    other = jnp.where(block < start, BIG + block, block)
-    return jnp.where((block >= start) & (block < start + BIG), block - start, other)
-
-
 def columns_of(slot):
     return slice(slot * BLK, (slot + 1) * BLK)
 
 
-def pack_kernel(weight_ref, grads_ref, query_ref, key_ref, value_ref, *refs):
-    out_ref, *half_refs = refs[-3:]
+def pack_kernel(copies, weight_ref, grads_ref, query_ref, key_ref, value_ref, *refs):
+    out_ref, *half_refs = refs[-1 - copies :]
     arrays = [
         query_ref[...].T,
         key_ref[...].T,
@@ -85,16 +81,13 @@
         half_ref[...] = grads_ref[columns_of(i), :]
 
 
-def pack(half, weight, grads, query, key, value, *after):
+def pack(half, copies, weight, grads, query, key, value, *after):
     rows, width = query.shape
     column = pl.BlockSpec((rows, width // 2), lambda i: (0, half))
-    shapes = [
-        jax.ShapeDtypeStruct((8, 2, 4, DH, BLK), bf16),
-        jax.ShapeDtypeStruct((BLK, grads.shape[1]), bf16),
-        jax.ShapeDtypeStruct((BLK, grads.shape[1]), bf16),
-    ]
-    return pl.pallas_call(
-        pack_kernel,
+    shapes = [jax.ShapeDtypeStruct((8, 2, 4, DH, BLK), bf16)]
+    shapes += [jax.ShapeDtypeStruct((BLK, grads.shape[1]), bf16)] * copies
+    return pl.pallas_call(
+        functools.partial(pack_kernel, copies),
         grid=(1,),
         in_specs=[
             pl.BlockSpec((width // 2, width), lambda i: (half, 0)),
@@ -311,68 +304,6 @@
     )(me, column, *atts, *grads)
 
 
-def add_kernel(*refs):
-    count = len(refs) - 4
-    for i in range(4):
-        total = refs[0][i].astype(f32)
-        for ref in refs[1:count]:
-            total = total + ref[i].astype(f32)
-        refs[count + i][...] = total.astype(bf16)
-
-
-def add_up(*arrays):
-    shape = arrays[0].shape[1:]
-    return pl.pallas_call(
-        add_kernel,
-        out_shape=[jax.ShapeDtypeStruct(shape, bf16)] * 4,
-        compiler_params=pltpu.CompilerParams(vmem_limit_bytes=65408 * 2**10),
-        cost_estimate=pl.CostEstimate(
-            flops=len(arrays) * arrays[0].size, bytes_accessed=2**20, transcendentals=0
-        ),
-        name="add_up",
-    )(*arrays)
-
-
-def nothing_kernel(*refs):
-    pass
-
-
-def once(array, *after):
-    anywhere = pl.BlockSpec(memory_space=pltpu.HBM)
-    return pl.pallas_call(
-        nothing_kernel,
-        in_specs=[anywhere] * (1 + len(after)),
-        out_specs=anywhere,
-        out_shape=jax.ShapeDtypeStruct(array.shape, array.dtype),
-        input_output_aliases={0: 0},
-        compiler_params=pltpu.CompilerParams(vmem_limit_bytes=65408 * 2**10),
-        cost_estimate=pl.CostEstimate(flops=0, bytes_accessed=0, transcendentals=0),
-        name="once",
-    )(array, *after)
-
-
-def add_kernel(*refs):
-    count = len(refs) - 4
-    for i in range(4):
-        total = refs[0][i].astype(f32)
-        for ref in refs[1:count]:
-            total = total + ref[i].astype(f32)
-        refs[count + i][...] = total.astype(bf16)
-
-
-def add_up(*arrays):
-    shape = arrays[0].shape[1:]
-    return pl.pallas_call(
-        add_kernel,
-        out_shape=[jax.ShapeDtypeStruct(shape, bf16)] * 4,
-        compiler_params=pltpu.CompilerParams(vmem_limit_bytes=65408 * 2**10),
-        cost_estimate=pl.CostEstimate(
-            flops=len(arrays) * arrays[0].size, bytes_accessed=2**20, transcendentals=0
-        ),
-        name="add_up",
-    )(*arrays)
-
-
 def nothing_kernel(*refs):
     pass
 
@@ -444,8 +375,8 @@
     me = scalar(lax.axis_index("grp"))
     core = lax.axis_index("dp") % 2
     operands = (out_weight, grads_own, queries[0], keys_in[0], value_rows[0])
-    packed_first, _, _ = pack(0, *operands)
-    packed_second, *grads_late = pack(1, *operands, packed_first)
+    (packed_first,) = pack(0, 0, *operands)
+    packed_second, *grads_late = pack(1, 2, *operands, packed_first)
     shape = (GBLOCKS, 4, DH, BLK)
     first = lax.all_to_all(packed_first, "grp", 0, 0, tiled=True).reshape(shape)
     packed_second = once(packed_second, first)

time: 155 us -> 154 us (level)
  no operation moved by 1% of the time
where the time goes in v4:
time: 154 us
  waiting for transfers between devices  54.9 us (36%)
  starting transfers between devices  51.8 us (34%)
  Pallas kernels  43.1 us (28%)
  other arithmetic  1.92 us (1%)
    pallas_call x2, Pallas kernels, attention(): pl.pallas_call(attention_kernel, grid=(1,), in_specs=[smem, smem, whole(p...  23.3 us
    all_to_all x1, waiting for transfers between devices, per_device(): lax.all_to_all(copies, both, 0, 0, axis_index_groups=same_core, tiled=True)  21.4 us
    all_to_all x1, waiting for transfers between devices, per_device(): first = lax.all_to_all(packed_first, 'grp', 0, 0, tiled=True).reshape(shape)  15.6 us
    all_to_all x1, starting transfers between devices, per_device(): lax.all_to_all(copies, both, 0, 0, axis_index_groups=same_core, tiled=True)  7.63 us
    all_to_all x1, starting transfers between devices, per_device(): first = lax.all_to_all(packed_first, 'grp', 0, 0, tiled=True).reshape(shape)  7.47 us
    pallas_call x2, Pallas kernels, pack(): pl.pallas_call(functools.partial(pack_kernel, copies), grid=(1,), in_spec...  7.3 us
    ppermute x1, waiting for transfers between devices, per_device(): other = lax.ppermute(send, 'grp', side)  5.71 us
    ppermute x3, waiting for transfers between devices, per_device(): lax.ppermute(parts[k], 'dp', [(i, i ^ 4 * k) for i in range(16)])  5.5 us
  transfers between devices with their start and end apart: 20, of which 11 were waited for; matrix products, arithmetic and copies ran while one was open for 1% of the time, Pallas kernels for 25%

profile of v4, /device:TPU:1, one launch (start us, length us, event | category | flops | bytes accessed | tf_op | source)
XLA Modules:
  0.0 153.9 jit_solution(4215119259671950871)
XLA Ops:
  0.6 3.6 %pack_heads.2.refs_0_ = bf16[8,2,4,80,128]{4,3,2,1,0:T(8,128)(2,1)} custom-call(bf16[1280,1280]{1,0:T(8,128)(2,1)} %weight_ref.3, bf16[256,1280]{1,0:T(8,128)(2,1)} %bitcast.56, bf16[256,1280]{1,0:T(8,128)(2,1)} %bitcast.59, bf16[256,1280]{1,0:T(8,128)(2,1)} %bitcast.61, bf16[256,1280]{1,0:T(8,128)(2,1)} %bitcast.63), custom_call_target="tpu_custom_call" | custom-call | flops 419430400 | bytes 5242880 | tf_op jit(solution)/shard_map/pack_heads/pallas_call | solution.py:89
  4.2 7.5 %all-to-all-start = ((bf16[8,2,4,80,128]{4,3,2,1,0:T(8,128)(2,1)}), bf16[8,2,4,80,128]{4,3,2,1,0:T(8,128)(2,1)}, u32[]{:S(2)}, u32[]{:S(2)}) async-start(bf16[8,2,4,80,128]{4,3,2,1,0:T(8,128)(2,1)} %pack_heads.2.refs_0_), calls=%async_computation | async-start | bytes 2621440 | tf_op jit(solution)/shard_map/all_to_all | solution.py:381
  11.7 3.7 %pack_heads.3 = (bf16[8,2,4,80,128]{4,3,2,1,0:T(8,128)(2,1)}, bf16[128,1280]{1,0:T(8,128)(2,1)}, bf16[128,1280]{1,0:T(8,128)(2,1)}) custom-call(bf16[1280,1280]{1,0:T(8,128)(2,1)} %weight_ref.3, bf16[256,1280]{1,0:T(8,128)(2,1)} %bitcast.57, bf16[256,1280]{1,0:T(8,128)(2,1)} %bitcast.60, bf16[256,1280]{1,0:T(8,128)(2,1)} %bitcast.62, ...), custom_call_target="tpu_custom_call" | custom-call | flops 419430400 | bytes 5242880 | tf_op jit(solution)/shard_map/pack_heads/pallas_call | solution.py:89
  15.4 15.6 %all-to-all-done = bf16[8,2,4,80,128]{4,3,2,1,0:T(8,128)(2,1)} async-done(((bf16[8,2,4,80,128]{4,3,2,1,0:T(8,128)(2,1)}), bf16[8,2,4,80,128]{4,3,2,1,0:T(8,128)(2,1)}, u32[]{:S(2)}, u32[]{:S(2)}) %all-to-all-start) | async-done | bytes 1310752 | tf_op jit(solution)/shard_map/all_to_all | solution.py:381
  31.0 4.3 %all-to-all-start.1 = ((bf16[8,2,4,80,128]{4,3,2,1,0:T(8,128)(2,1)}), bf16[8,2,4,80,128]{4,3,2,1,0:T(8,128)(2,1)}, u32[]{:S(2)}, u32[]{:S(2)}) async-start(bf16[8,2,4,80,128]{4,3,2,1,0:T(8,128)(2,1)} %once.9), calls=%async_computation.1 | async-start | bytes 2621440 | tf_op jit(solution)/shard_map/all_to_all | solution.py:383
  35.3 11.7 %attention_grads.2 = (bf16[80,1024]{1,0:T(8,128)(2,1)}, bf16[80,1024]{1,0:T(8,128)(2,1)}, bf16[16,3,160,128]{3,2,1,0:T(8,128)(2,1)}) custom-call(s32[1,16]{1,0:T(1,128)} %ids_ref.3, s32[1]{0:T(128)} %bitcast.me_ref, bf16[16,4,80,128]{3,2,1,0:T(8,128)(2,1)} %bitcast.5.refs_1_.in_ref), custom_call_target="tpu_custom_call" | custom-call | flops 12079595520 | bytes 4194304 | tf_op jit(solution)/shard_map/attention_grads/pallas_call | solution.py:195
  46.9 2.8 %collective-permute-start.4 = (bf16[80,1024]{1,0:T(8,128)(2,1)}, bf16[80,1024]{1,0:T(8,128)(2,1)}, u32[]{:S(2)}, u32[]{:S(2)}) collective-permute-start(bf16[80,1024]{1,0:T(8,128)(2,1)} %get-tuple-element.23.refs_1_), channel_id=1, source_target_pairs={{0,16},{16,0},{32,48},{48,32},{64,80},{80,64},{96,112},{112,96},{1... | collective-permute-start | bytes 491528 | tf_op jit(solution)/shard_map/ppermute | solution.py:392
  49.8 2.4 %collective-permute-start.2 = (bf16[128,1280]{1,0:T(8,128)(2,1)}, bf16[128,1280]{1,0:T(8,128)(2,1)}, u32[]{:S(2)}, u32[]{:S(2)}) collective-permute-start(bf16[128,1280]{1,0:T(8,128)(2,1)} %once.10), channel_id=1, source_target_pairs={{0,96},{16,112},{32,0},{48,16},{64,32},{80,48},{96,64},{112,80},{1... | collective-permute-start | bytes 983048 | tf_op jit(solution)/shard_map/ppermute | solution.py:389
  52.2 2.7 %collective-permute-start.3 = (bf16[128,1280]{1,0:T(8,128)(2,1)}, bf16[128,1280]{1,0:T(8,128)(2,1)}, u32[]{:S(2)}, u32[]{:S(2)}) collective-permute-start(bf16[128,1280]{1,0:T(8,128)(2,1)} %once.11), channel_id=1, source_target_pairs={{0,96},{16,112},{32,0},{48,16},{64,32},{80,48},{96,64},{112,80},{1... | collective-permute-start | bytes 983048 | tf_op jit(solution)/shard_map/ppermute | solution.py:389
  54.9 11.7 %attention_grads.3 = (bf16[80,1024]{1,0:T(8,128)(2,1)}, bf16[80,1024]{1,0:T(8,128)(2,1)}, bf16[16,3,160,128]{3,2,1,0:T(8,128)(2,1)}) custom-call(s32[1,16]{1,0:T(1,128)} %ids_ref.3, s32[1]{0:T(128)} %bitcast.me_ref, bf16[16,4,80,128]{3,2,1,0:T(8,128)(2,1)} %bitcast.6.in_ref, ...), custom_call_target="tpu_custom_call", output_to_operand_aliasing={{2}: (3, {})} | custom-call | flops 12079595520 | bytes 4194304 | tf_op jit(solution)/shard_map/attention_grads/pallas_call | solution.py:195
  66.6 2.7 %collective-permute-start.6 = (bf16[128,1280]{1,0:T(8,128)(2,1)}, bf16[128,1280]{1,0:T(8,128)(2,1)}, u32[]{:S(2)}, u32[]{:S(2)}) collective-permute-start(bf16[128,1280]{1,0:T(8,128)(2,1)} %once.13.refs_3_.refs_5_), channel_id=1, source_target_pairs={{0,96},{16,112},{32,0},{48,16},{64,32},{80,48},{96,64},{112,80},{1... | collective-permute-start | bytes 983048 | tf_op jit(solution)/shard_map/ppermute | solution.py:395
  69.7 5.7 %collective-permute-done.5.refs_1_.refs_3_ = bf16[80,1024]{1,0:T(8,128)(2,1)} collective-permute-done((bf16[80,1024]{1,0:T(8,128)(2,1)}, bf16[80,1024]{1,0:T(8,128)(2,1)}, u32[]{:S(2)}, u32[]{:S(2)}) %collective-permute-start.5) | collective-permute-done | bytes 163872 | tf_op jit(solution)/shard_map/ppermute | solution.py:398
  76.7 4.3 %all-to-all-start.2 = ((bf16[8,2,3,160,128]{4,3,2,1,0:T(8,128)(2,1)}), bf16[8,2,3,160,128]{4,3,2,1,0:T(8,128)(2,1)}, u32[]{:S(2)}, u32[]{:S(2)}) async-start(bf16[8,2,3,160,128]{4,3,2,1,0:T(8,128)(2,1)} %bitcast.55), calls=%async_computation.2 | async-start | bytes 3932160 | tf_op jit(solution)/shard_map/all_to_all | solution.py:400
  81.1 4.1 %weight_terms.1 = (bf16[4,4,112,128]{3,2,1,0:T(8,128)(2,1)}, bf16[4,4,112,128]{3,2,1,0:T(8,128)(2,1)}) custom-call(s32[1]{0:T(128)} %bitcast.me_ref, s32[1]{0:T(128)} %bitcast.12.column_ref, bf16[80,1024]{1,0:T(8,128)(2,1)} %get-tuple-element.28.refs_0_, bf16[80,1024]{1,0:T(8,128)(2,1)} %get-tuple-element.29.refs_1_, ...), custom_call_target="tpu_custom_call" | custom-call | flops 838860800 | bytes 6291456 | tf_op jit(solution)/shard_map/weight_terms/pallas_call | solution.py:289
  85.2 4.7 %collective-permute-start.8 = (bf16[4,4,112,128]{3,2,1,0:T(8,128)(2,1)}, bf16[4,4,112,128]{3,2,1,0:T(8,128)(2,1)S(1)}, u32[]{:S(2)}, u32[]{:S(2)}) collective-permute-start(bf16[4,4,112,128]{3,2,1,0:T(8,128)(2,1)} %get-tuple-element.31), channel_id=1, source_target_pairs={{0,1},{1,0},{2,3},{3,2},{4,5},{5,4},{6,7},{7,6},{8,9},{9,8},{10,11... | collective-permute-start | bytes 1376264 | tf_op jit(solution)/shard_map/ppermute | solution.py:405
  92.8 3.9 %collective-permute-start.11 = (bf16[4,112,128]{2,1,0:T(8,128)(2,1)S(1)}, bf16[4,112,128]{2,1,0:T(8,128)(2,1)S(1)}, u32[]{:S(2)}, u32[]{:S(2)}) collective-permute-start(bf16[4,112,128]{2,1,0:T(8,128)(2,1)S(1)} %get-tuple-element.33), channel_id=1, source_target_pairs={{0,12},{1,13},{2,14},{3,15},{4,8},{5,9},{6,10},{7,11},{8,4},{9,5},... | collective-permute-start | bytes 344072 | tf_op jit(solution)/shard_map/ppermute | solution.py:408
  97.3 4.1 %collective-permute-done.11 = bf16[4,112,128]{2,1,0:T(8,128)(2,1)S(1)} collective-permute-done((bf16[4,112,128]{2,1,0:T(8,128)(2,1)S(1)}, bf16[4,112,128]{2,1,0:T(8,128)(2,1)S(1)}, u32[]{:S(2)}, u32[]{:S(2)}) %collective-permute-start.11) | collective-permute-done | bytes 114720 | tf_op jit(solution)/shard_map/ppermute | solution.py:408
  103.3 3.0 %collective-permute-start.14 = (bf16[112,128]{1,0:T(8,128)(2,1)S(1)}, bf16[112,128]{1,0:T(8,128)(2,1)S(1)}, u32[]{:S(2)}, u32[]{:S(2)}) collective-permute-start(bf16[112,128]{1,0:T(8,128)(2,1)S(1)} %get-tuple-element.37), channel_id=1, source_target_pairs={{0,18},{1,19},{2,16},{3,17},{4,22},{5,23},{6,20},{7,21},{8,26},{9,... | collective-permute-start | bytes 86024 | tf_op jit(solution)/shard_map/ppermute | solution.py:412
  108.0 2.6 %collective-permute-done.13 = bf16[112,128]{1,0:T(8,128)(2,1)S(1)} collective-permute-done((bf16[112,128]{1,0:T(8,128)(2,1)S(1)}, bf16[112,128]{1,0:T(8,128)(2,1)S(1)}, u32[]{:S(2)}, u32[]{:S(2)}) %collective-permute-start.13) | collective-permute-done | bytes 28704 | tf_op jit(solution)/shard_map/ppermute | solution.py:412
  112.8 7.6 %all-to-all-start.3 = ((bf16[64,112,128]{2,1,0:T(8,128)(2,1)}), bf16[64,112,128]{2,1,0:T(8,128)(2,1)}, u32[]{:S(2)}, u32[]{:S(2)}) async-start(bf16[64,112,128]{2,1,0:T(8,128)(2,1)} %broadcast_in_dim.18), calls=%async_computation.3 | async-start | bytes 3670016 | tf_op jit(solution)/shard_map/all_to_all | solution.py:418
  120.4 3.0 %unpack_heads.1 = (bf16[256,1280]{1,0:T(8,128)(2,1)}, bf16[256,1280]{1,0:T(8,128)(2,1)}, bf16[256,1280]{1,0:T(8,128)(2,1)}) custom-call(bf16[8,2,3,160,128]{4,3,2,1,0:T(8,128)(2,1)} %all-to-all-done.2.in_ref.refs_0_), custom_call_target="tpu_custom_call" | custom-call | bytes 4194304 | tf_op jit(solution)/shard_map/unpack_heads/pallas_call | solution.py:233
  123.5 21.4 %all-to-all-done.3.refs_0_ = bf16[64,112,128]{2,1,0:T(8,128)(2,1)} async-done(((bf16[64,112,128]{2,1,0:T(8,128)(2,1)}), bf16[64,112,128]{2,1,0:T(8,128)(2,1)}, u32[]{:S(2)}, u32[]{:S(2)}) %all-to-all-start.3) | async-done | bytes 1835040 | tf_op jit(solution)/shard_map/all_to_all | solution.py:418
  144.8 3.6 %collective-permute-start.15 = (bf16[8,896,128]{2,1,0:T(8,128)(2,1)}, bf16[8,896,128]{2,1,0:T(8,128)(2,1)S(1)}, u32[]{:S(2)}, u32[]{:S(2)}) collective-permute-start(bf16[8,896,128]{2,1,0:T(8,128)(2,1)} %bitcast.25.in_ref), channel_id=1, source_target_pairs={{0,1},{1,0},{2,3},{3,2},{4,5},{5,4},{6,7},{7,6},{8,9},{9,8},{10,11... | collective-permute-start | bytes 5505032 | tf_op jit(solution)/shard_map/ppermute | solution.py:421
  148.4 3.0 %finish_weight.2.refs_0_ = f32[2,8,80,1280]{3,2,1,0:T(8,128)} custom-call(s32[1]{0:T(128)} %bitcast.26.core_ref, bf16[8,896,128]{2,1,0:T(8,128)(2,1)} %bitcast.25.in_ref), custom_call_target="tpu_custom_call" | custom-call | bytes 5242880 | tf_op jit(solution)/shard_map/finish_weight/pallas_call | solution.py:351
  (38 shorter events, 13.3 us)
Async XLA Ops:
  4.2 26.8 %all-to-all-start = ((bf16[8,2,4,80,128]{4,3,2,1,0:T(8,128)(2,1)}), bf16[8,2,4,80,128]{4,3,2,1,0:T(8,128)(2,1)}, u32[]{:S(2)}, u32[]{:S(2)}) async-start(bf16[8,2,4,80,128]{4,3,2,1,0:T(8,128)(2,1)} %pack_heads.2.refs_0_), calls=%async_computation | async-start | bytes 2621440 | tf_op jit(solution)/shard_map/all_to_all | solution.py:381
  31.0 23.9 %all-to-all-start.1 = ((bf16[8,2,4,80,128]{4,3,2,1,0:T(8,128)(2,1)}), bf16[8,2,4,80,128]{4,3,2,1,0:T(8,128)(2,1)}, u32[]{:S(2)}, u32[]{:S(2)}) async-start(bf16[8,2,4,80,128]{4,3,2,1,0:T(8,128)(2,1)} %once.9), calls=%async_computation.1 | async-start | bytes 2621440 | tf_op jit(solution)/shard_map/all_to_all | solution.py:383
  46.9 22.3 %collective-permute-start.4 = (bf16[80,1024]{1,0:T(8,128)(2,1)}, bf16[80,1024]{1,0:T(8,128)(2,1)}, u32[]{:S(2)}, u32[]{:S(2)}) collective-permute-start(bf16[80,1024]{1,0:T(8,128)(2,1)} %get-tuple-element.23.refs_1_), channel_id=1, source_target_pairs={{0,16},{16,0},{32,48},{48,32},{64,80},{80,64},{96,112},{112,96},{1... | collective-permute-start | bytes 491528 | tf_op jit(solution)/shard_map/ppermute | solution.py:392
  49.8 16.8 %collective-permute-start.2 = (bf16[128,1280]{1,0:T(8,128)(2,1)}, bf16[128,1280]{1,0:T(8,128)(2,1)}, u32[]{:S(2)}, u32[]{:S(2)}) collective-permute-start(bf16[128,1280]{1,0:T(8,128)(2,1)} %once.10), channel_id=1, source_target_pairs={{0,96},{16,112},{32,0},{48,16},{64,32},{80,48},{96,64},{112,80},{1... | collective-permute-start | bytes 983048 | tf_op jit(solution)/shard_map/ppermute | solution.py:389
  52.2 17.0 %collective-permute-start = (bf16[128,1280]{1,0:T(8,128)(2,1)}, bf16[128,1280]{1,0:T(8,128)(2,1)}, u32[]{:S(2)}, u32[]{:S(2)}) collective-permute-start(bf16[128,1280]{1,0:T(8,128)(2,1)} %once.10), channel_id=1, source_target_pairs={{0,32},{16,48},{32,64},{48,80},{64,96},{80,112},{96,0},{112,16},{1... | collective-permute-start | bytes 983048 | tf_op jit(solution)/shard_map/ppermute | solution.py:388
  52.2 17.0 %collective-permute-start.3 = (bf16[128,1280]{1,0:T(8,128)(2,1)}, bf16[128,1280]{1,0:T(8,128)(2,1)}, u32[]{:S(2)}, u32[]{:S(2)}) collective-permute-start(bf16[128,1280]{1,0:T(8,128)(2,1)} %once.11), channel_id=1, source_target_pairs={{0,96},{16,112},{32,0},{48,16},{64,32},{80,48},{96,64},{112,80},{1... | collective-permute-start | bytes 983048 | tf_op jit(solution)/shard_map/ppermute | solution.py:389
  54.9 14.4 %collective-permute-start.1 = (bf16[128,1280]{1,0:T(8,128)(2,1)}, bf16[128,1280]{1,0:T(8,128)(2,1)}, u32[]{:S(2)}, u32[]{:S(2)}) collective-permute-start(bf16[128,1280]{1,0:T(8,128)(2,1)} %once.11), channel_id=1, source_target_pairs={{0,32},{16,48},{32,64},{48,80},{64,96},{80,112},{96,0},{112,16},{1... | collective-permute-start | bytes 983048 | tf_op jit(solution)/shard_map/ppermute | solution.py:388
  66.6 8.8 %collective-permute-start.6 = (bf16[128,1280]{1,0:T(8,128)(2,1)}, bf16[128,1280]{1,0:T(8,128)(2,1)}, u32[]{:S(2)}, u32[]{:S(2)}) collective-permute-start(bf16[128,1280]{1,0:T(8,128)(2,1)} %once.13.refs_3_.refs_5_), channel_id=1, source_target_pairs={{0,96},{16,112},{32,0},{48,16},{64,32},{80,48},{96,64},{112,80},{1... | collective-permute-start | bytes 983048 | tf_op jit(solution)/shard_map/ppermute | solution.py:395
  69.3 7.5 %collective-permute-start.7 = (bf16[128,1280]{1,0:T(8,128)(2,1)}, bf16[128,1280]{1,0:T(8,128)(2,1)}, u32[]{:S(2)}, u32[]{:S(2)}) collective-permute-start(bf16[128,1280]{1,0:T(8,128)(2,1)} %once.12.refs_2_.refs_10_), channel_id=1, source_target_pairs={{0,32},{16,48},{32,64},{48,80},{64,96},{80,112},{96,0},{112,16},{1... | collective-permute-start | bytes 983048 | tf_op jit(solution)/shard_map/ppermute | solution.py:395
  69.3 6.1 %collective-permute-start.5 = (bf16[80,1024]{1,0:T(8,128)(2,1)}, bf16[80,1024]{1,0:T(8,128)(2,1)}, u32[]{:S(2)}, u32[]{:S(2)}) collective-permute-start(bf16[80,1024]{1,0:T(8,128)(2,1)} %once.15), channel_id=1, source_target_pairs={{0,16},{16,0},{32,48},{48,32},{64,80},{80,64},{96,112},{112,96},{1... | collective-permute-start | bytes 491528 | tf_op jit(solution)/shard_map/ppermute | solution.py:398
  76.7 30.3 %all-to-all-start.2 = ((bf16[8,2,3,160,128]{4,3,2,1,0:T(8,128)(2,1)}), bf16[8,2,3,160,128]{4,3,2,1,0:T(8,128)(2,1)}, u32[]{:S(2)}, u32[]{:S(2)}) async-start(bf16[8,2,3,160,128]{4,3,2,1,0:T(8,128)(2,1)} %bitcast.55), calls=%async_computation.2 | async-start | bytes 3932160 | tf_op jit(solution)/shard_map/all_to_all | solution.py:400
  85.2 6.4 %collective-permute-start.8 = (bf16[4,4,112,128]{3,2,1,0:T(8,128)(2,1)}, bf16[4,4,112,128]{3,2,1,0:T(8,128)(2,1)S(1)}, u32[]{:S(2)}, u32[]{:S(2)}) collective-permute-start(bf16[4,4,112,128]{3,2,1,0:T(8,128)(2,1)} %get-tuple-element.31), channel_id=1, source_target_pairs={{0,1},{1,0},{2,3},{3,2},{4,5},{5,4},{6,7},{7,6},{8,9},{9,8},{10,11... | collective-permute-start | bytes 1376264 | tf_op jit(solution)/shard_map/ppermute | solution.py:405
  92.8 8.7 %collective-permute-start.11 = (bf16[4,112,128]{2,1,0:T(8,128)(2,1)S(1)}, bf16[4,112,128]{2,1,0:T(8,128)(2,1)S(1)}, u32[]{:S(2)}, u32[]{:S(2)}) collective-permute-start(bf16[4,112,128]{2,1,0:T(8,128)(2,1)S(1)} %get-tuple-element.33), channel_id=1, source_target_pairs={{0,12},{1,13},{2,14},{3,15},{4,8},{5,9},{6,10},{7,11},{8,4},{9,5},... | collective-permute-start | bytes 344072 | tf_op jit(solution)/shard_map/ppermute | solution.py:408
  96.6 5.6 %collective-permute-start.10 = (bf16[4,112,128]{2,1,0:T(8,128)(2,1)S(1)}, bf16[4,112,128]{2,1,0:T(8,128)(2,1)S(1)}, u32[]{:S(2)}, u32[]{:S(2)}) collective-permute-start(bf16[4,112,128]{2,1,0:T(8,128)(2,1)S(1)} %get-tuple-element.34), channel_id=1, source_target_pairs={{0,8},{1,9},{2,10},{3,11},{4,12},{5,13},{6,14},{7,15},{8,0},{9,1},... | collective-permute-start | bytes 344072 | tf_op jit(solution)/shard_map/ppermute | solution.py:408
  96.6 6.2 %collective-permute-start.9 = (bf16[4,112,128]{2,1,0:T(8,128)(2,1)S(1)}, bf16[4,112,128]{2,1,0:T(8,128)(2,1)S(1)}, u32[]{:S(2)}, u32[]{:S(2)}) collective-permute-start(bf16[4,112,128]{2,1,0:T(8,128)(2,1)S(1)} %get-tuple-element.35), channel_id=1, source_target_pairs={{0,4},{1,5},{2,6},{3,7},{4,0},{5,1},{6,2},{7,3},{8,12},{9,13},{10,... | collective-permute-start | bytes 344072 | tf_op jit(solution)/shard_map/ppermute | solution.py:408
  102.8 4.7 %collective-permute-start.12 = (bf16[112,128]{1,0:T(8,128)(2,1)S(1)}, bf16[112,128]{1,0:T(8,128)(2,1)S(1)}, u32[]{:S(2)}, u32[]{:S(2)}) collective-permute-start(bf16[112,128]{1,0:T(8,128)(2,1)S(1)} %get-tuple-element.36), channel_id=1, source_target_pairs={{0,2},{1,3},{2,0},{3,1},{4,6},{5,7},{6,4},{7,5},{8,10},{9,11},{10,... | collective-permute-start | bytes 86024 | tf_op jit(solution)/shard_map/ppermute | solution.py:412
  103.3 4.7 %collective-permute-start.14 = (bf16[112,128]{1,0:T(8,128)(2,1)S(1)}, bf16[112,128]{1,0:T(8,128)(2,1)S(1)}, u32[]{:S(2)}, u32[]{:S(2)}) collective-permute-start(bf16[112,128]{1,0:T(8,128)(2,1)S(1)} %get-tuple-element.37), channel_id=1, source_target_pairs={{0,18},{1,19},{2,16},{3,17},{4,22},{5,23},{6,20},{7,21},{8,26},{9,... | collective-permute-start | bytes 86024 | tf_op jit(solution)/shard_map/ppermute | solution.py:412
  106.3 4.3 %collective-permute-start.13 = (bf16[112,128]{1,0:T(8,128)(2,1)S(1)}, bf16[112,128]{1,0:T(8,128)(2,1)S(1)}, u32[]{:S(2)}, u32[]{:S(2)}) collective-permute-start(bf16[112,128]{1,0:T(8,128)(2,1)S(1)} %get-tuple-element.38), channel_id=1, source_target_pairs={{0,16},{1,17},{2,18},{3,19},{4,20},{5,21},{6,22},{7,23},{8,24},{9,... | collective-permute-start | bytes 86024 | tf_op jit(solution)/shard_map/ppermute | solution.py:412
  112.8 32.1 %all-to-all-start.3 = ((bf16[64,112,128]{2,1,0:T(8,128)(2,1)}), bf16[64,112,128]{2,1,0:T(8,128)(2,1)}, u32[]{:S(2)}, u32[]{:S(2)}) async-start(bf16[64,112,128]{2,1,0:T(8,128)(2,1)} %broadcast_in_dim.18), calls=%async_computation.3 | async-start | bytes 3670016 | tf_op jit(solution)/shard_map/all_to_all | solution.py:418
  144.8 7.2 %collective-permute-start.15 = (bf16[8,896,128]{2,1,0:T(8,128)(2,1)}, bf16[8,896,128]{2,1,0:T(8,128)(2,1)S(1)}, u32[]{:S(2)}, u32[]{:S(2)}) collective-permute-start(bf16[8,896,128]{2,1,0:T(8,128)(2,1)} %bitcast.25.in_ref), channel_id=1, source_target_pairs={{0,1},{1,0},{2,3},{3,2},{4,5},{5,4},{6,7},{7,6},{8,9},{9,8},{10,11... | collective-permute-start | bytes 5505032 | tf_op jit(solution)/shard_map/ppermute | solution.py:421

commit v5 on v4

--- a/solution.py
+++ b/solution.py
@@ -239,7 +239,7 @@
     )(received)
 
 
-CROWS = 112
+CROWS = 104
 
 
 def weight_kernel(me_ref, column_ref, *refs):
@@ -263,7 +263,7 @@
     blocks = []
     for j in range(0, width, 2 * BLK):
         right = jnp.concatenate([ref[:, j : j + 2 * BLK] for ref in grads_refs], axis=0)
-        blocks.append(nn(left, right).astype(bf16))
+        blocks.append(nn(left, right))
     product = jnp.concatenate(blocks, axis=1)
     per_core = product.shape[1] // BLK // 2
     for which in range(2):
@@ -272,13 +272,14 @@
                 rows_ref[j * PAIR : (j + 1) * PAIR, :] = product[
                     which * PAIR : (which + 1) * PAIR, columns_of(half * per_core + j)
                 ]
-            rows_ref[per_core * PAIR :, :] = jnp.zeros((8 * CROWS - per_core * PAIR, BLK), bf16)
+            rows_ref[per_core * PAIR :, :] = jnp.zeros((8 * CROWS - per_core * PAIR, BLK), f32)
 
             def store(out_ref):
                 for j in range(8):
                     along_z = lax.bitwise_xor(z, j // 2)
                     along_y = which * 2 + lax.bitwise_xor(low, j % 2)
-                    out_ref[along_z, along_y] = rows_ref[j * CROWS : (j + 1) * CROWS, :]
+                    chunk = rows_ref[j * CROWS : (j + 1) * CROWS, :]
+                    out_ref[along_z, along_y] = chunk.astype(bf16)
 
             pl.when(core == half)(lambda: store(out_refs[0]))
             pl.when(core != half)(lambda: store(out_refs[1]))
@@ -294,7 +295,7 @@
         scratch_shapes=[
             pltpu.VMEM((2 * PAIR, atts[0].shape[1]), bf16),
             pltpu.VMEM((2 * PAIR, atts[0].shape[1]), bf16),
-            pltpu.VMEM((8 * CROWS, BLK), bf16),
+            pltpu.VMEM((8 * CROWS, BLK), f32),
         ],
         compiler_params=pltpu.CompilerParams(vmem_limit_bytes=65408 * 2**10),
         cost_estimate=pl.CostEstimate(

time: 154 us -> 152 us (0.987)
  waiting for transfers between devices: 54.9 us -> 52.6 us
    all_to_all x1, waiting for transfers between devices: 21.4 us -> 19.8 us  [per_device(): lax.all_to_all(copies, both, 0, 0, axis_index_groups=same_core, tiled=True)]
where the time goes in v5:
time: 152 us
  waiting for transfers between devices  52.6 us (35%)
  starting transfers between devices  52 us (34%)
  Pallas kernels  43.1 us (28%)
  other arithmetic  1.89 us (1%)
    pallas_call x2, Pallas kernels, attention(): pl.pallas_call(attention_kernel, grid=(1,), in_specs=[smem, smem, whole(p...  23.3 us
    all_to_all x1, waiting for transfers between devices, per_device(): lax.all_to_all(copies, both, 0, 0, axis_index_groups=same_core, tiled=True)  19.8 us
    all_to_all x1, waiting for transfers between devices, per_device(): first = lax.all_to_all(packed_first, 'grp', 0, 0, tiled=True).reshape(shape)  15.6 us
    all_to_all x1, starting transfers between devices, per_device(): lax.all_to_all(copies, both, 0, 0, axis_index_groups=same_core, tiled=True)  7.71 us
    all_to_all x1, starting transfers between devices, per_device(): first = lax.all_to_all(packed_first, 'grp', 0, 0, tiled=True).reshape(shape)  7.47 us
    pallas_call x2, Pallas kernels, pack(): pl.pallas_call(functools.partial(pack_kernel, copies), grid=(1,), in_spec...  7.3 us
    ppermute x1, waiting for transfers between devices, per_device(): other = lax.ppermute(send, 'grp', side)  5.71 us
    ppermute x3, waiting for transfers between devices, per_device(): lax.ppermute(parts[k], 'dp', [(i, i ^ 4 * k) for i in range(16)])  5.15 us
  transfers between devices with their start and end apart: 20, of which 11 were waited for; matrix products, arithmetic and copies ran while one was open for 1% of the time, Pallas kernels for 25%

profile of v5, /device:TPU:1, one launch (start us, length us, event | category | flops | bytes accessed | tf_op | source)
XLA Modules:
  0.0 151.8 jit_solution(18399955006613880789)
XLA Ops:
  0.6 3.6 %pack_heads.2.refs_0_ = bf16[8,2,4,80,128]{4,3,2,1,0:T(8,128)(2,1)} custom-call(bf16[1280,1280]{1,0:T(8,128)(2,1)} %weight_ref.3, bf16[256,1280]{1,0:T(8,128)(2,1)} %bitcast.56, bf16[256,1280]{1,0:T(8,128)(2,1)} %bitcast.59, bf16[256,1280]{1,0:T(8,128)(2,1)} %bitcast.61, bf16[256,1280]{1,0:T(8,128)(2,1)} %bitcast.63), custom_call_target="tpu_custom_call" | custom-call | flops 419430400 | bytes 5242880 | tf_op jit(solution)/shard_map/pack_heads/pallas_call | solution.py:89
  4.2 7.5 %all-to-all-start = ((bf16[8,2,4,80,128]{4,3,2,1,0:T(8,128)(2,1)}), bf16[8,2,4,80,128]{4,3,2,1,0:T(8,128)(2,1)}, u32[]{:S(2)}, u32[]{:S(2)}) async-start(bf16[8,2,4,80,128]{4,3,2,1,0:T(8,128)(2,1)} %pack_heads.2.refs_0_), calls=%async_computation | async-start | bytes 2621440 | tf_op jit(solution)/shard_map/all_to_all | solution.py:382
  11.7 3.7 %pack_heads.3 = (bf16[8,2,4,80,128]{4,3,2,1,0:T(8,128)(2,1)}, bf16[128,1280]{1,0:T(8,128)(2,1)}, bf16[128,1280]{1,0:T(8,128)(2,1)}) custom-call(bf16[1280,1280]{1,0:T(8,128)(2,1)} %weight_ref.3, bf16[256,1280]{1,0:T(8,128)(2,1)} %bitcast.57, bf16[256,1280]{1,0:T(8,128)(2,1)} %bitcast.60, bf16[256,1280]{1,0:T(8,128)(2,1)} %bitcast.62, ...), custom_call_target="tpu_custom_call" | custom-call | flops 419430400 | bytes 5242880 | tf_op jit(solution)/shard_map/pack_heads/pallas_call | solution.py:89
  15.4 15.6 %all-to-all-done = bf16[8,2,4,80,128]{4,3,2,1,0:T(8,128)(2,1)} async-done(((bf16[8,2,4,80,128]{4,3,2,1,0:T(8,128)(2,1)}), bf16[8,2,4,80,128]{4,3,2,1,0:T(8,128)(2,1)}, u32[]{:S(2)}, u32[]{:S(2)}) %all-to-all-start) | async-done | bytes 1310752 | tf_op jit(solution)/shard_map/all_to_all | solution.py:382
  31.0 4.3 %all-to-all-start.1 = ((bf16[8,2,4,80,128]{4,3,2,1,0:T(8,128)(2,1)}), bf16[8,2,4,80,128]{4,3,2,1,0:T(8,128)(2,1)}, u32[]{:S(2)}, u32[]{:S(2)}) async-start(bf16[8,2,4,80,128]{4,3,2,1,0:T(8,128)(2,1)} %once.9), calls=%async_computation.1 | async-start | bytes 2621440 | tf_op jit(solution)/shard_map/all_to_all | solution.py:384
  35.3 11.7 %attention_grads.2 = (bf16[80,1024]{1,0:T(8,128)(2,1)}, bf16[80,1024]{1,0:T(8,128)(2,1)}, bf16[16,3,160,128]{3,2,1,0:T(8,128)(2,1)}) custom-call(s32[1,16]{1,0:T(1,128)} %ids_ref.3, s32[1]{0:T(128)} %bitcast.me_ref, bf16[16,4,80,128]{3,2,1,0:T(8,128)(2,1)} %bitcast.5.refs_1_.in_ref), custom_call_target="tpu_custom_call" | custom-call | flops 12079595520 | bytes 4194304 | tf_op jit(solution)/shard_map/attention_grads/pallas_call | solution.py:195
  46.9 2.8 %collective-permute-start.4 = (bf16[80,1024]{1,0:T(8,128)(2,1)}, bf16[80,1024]{1,0:T(8,128)(2,1)}, u32[]{:S(2)}, u32[]{:S(2)}) collective-permute-start(bf16[80,1024]{1,0:T(8,128)(2,1)} %get-tuple-element.23.refs_1_), channel_id=1, source_target_pairs={{0,16},{16,0},{32,48},{48,32},{64,80},{80,64},{96,112},{112,96},{1... | collective-permute-start | bytes 491528 | tf_op jit(solution)/shard_map/ppermute | solution.py:393
  49.8 2.4 %collective-permute-start.2 = (bf16[128,1280]{1,0:T(8,128)(2,1)}, bf16[128,1280]{1,0:T(8,128)(2,1)}, u32[]{:S(2)}, u32[]{:S(2)}) collective-permute-start(bf16[128,1280]{1,0:T(8,128)(2,1)} %once.10), channel_id=1, source_target_pairs={{0,96},{16,112},{32,0},{48,16},{64,32},{80,48},{96,64},{112,80},{1... | collective-permute-start | bytes 983048 | tf_op jit(solution)/shard_map/ppermute | solution.py:390
  52.2 2.7 %collective-permute-start.3 = (bf16[128,1280]{1,0:T(8,128)(2,1)}, bf16[128,1280]{1,0:T(8,128)(2,1)}, u32[]{:S(2)}, u32[]{:S(2)}) collective-permute-start(bf16[128,1280]{1,0:T(8,128)(2,1)} %once.11), channel_id=1, source_target_pairs={{0,96},{16,112},{32,0},{48,16},{64,32},{80,48},{96,64},{112,80},{1... | collective-permute-start | bytes 983048 | tf_op jit(solution)/shard_map/ppermute | solution.py:390
  54.9 11.7 %attention_grads.3 = (bf16[80,1024]{1,0:T(8,128)(2,1)}, bf16[80,1024]{1,0:T(8,128)(2,1)}, bf16[16,3,160,128]{3,2,1,0:T(8,128)(2,1)}) custom-call(s32[1,16]{1,0:T(1,128)} %ids_ref.3, s32[1]{0:T(128)} %bitcast.me_ref, bf16[16,4,80,128]{3,2,1,0:T(8,128)(2,1)} %bitcast.6.in_ref, ...), custom_call_target="tpu_custom_call", output_to_operand_aliasing={{2}: (3, {})} | custom-call | flops 12079595520 | bytes 4194304 | tf_op jit(solution)/shard_map/attention_grads/pallas_call | solution.py:195
  66.6 2.7 %collective-permute-start.6 = (bf16[128,1280]{1,0:T(8,128)(2,1)}, bf16[128,1280]{1,0:T(8,128)(2,1)}, u32[]{:S(2)}, u32[]{:S(2)}) collective-permute-start(bf16[128,1280]{1,0:T(8,128)(2,1)} %once.13.refs_3_.refs_5_), channel_id=1, source_target_pairs={{0,96},{16,112},{32,0},{48,16},{64,32},{80,48},{96,64},{112,80},{1... | collective-permute-start | bytes 983048 | tf_op jit(solution)/shard_map/ppermute | solution.py:396
  69.7 5.7 %collective-permute-done.5.refs_1_.refs_3_ = bf16[80,1024]{1,0:T(8,128)(2,1)} collective-permute-done((bf16[80,1024]{1,0:T(8,128)(2,1)}, bf16[80,1024]{1,0:T(8,128)(2,1)}, u32[]{:S(2)}, u32[]{:S(2)}) %collective-permute-start.5) | collective-permute-done | bytes 163872 | tf_op jit(solution)/shard_map/ppermute | solution.py:399
  76.7 4.3 %all-to-all-start.2 = ((bf16[8,2,3,160,128]{4,3,2,1,0:T(8,128)(2,1)}), bf16[8,2,3,160,128]{4,3,2,1,0:T(8,128)(2,1)}, u32[]{:S(2)}, u32[]{:S(2)}) async-start(bf16[8,2,3,160,128]{4,3,2,1,0:T(8,128)(2,1)} %bitcast.55), calls=%async_computation.2 | async-start | bytes 3932160 | tf_op jit(solution)/shard_map/all_to_all | solution.py:401
  81.1 4.1 %weight_terms.1 = (bf16[4,4,104,128]{3,2,1,0:T(8,128)(2,1)}, bf16[4,4,104,128]{3,2,1,0:T(8,128)(2,1)}) custom-call(s32[1]{0:T(128)} %bitcast.me_ref, s32[1]{0:T(128)} %bitcast.12.column_ref, bf16[80,1024]{1,0:T(8,128)(2,1)} %get-tuple-element.28.refs_0_, bf16[80,1024]{1,0:T(8,128)(2,1)} %get-tuple-element.29.refs_1_, ...), custom_call_target="tpu_custom_call" | custom-call | flops 838860800 | bytes 6291456 | tf_op jit(solution)/shard_map/weight_terms/pallas_call | solution.py:290
  85.2 4.7 %collective-permute-start.8 = (bf16[4,4,104,128]{3,2,1,0:T(8,128)(2,1)}, bf16[4,4,104,128]{3,2,1,0:T(8,128)(2,1)S(1)}, u32[]{:S(2)}, u32[]{:S(2)}) collective-permute-start(bf16[4,4,104,128]{3,2,1,0:T(8,128)(2,1)} %get-tuple-element.31), channel_id=1, source_target_pairs={{0,1},{1,0},{2,3},{3,2},{4,5},{5,4},{6,7},{7,6},{8,9},{9,8},{10,11... | collective-permute-start | bytes 1277960 | tf_op jit(solution)/shard_map/ppermute | solution.py:406
  92.7 3.9 %collective-permute-start.11 = (bf16[4,104,128]{2,1,0:T(8,128)(2,1)S(1)}, bf16[4,104,128]{2,1,0:T(8,128)(2,1)S(1)}, u32[]{:S(2)}, u32[]{:S(2)}) collective-permute-start(bf16[4,104,128]{2,1,0:T(8,128)(2,1)S(1)} %get-tuple-element.33), channel_id=1, source_target_pairs={{0,12},{1,13},{2,14},{3,15},{4,8},{5,9},{6,10},{7,11},{8,4},{9,5},... | collective-permute-start | bytes 319496 | tf_op jit(solution)/shard_map/ppermute | solution.py:409
  97.2 3.8 %collective-permute-done.11 = bf16[4,104,128]{2,1,0:T(8,128)(2,1)S(1)} collective-permute-done((bf16[4,104,128]{2,1,0:T(8,128)(2,1)S(1)}, bf16[4,104,128]{2,1,0:T(8,128)(2,1)S(1)}, u32[]{:S(2)}, u32[]{:S(2)}) %collective-permute-start.11) | collective-permute-done | bytes 106528 | tf_op jit(solution)/shard_map/ppermute | solution.py:409
  102.9 3.0 %collective-permute-start.14 = (bf16[104,128]{1,0:T(8,128)(2,1)S(1)}, bf16[104,128]{1,0:T(8,128)(2,1)S(1)}, u32[]{:S(2)}, u32[]{:S(2)}) collective-permute-start(bf16[104,128]{1,0:T(8,128)(2,1)S(1)} %get-tuple-element.37), channel_id=1, source_target_pairs={{0,18},{1,19},{2,16},{3,17},{4,22},{5,23},{6,20},{7,21},{8,26},{9,... | collective-permute-start | bytes 79880 | tf_op jit(solution)/shard_map/ppermute | solution.py:413
  108.0 2.2 %collective-permute-done.13 = bf16[104,128]{1,0:T(8,128)(2,1)S(1)} collective-permute-done((bf16[104,128]{1,0:T(8,128)(2,1)S(1)}, bf16[104,128]{1,0:T(8,128)(2,1)S(1)}, u32[]{:S(2)}, u32[]{:S(2)}) %collective-permute-start.13) | collective-permute-done | bytes 26656 | tf_op jit(solution)/shard_map/ppermute | solution.py:413
  112.2 7.7 %all-to-all-start.3 = ((bf16[64,104,128]{2,1,0:T(8,128)(2,1)}), bf16[64,104,128]{2,1,0:T(8,128)(2,1)}, u32[]{:S(2)}, u32[]{:S(2)}) async-start(bf16[64,104,128]{2,1,0:T(8,128)(2,1)} %broadcast_in_dim.18), calls=%async_computation.3 | async-start | bytes 3407872 | tf_op jit(solution)/shard_map/all_to_all | solution.py:419
  119.9 3.0 %unpack_heads.1 = (bf16[256,1280]{1,0:T(8,128)(2,1)}, bf16[256,1280]{1,0:T(8,128)(2,1)}, bf16[256,1280]{1,0:T(8,128)(2,1)}) custom-call(bf16[8,2,3,160,128]{4,3,2,1,0:T(8,128)(2,1)} %all-to-all-done.2.in_ref.refs_0_), custom_call_target="tpu_custom_call" | custom-call | bytes 4194304 | tf_op jit(solution)/shard_map/unpack_heads/pallas_call | solution.py:233
  122.9 19.8 %all-to-all-done.3.refs_0_ = bf16[64,104,128]{2,1,0:T(8,128)(2,1)} async-done(((bf16[64,104,128]{2,1,0:T(8,128)(2,1)}), bf16[64,104,128]{2,1,0:T(8,128)(2,1)}, u32[]{:S(2)}, u32[]{:S(2)}) %all-to-all-start.3) | async-done | bytes 1703968 | tf_op jit(solution)/shard_map/all_to_all | solution.py:419
  142.7 3.8 %collective-permute-start.15 = (bf16[8,832,128]{2,1,0:T(8,128)(2,1)}, bf16[8,832,128]{2,1,0:T(8,128)(2,1)S(1)}, u32[]{:S(2)}, u32[]{:S(2)}) collective-permute-start(bf16[8,832,128]{2,1,0:T(8,128)(2,1)} %bitcast.25.in_ref), channel_id=1, source_target_pairs={{0,1},{1,0},{2,3},{3,2},{4,5},{5,4},{6,7},{7,6},{8,9},{9,8},{10,11... | collective-permute-start | bytes 5111816 | tf_op jit(solution)/shard_map/ppermute | solution.py:422
  146.6 3.0 %finish_weight.2.refs_0_ = f32[2,8,80,1280]{3,2,1,0:T(8,128)} custom-call(s32[1]{0:T(128)} %bitcast.26.core_ref, bf16[8,832,128]{2,1,0:T(8,128)(2,1)} %bitcast.25.in_ref), custom_call_target="tpu_custom_call" | custom-call | bytes 5242880 | tf_op jit(solution)/shard_map/finish_weight/pallas_call | solution.py:352
  (38 shorter events, 13.4 us)
Async XLA Ops:
  4.2 26.8 %all-to-all-start = ((bf16[8,2,4,80,128]{4,3,2,1,0:T(8,128)(2,1)}), bf16[8,2,4,80,128]{4,3,2,1,0:T(8,128)(2,1)}, u32[]{:S(2)}, u32[]{:S(2)}) async-start(bf16[8,2,4,80,128]{4,3,2,1,0:T(8,128)(2,1)} %pack_heads.2.refs_0_), calls=%async_computation | async-start | bytes 2621440 | tf_op jit(solution)/shard_map/all_to_all | solution.py:382
  31.0 23.9 %all-to-all-start.1 = ((bf16[8,2,4,80,128]{4,3,2,1,0:T(8,128)(2,1)}), bf16[8,2,4,80,128]{4,3,2,1,0:T(8,128)(2,1)}, u32[]{:S(2)}, u32[]{:S(2)}) async-start(bf16[8,2,4,80,128]{4,3,2,1,0:T(8,128)(2,1)} %once.9), calls=%async_computation.1 | async-start | bytes 2621440 | tf_op jit(solution)/shard_map/all_to_all | solution.py:384
  46.9 22.3 %collective-permute-start.4 = (bf16[80,1024]{1,0:T(8,128)(2,1)}, bf16[80,1024]{1,0:T(8,128)(2,1)}, u32[]{:S(2)}, u32[]{:S(2)}) collective-permute-start(bf16[80,1024]{1,0:T(8,128)(2,1)} %get-tuple-element.23.refs_1_), channel_id=1, source_target_pairs={{0,16},{16,0},{32,48},{48,32},{64,80},{80,64},{96,112},{112,96},{1... | collective-permute-start | bytes 491528 | tf_op jit(solution)/shard_map/ppermute | solution.py:393
  49.8 16.8 %collective-permute-start.2 = (bf16[128,1280]{1,0:T(8,128)(2,1)}, bf16[128,1280]{1,0:T(8,128)(2,1)}, u32[]{:S(2)}, u32[]{:S(2)}) collective-permute-start(bf16[128,1280]{1,0:T(8,128)(2,1)} %once.10), channel_id=1, source_target_pairs={{0,96},{16,112},{32,0},{48,16},{64,32},{80,48},{96,64},{112,80},{1... | collective-permute-start | bytes 983048 | tf_op jit(solution)/shard_map/ppermute | solution.py:390
  52.2 17.0 %collective-permute-start = (bf16[128,1280]{1,0:T(8,128)(2,1)}, bf16[128,1280]{1,0:T(8,128)(2,1)}, u32[]{:S(2)}, u32[]{:S(2)}) collective-permute-start(bf16[128,1280]{1,0:T(8,128)(2,1)} %once.10), channel_id=1, source_target_pairs={{0,32},{16,48},{32,64},{48,80},{64,96},{80,112},{96,0},{112,16},{1... | collective-permute-start | bytes 983048 | tf_op jit(solution)/shard_map/ppermute | solution.py:389
  52.2 17.0 %collective-permute-start.3 = (bf16[128,1280]{1,0:T(8,128)(2,1)}, bf16[128,1280]{1,0:T(8,128)(2,1)}, u32[]{:S(2)}, u32[]{:S(2)}) collective-permute-start(bf16[128,1280]{1,0:T(8,128)(2,1)} %once.11), channel_id=1, source_target_pairs={{0,96},{16,112},{32,0},{48,16},{64,32},{80,48},{96,64},{112,80},{1... | collective-permute-start | bytes 983048 | tf_op jit(solution)/shard_map/ppermute | solution.py:390
  54.9 14.4 %collective-permute-start.1 = (bf16[128,1280]{1,0:T(8,128)(2,1)}, bf16[128,1280]{1,0:T(8,128)(2,1)}, u32[]{:S(2)}, u32[]{:S(2)}) collective-permute-start(bf16[128,1280]{1,0:T(8,128)(2,1)} %once.11), channel_id=1, source_target_pairs={{0,32},{16,48},{32,64},{48,80},{64,96},{80,112},{96,0},{112,16},{1... | collective-permute-start | bytes 983048 | tf_op jit(solution)/shard_map/ppermute | solution.py:389
  66.6 8.8 %collective-permute-start.6 = (bf16[128,1280]{1,0:T(8,128)(2,1)}, bf16[128,1280]{1,0:T(8,128)(2,1)}, u32[]{:S(2)}, u32[]{:S(2)}) collective-permute-start(bf16[128,1280]{1,0:T(8,128)(2,1)} %once.13.refs_3_.refs_5_), channel_id=1, source_target_pairs={{0,96},{16,112},{32,0},{48,16},{64,32},{80,48},{96,64},{112,80},{1... | collective-permute-start | bytes 983048 | tf_op jit(solution)/shard_map/ppermute | solution.py:396
  69.3 7.5 %collective-permute-start.7 = (bf16[128,1280]{1,0:T(8,128)(2,1)}, bf16[128,1280]{1,0:T(8,128)(2,1)}, u32[]{:S(2)}, u32[]{:S(2)}) collective-permute-start(bf16[128,1280]{1,0:T(8,128)(2,1)} %once.12.refs_2_.refs_10_), channel_id=1, source_target_pairs={{0,32},{16,48},{32,64},{48,80},{64,96},{80,112},{96,0},{112,16},{1... | collective-permute-start | bytes 983048 | tf_op jit(solution)/shard_map/ppermute | solution.py:396
  69.3 6.1 %collective-permute-start.5 = (bf16[80,1024]{1,0:T(8,128)(2,1)}, bf16[80,1024]{1,0:T(8,128)(2,1)}, u32[]{:S(2)}, u32[]{:S(2)}) collective-permute-start(bf16[80,1024]{1,0:T(8,128)(2,1)} %once.15), channel_id=1, source_target_pairs={{0,16},{16,0},{32,48},{48,32},{64,80},{80,64},{96,112},{112,96},{1... | collective-permute-start | bytes 491528 | tf_op jit(solution)/shard_map/ppermute | solution.py:399
  76.7 29.9 %all-to-all-start.2 = ((bf16[8,2,3,160,128]{4,3,2,1,0:T(8,128)(2,1)}), bf16[8,2,3,160,128]{4,3,2,1,0:T(8,128)(2,1)}, u32[]{:S(2)}, u32[]{:S(2)}) async-start(bf16[8,2,3,160,128]{4,3,2,1,0:T(8,128)(2,1)} %bitcast.55), calls=%async_computation.2 | async-start | bytes 3932160 | tf_op jit(solution)/shard_map/all_to_all | solution.py:401
  85.2 6.3 %collective-permute-start.8 = (bf16[4,4,104,128]{3,2,1,0:T(8,128)(2,1)}, bf16[4,4,104,128]{3,2,1,0:T(8,128)(2,1)S(1)}, u32[]{:S(2)}, u32[]{:S(2)}) collective-permute-start(bf16[4,4,104,128]{3,2,1,0:T(8,128)(2,1)} %get-tuple-element.31), channel_id=1, source_target_pairs={{0,1},{1,0},{2,3},{3,2},{4,5},{5,4},{6,7},{7,6},{8,9},{9,8},{10,11... | collective-permute-start | bytes 1277960 | tf_op jit(solution)/shard_map/ppermute | solution.py:406
  92.7 8.3 %collective-permute-start.11 = (bf16[4,104,128]{2,1,0:T(8,128)(2,1)S(1)}, bf16[4,104,128]{2,1,0:T(8,128)(2,1)S(1)}, u32[]{:S(2)}, u32[]{:S(2)}) collective-permute-start(bf16[4,104,128]{2,1,0:T(8,128)(2,1)S(1)} %get-tuple-element.33), channel_id=1, source_target_pairs={{0,12},{1,13},{2,14},{3,15},{4,8},{5,9},{6,10},{7,11},{8,4},{9,5},... | collective-permute-start | bytes 319496 | tf_op jit(solution)/shard_map/ppermute | solution.py:409
  96.6 5.4 %collective-permute-start.10 = (bf16[4,104,128]{2,1,0:T(8,128)(2,1)S(1)}, bf16[4,104,128]{2,1,0:T(8,128)(2,1)S(1)}, u32[]{:S(2)}, u32[]{:S(2)}) collective-permute-start(bf16[4,104,128]{2,1,0:T(8,128)(2,1)S(1)} %get-tuple-element.34), channel_id=1, source_target_pairs={{0,8},{1,9},{2,10},{3,11},{4,12},{5,13},{6,14},{7,15},{8,0},{9,1},... | collective-permute-start | bytes 319496 | tf_op jit(solution)/shard_map/ppermute | solution.py:409
  96.6 5.8 %collective-permute-start.9 = (bf16[4,104,128]{2,1,0:T(8,128)(2,1)S(1)}, bf16[4,104,128]{2,1,0:T(8,128)(2,1)S(1)}, u32[]{:S(2)}, u32[]{:S(2)}) collective-permute-start(bf16[4,104,128]{2,1,0:T(8,128)(2,1)S(1)} %get-tuple-element.35), channel_id=1, source_target_pairs={{0,4},{1,5},{2,6},{3,7},{4,0},{5,1},{6,2},{7,3},{8,12},{9,13},{10,... | collective-permute-start | bytes 319496 | tf_op jit(solution)/shard_map/ppermute | solution.py:409
  102.4 4.7 %collective-permute-start.12 = (bf16[104,128]{1,0:T(8,128)(2,1)S(1)}, bf16[104,128]{1,0:T(8,128)(2,1)S(1)}, u32[]{:S(2)}, u32[]{:S(2)}) collective-permute-start(bf16[104,128]{1,0:T(8,128)(2,1)S(1)} %get-tuple-element.36), channel_id=1, source_target_pairs={{0,2},{1,3},{2,0},{3,1},{4,6},{5,7},{6,4},{7,5},{8,10},{9,11},{10,... | collective-permute-start | bytes 79880 | tf_op jit(solution)/shard_map/ppermute | solution.py:413
  102.9 5.1 %collective-permute-start.14 = (bf16[104,128]{1,0:T(8,128)(2,1)S(1)}, bf16[104,128]{1,0:T(8,128)(2,1)S(1)}, u32[]{:S(2)}, u32[]{:S(2)}) collective-permute-start(bf16[104,128]{1,0:T(8,128)(2,1)S(1)} %get-tuple-element.37), channel_id=1, source_target_pairs={{0,18},{1,19},{2,16},{3,17},{4,22},{5,23},{6,20},{7,21},{8,26},{9,... | collective-permute-start | bytes 79880 | tf_op jit(solution)/shard_map/ppermute | solution.py:413
  105.9 4.2 %collective-permute-start.13 = (bf16[104,128]{1,0:T(8,128)(2,1)S(1)}, bf16[104,128]{1,0:T(8,128)(2,1)S(1)}, u32[]{:S(2)}, u32[]{:S(2)}) collective-permute-start(bf16[104,128]{1,0:T(8,128)(2,1)S(1)} %get-tuple-element.38), channel_id=1, source_target_pairs={{0,16},{1,17},{2,18},{3,19},{4,20},{5,21},{6,22},{7,23},{8,24},{9,... | collective-permute-start | bytes 79880 | tf_op jit(solution)/shard_map/ppermute | solution.py:413
  112.2 30.5 %all-to-all-start.3 = ((bf16[64,104,128]{2,1,0:T(8,128)(2,1)}), bf16[64,104,128]{2,1,0:T(8,128)(2,1)}, u32[]{:S(2)}, u32[]{:S(2)}) async-start(bf16[64,104,128]{2,1,0:T(8,128)(2,1)} %broadcast_in_dim.18), calls=%async_computation.3 | async-start | bytes 3407872 | tf_op jit(solution)/shard_map/all_to_all | solution.py:419
  142.7 7.2 %collective-permute-start.15 = (bf16[8,832,128]{2,1,0:T(8,128)(2,1)}, bf16[8,832,128]{2,1,0:T(8,128)(2,1)S(1)}, u32[]{:S(2)}, u32[]{:S(2)}) collective-permute-start(bf16[8,832,128]{2,1,0:T(8,128)(2,1)} %bitcast.25.in_ref), channel_id=1, source_target_pairs={{0,1},{1,0},{2,3},{3,2},{4,5},{5,4},{6,7},{7,6},{8,9},{9,8},{10,11... | collective-permute-start | bytes 5111816 | tf_op jit(solution)/shard_map/ppermute | solution.py:422

commit v6 on v5

--- a/solution.py
+++ b/solution.py
@@ -323,21 +323,6 @@
     )(array, *after)
 
 
-def one_kernel(*refs):
-    refs[-1][0, 0] = 1.0
-
-
-def one_after(*after):
-    return pl.pallas_call(
-        one_kernel,
-        in_specs=[pl.BlockSpec(memory_space=pltpu.HBM)] * len(after),
-        out_specs=pl.BlockSpec(memory_space=pltpu.SMEM),
-        out_shape=jax.ShapeDtypeStruct((1, 1), f32),
-        cost_estimate=pl.CostEstimate(flops=0, bytes_accessed=0, transcendentals=0),
-        name="one_after",
-    )(*after)
-
-
 def finish_kernel(core_ref, in_ref, *refs):
     out_ref = refs[-1]
     for pair in range(in_ref.shape[0]):
@@ -394,8 +379,7 @@
     grads_right[0] = once(grads_right[0], send)
     grads_left[1] = once(grads_left[1], send)
     grads_far = [lax.ppermute(grads_right[0], "grp", down), lax.ppermute(grads_left[1], "grp", up)]
-    send = once(send, *grads_left, *grads_right)
-    send = once(send, other_first)
+    send = once(send, other_first, *grads_left, *grads_right)
     other = lax.ppermute(send, "grp", side)
     out = once(out, other, *grads_far)
     back = lax.all_to_all(out.reshape(8, 2, 3, PAIR, BLK), "grp", 0, 0, tiled=True)
@@ -413,7 +397,7 @@
         lax.ppermute(parts[k], both, [(i, i ^ (16 * (k // 2) + 2 * (k % 2))) for i in range(128)])
         for k in range(1, 4)
     ]
-    part = (sum(item.astype(f32) for item in parts) * one_after(back)).astype(bf16)
+    part = sum(item.astype(f32) for item in parts).astype(bf16)
     copies = jnp.broadcast_to(part[None], (64,) + part.shape)
     same_core = [[i * 2 + c for i in range(64)] for c in range(2)]
     own = lax.all_to_all(copies, both, 0, 0, axis_index_groups=same_core, tiled=True)

time: 152 us -> 152 us (level)
  no operation moved by 1% of the time
where the time goes in v6:
time: 152 us; the launch traced here: 151 us
  waiting for transfers between devices  53.1 us (35%)
  starting transfers between devices  52 us (34%)
  Pallas kernels  42.6 us (28%)
    pallas_call x2, Pallas kernels, attention(): pl.pallas_call(attention_kernel, grid=(1,), in_specs=[smem, smem, whole(p...  23.3 us
    all_to_all x1, waiting for transfers between devices, per_device(): lax.all_to_all(copies, both, 0, 0, axis_index_groups=same_core, tiled=True)  19.8 us
    all_to_all x1, waiting for transfers between devices, per_device(): first = lax.all_to_all(packed_first, 'grp', 0, 0, tiled=True).reshape(shape)  15.6 us
    all_to_all x1, starting transfers between devices, per_device(): lax.all_to_all(copies, both, 0, 0, axis_index_groups=same_core, tiled=True)  7.7 us
    all_to_all x1, starting transfers between devices, per_device(): first = lax.all_to_all(packed_first, 'grp', 0, 0, tiled=True).reshape(shape)  7.47 us
    pallas_call x2, Pallas kernels, pack(): pl.pallas_call(functools.partial(pack_kernel, copies), grid=(1,), in_spec...  7.3 us
    ppermute x1, waiting for transfers between devices, per_device(): other = lax.ppermute(send, 'grp', side)  5.7 us
    ppermute x3, waiting for transfers between devices, per_device(): lax.ppermute(parts[k], 'dp', [(i, i ^ 4 * k) for i in range(16)])  5.15 us
  transfers between devices with their start and end apart: 20, of which 11 were waited for; matrix products, arithmetic and copies ran while one was open for 1% of the time, Pallas kernels for 25%

profile of v6, /device:TPU:1, one launch (start us, length us, event | category | flops | bytes accessed | tf_op | source)
XLA Modules:
  0.0 151.2 jit_solution(6841286587848285443)
XLA Ops:
  0.6 3.6 %pack_heads.2.refs_0_ = bf16[8,2,4,80,128]{4,3,2,1,0:T(8,128)(2,1)} custom-call(bf16[1280,1280]{1,0:T(8,128)(2,1)} %weight_ref.3, bf16[256,1280]{1,0:T(8,128)(2,1)} %bitcast.55, bf16[256,1280]{1,0:T(8,128)(2,1)} %bitcast.58, bf16[256,1280]{1,0:T(8,128)(2,1)} %bitcast.60, bf16[256,1280]{1,0:T(8,128)(2,1)} %bitcast.62), custom_call_target="tpu_custom_call" | custom-call | flops 419430400 | bytes 5242880 | tf_op jit(solution)/shard_map/pack_heads/pallas_call | solution.py:89
  4.2 7.5 %all-to-all-start = ((bf16[8,2,4,80,128]{4,3,2,1,0:T(8,128)(2,1)}), bf16[8,2,4,80,128]{4,3,2,1,0:T(8,128)(2,1)}, u32[]{:S(2)}, u32[]{:S(2)}) async-start(bf16[8,2,4,80,128]{4,3,2,1,0:T(8,128)(2,1)} %pack_heads.2.refs_0_), calls=%async_computation | async-start | bytes 2621440 | tf_op jit(solution)/shard_map/all_to_all | solution.py:367
  11.7 3.7 %pack_heads.3 = (bf16[8,2,4,80,128]{4,3,2,1,0:T(8,128)(2,1)}, bf16[128,1280]{1,0:T(8,128)(2,1)}, bf16[128,1280]{1,0:T(8,128)(2,1)}) custom-call(bf16[1280,1280]{1,0:T(8,128)(2,1)} %weight_ref.3, bf16[256,1280]{1,0:T(8,128)(2,1)} %bitcast.56, bf16[256,1280]{1,0:T(8,128)(2,1)} %bitcast.59, bf16[256,1280]{1,0:T(8,128)(2,1)} %bitcast.61, ...), custom_call_target="tpu_custom_call" | custom-call | flops 419430400 | bytes 5242880 | tf_op jit(solution)/shard_map/pack_heads/pallas_call | solution.py:89
  15.4 15.6 %all-to-all-done = bf16[8,2,4,80,128]{4,3,2,1,0:T(8,128)(2,1)} async-done(((bf16[8,2,4,80,128]{4,3,2,1,0:T(8,128)(2,1)}), bf16[8,2,4,80,128]{4,3,2,1,0:T(8,128)(2,1)}, u32[]{:S(2)}, u32[]{:S(2)}) %all-to-all-start) | async-done | bytes 1310752 | tf_op jit(solution)/shard_map/all_to_all | solution.py:367
  31.0 4.3 %all-to-all-start.1 = ((bf16[8,2,4,80,128]{4,3,2,1,0:T(8,128)(2,1)}), bf16[8,2,4,80,128]{4,3,2,1,0:T(8,128)(2,1)}, u32[]{:S(2)}, u32[]{:S(2)}) async-start(bf16[8,2,4,80,128]{4,3,2,1,0:T(8,128)(2,1)} %once.8), calls=%async_computation.1 | async-start | bytes 2621440 | tf_op jit(solution)/shard_map/all_to_all | solution.py:369
  35.3 11.7 %attention_grads.2 = (bf16[80,1024]{1,0:T(8,128)(2,1)}, bf16[80,1024]{1,0:T(8,128)(2,1)}, bf16[16,3,160,128]{3,2,1,0:T(8,128)(2,1)}) custom-call(s32[1,16]{1,0:T(1,128)} %ids_ref.3, s32[1]{0:T(128)} %bitcast.me_ref, bf16[16,4,80,128]{3,2,1,0:T(8,128)(2,1)} %bitcast.5.refs_1_.in_ref), custom_call_target="tpu_custom_call" | custom-call | flops 12079595520 | bytes 4194304 | tf_op jit(solution)/shard_map/attention_grads/pallas_call | solution.py:195
  47.0 2.8 %collective-permute-start = (bf16[80,1024]{1,0:T(8,128)(2,1)}, bf16[80,1024]{1,0:T(8,128)(2,1)}, u32[]{:S(2)}, u32[]{:S(2)}) collective-permute-start(bf16[80,1024]{1,0:T(8,128)(2,1)} %get-tuple-element.22.refs_1_), channel_id=1, source_target_pairs={{0,16},{16,0},{32,48},{48,32},{64,80},{80,64},{96,112},{112,96},{1... | collective-permute-start | bytes 491528 | tf_op jit(solution)/shard_map/ppermute | solution.py:378
  49.8 2.4 %collective-permute-start.3 = (bf16[128,1280]{1,0:T(8,128)(2,1)}, bf16[128,1280]{1,0:T(8,128)(2,1)}, u32[]{:S(2)}, u32[]{:S(2)}) collective-permute-start(bf16[128,1280]{1,0:T(8,128)(2,1)} %once.9), channel_id=1, source_target_pairs={{0,96},{16,112},{32,0},{48,16},{64,32},{80,48},{96,64},{112,80},{1... | collective-permute-start | bytes 983048 | tf_op jit(solution)/shard_map/ppermute | solution.py:375
  52.2 2.7 %collective-permute-start.4 = (bf16[128,1280]{1,0:T(8,128)(2,1)}, bf16[128,1280]{1,0:T(8,128)(2,1)}, u32[]{:S(2)}, u32[]{:S(2)}) collective-permute-start(bf16[128,1280]{1,0:T(8,128)(2,1)} %once.10), channel_id=1, source_target_pairs={{0,96},{16,112},{32,0},{48,16},{64,32},{80,48},{96,64},{112,80},{1... | collective-permute-start | bytes 983048 | tf_op jit(solution)/shard_map/ppermute | solution.py:375
  54.9 11.7 %attention_grads.3 = (bf16[80,1024]{1,0:T(8,128)(2,1)}, bf16[80,1024]{1,0:T(8,128)(2,1)}, bf16[16,3,160,128]{3,2,1,0:T(8,128)(2,1)}) custom-call(s32[1,16]{1,0:T(1,128)} %ids_ref.3, s32[1]{0:T(128)} %bitcast.me_ref, bf16[16,4,80,128]{3,2,1,0:T(8,128)(2,1)} %bitcast.6.in_ref, ...), custom_call_target="tpu_custom_call", output_to_operand_aliasing={{2}: (3, {})} | custom-call | flops 12079595520 | bytes 4194304 | tf_op jit(solution)/shard_map/attention_grads/pallas_call | solution.py:195
  66.6 2.7 %collective-permute-start.6 = (bf16[128,1280]{1,0:T(8,128)(2,1)}, bf16[128,1280]{1,0:T(8,128)(2,1)}, u32[]{:S(2)}, u32[]{:S(2)}) collective-permute-start(bf16[128,1280]{1,0:T(8,128)(2,1)} %once.12.refs_4_.refs_5_), channel_id=1, source_target_pairs={{0,96},{16,112},{32,0},{48,16},{64,32},{80,48},{96,64},{112,80},{1... | collective-permute-start | bytes 983048 | tf_op jit(solution)/shard_map/ppermute | solution.py:381
  69.7 5.7 %collective-permute-done.5.refs_1_.refs_3_ = bf16[80,1024]{1,0:T(8,128)(2,1)} collective-permute-done((bf16[80,1024]{1,0:T(8,128)(2,1)}, bf16[80,1024]{1,0:T(8,128)(2,1)}, u32[]{:S(2)}, u32[]{:S(2)}) %collective-permute-start.5) | collective-permute-done | bytes 163872 | tf_op jit(solution)/shard_map/ppermute | solution.py:383
  76.7 4.3 %all-to-all-start.2 = ((bf16[8,2,3,160,128]{4,3,2,1,0:T(8,128)(2,1)}), bf16[8,2,3,160,128]{4,3,2,1,0:T(8,128)(2,1)}, u32[]{:S(2)}, u32[]{:S(2)}) async-start(bf16[8,2,3,160,128]{4,3,2,1,0:T(8,128)(2,1)} %bitcast.54), calls=%async_computation.2 | async-start | bytes 3932160 | tf_op jit(solution)/shard_map/all_to_all | solution.py:385
  81.1 4.1 %weight_terms.1 = (bf16[4,4,104,128]{3,2,1,0:T(8,128)(2,1)}, bf16[4,4,104,128]{3,2,1,0:T(8,128)(2,1)}) custom-call(s32[1]{0:T(128)} %bitcast.me_ref, s32[1]{0:T(128)} %bitcast.12.column_ref, bf16[80,1024]{1,0:T(8,128)(2,1)} %get-tuple-element.28.refs_0_, bf16[80,1024]{1,0:T(8,128)(2,1)} %get-tuple-element.29.refs_1_, ...), custom_call_target="tpu_custom_call" | custom-call | flops 838860800 | bytes 6291456 | tf_op jit(solution)/shard_map/weight_terms/pallas_call | solution.py:290
  85.2 4.7 %collective-permute-start.8 = (bf16[4,4,104,128]{3,2,1,0:T(8,128)(2,1)}, bf16[4,4,104,128]{3,2,1,0:T(8,128)(2,1)S(1)}, u32[]{:S(2)}, u32[]{:S(2)}) collective-permute-start(bf16[4,4,104,128]{3,2,1,0:T(8,128)(2,1)} %get-tuple-element.31), channel_id=1, source_target_pairs={{0,1},{1,0},{2,3},{3,2},{4,5},{5,4},{6,7},{7,6},{8,9},{9,8},{10,11... | collective-permute-start | bytes 1277960 | tf_op jit(solution)/shard_map/ppermute | solution.py:390
  92.7 3.9 %collective-permute-start.11 = (bf16[4,104,128]{2,1,0:T(8,128)(2,1)S(1)}, bf16[4,104,128]{2,1,0:T(8,128)(2,1)S(1)}, u32[]{:S(2)}, u32[]{:S(2)}) collective-permute-start(bf16[4,104,128]{2,1,0:T(8,128)(2,1)S(1)} %get-tuple-element.33), channel_id=1, source_target_pairs={{0,12},{1,13},{2,14},{3,15},{4,8},{5,9},{6,10},{7,11},{8,4},{9,5},... | collective-permute-start | bytes 319496 | tf_op jit(solution)/shard_map/ppermute | solution.py:393
  97.2 3.8 %collective-permute-done.11 = bf16[4,104,128]{2,1,0:T(8,128)(2,1)S(1)} collective-permute-done((bf16[4,104,128]{2,1,0:T(8,128)(2,1)S(1)}, bf16[4,104,128]{2,1,0:T(8,128)(2,1)S(1)}, u32[]{:S(2)}, u32[]{:S(2)}) %collective-permute-start.11) | collective-permute-done | bytes 106528 | tf_op jit(solution)/shard_map/ppermute | solution.py:393
  102.9 3.0 %collective-permute-start.14 = (bf16[104,128]{1,0:T(8,128)(2,1)S(1)}, bf16[104,128]{1,0:T(8,128)(2,1)S(1)}, u32[]{:S(2)}, u32[]{:S(2)}) collective-permute-start(bf16[104,128]{1,0:T(8,128)(2,1)S(1)} %get-tuple-element.37), channel_id=1, source_target_pairs={{0,18},{1,19},{2,16},{3,17},{4,22},{5,23},{6,20},{7,21},{8,26},{9,... | collective-permute-start | bytes 79880 | tf_op jit(solution)/shard_map/ppermute | solution.py:397
  108.0 2.2 %collective-permute-done.13 = bf16[104,128]{1,0:T(8,128)(2,1)S(1)} collective-permute-done((bf16[104,128]{1,0:T(8,128)(2,1)S(1)}, bf16[104,128]{1,0:T(8,128)(2,1)S(1)}, u32[]{:S(2)}, u32[]{:S(2)}) %collective-permute-start.13) | collective-permute-done | bytes 26656 | tf_op jit(solution)/shard_map/ppermute | solution.py:397
  111.6 7.7 %all-to-all-start.3 = ((bf16[64,104,128]{2,1,0:T(8,128)(2,1)}), bf16[64,104,128]{2,1,0:T(8,128)(2,1)}, u32[]{:S(2)}, u32[]{:S(2)}) async-start(bf16[64,104,128]{2,1,0:T(8,128)(2,1)} %broadcast_in_dim.18), calls=%async_computation.3 | async-start | bytes 3407872 | tf_op jit(solution)/shard_map/all_to_all | solution.py:403
  119.3 3.0 %unpack_heads.1 = (bf16[256,1280]{1,0:T(8,128)(2,1)}, bf16[256,1280]{1,0:T(8,128)(2,1)}, bf16[256,1280]{1,0:T(8,128)(2,1)}) custom-call(bf16[8,2,3,160,128]{4,3,2,1,0:T(8,128)(2,1)} %all-to-all-done.2.in_ref), custom_call_target="tpu_custom_call" | custom-call | bytes 4194304 | tf_op jit(solution)/shard_map/unpack_heads/pallas_call | solution.py:233
  122.3 19.8 %all-to-all-done.3.refs_0_ = bf16[64,104,128]{2,1,0:T(8,128)(2,1)} async-done(((bf16[64,104,128]{2,1,0:T(8,128)(2,1)}), bf16[64,104,128]{2,1,0:T(8,128)(2,1)}, u32[]{:S(2)}, u32[]{:S(2)}) %all-to-all-start.3) | async-done | bytes 1703968 | tf_op jit(solution)/shard_map/all_to_all | solution.py:403
  142.1 3.8 %collective-permute-start.15 = (bf16[8,832,128]{2,1,0:T(8,128)(2,1)}, bf16[8,832,128]{2,1,0:T(8,128)(2,1)S(1)}, u32[]{:S(2)}, u32[]{:S(2)}) collective-permute-start(bf16[8,832,128]{2,1,0:T(8,128)(2,1)} %bitcast.24.in_ref), channel_id=1, source_target_pairs={{0,1},{1,0},{2,3},{3,2},{4,5},{5,4},{6,7},{7,6},{8,9},{9,8},{10,11... | collective-permute-start | bytes 5111816 | tf_op jit(solution)/shard_map/ppermute | solution.py:406
  145.9 3.0 %finish_weight.2.refs_0_ = f32[2,8,80,1280]{3,2,1,0:T(8,128)} custom-call(s32[1]{0:T(128)} %bitcast.25.core_ref, bf16[8,832,128]{2,1,0:T(8,128)(2,1)} %bitcast.24.in_ref), custom_call_target="tpu_custom_call" | custom-call | bytes 5242880 | tf_op jit(solution)/shard_map/finish_weight/pallas_call | solution.py:337
  (36 shorter events, 12.8 us)
Async XLA Ops:
  4.2 26.8 %all-to-all-start = ((bf16[8,2,4,80,128]{4,3,2,1,0:T(8,128)(2,1)}), bf16[8,2,4,80,128]{4,3,2,1,0:T(8,128)(2,1)}, u32[]{:S(2)}, u32[]{:S(2)}) async-start(bf16[8,2,4,80,128]{4,3,2,1,0:T(8,128)(2,1)} %pack_heads.2.refs_0_), calls=%async_computation | async-start | bytes 2621440 | tf_op jit(solution)/shard_map/all_to_all | solution.py:367
  31.0 23.9 %all-to-all-start.1 = ((bf16[8,2,4,80,128]{4,3,2,1,0:T(8,128)(2,1)}), bf16[8,2,4,80,128]{4,3,2,1,0:T(8,128)(2,1)}, u32[]{:S(2)}, u32[]{:S(2)}) async-start(bf16[8,2,4,80,128]{4,3,2,1,0:T(8,128)(2,1)} %once.8), calls=%async_computation.1 | async-start | bytes 2621440 | tf_op jit(solution)/shard_map/all_to_all | solution.py:369
  47.0 22.3 %collective-permute-start = (bf16[80,1024]{1,0:T(8,128)(2,1)}, bf16[80,1024]{1,0:T(8,128)(2,1)}, u32[]{:S(2)}, u32[]{:S(2)}) collective-permute-start(bf16[80,1024]{1,0:T(8,128)(2,1)} %get-tuple-element.22.refs_1_), channel_id=1, source_target_pairs={{0,16},{16,0},{32,48},{48,32},{64,80},{80,64},{96,112},{112,96},{1... | collective-permute-start | bytes 491528 | tf_op jit(solution)/shard_map/ppermute | solution.py:378
  49.8 16.8 %collective-permute-start.3 = (bf16[128,1280]{1,0:T(8,128)(2,1)}, bf16[128,1280]{1,0:T(8,128)(2,1)}, u32[]{:S(2)}, u32[]{:S(2)}) collective-permute-start(bf16[128,1280]{1,0:T(8,128)(2,1)} %once.9), channel_id=1, source_target_pairs={{0,96},{16,112},{32,0},{48,16},{64,32},{80,48},{96,64},{112,80},{1... | collective-permute-start | bytes 983048 | tf_op jit(solution)/shard_map/ppermute | solution.py:375
  52.2 17.1 %collective-permute-start.1 = (bf16[128,1280]{1,0:T(8,128)(2,1)}, bf16[128,1280]{1,0:T(8,128)(2,1)}, u32[]{:S(2)}, u32[]{:S(2)}) collective-permute-start(bf16[128,1280]{1,0:T(8,128)(2,1)} %once.9), channel_id=1, source_target_pairs={{0,32},{16,48},{32,64},{48,80},{64,96},{80,112},{96,0},{112,16},{1... | collective-permute-start | bytes 983048 | tf_op jit(solution)/shard_map/ppermute | solution.py:374
  52.2 17.1 %collective-permute-start.4 = (bf16[128,1280]{1,0:T(8,128)(2,1)}, bf16[128,1280]{1,0:T(8,128)(2,1)}, u32[]{:S(2)}, u32[]{:S(2)}) collective-permute-start(bf16[128,1280]{1,0:T(8,128)(2,1)} %once.10), channel_id=1, source_target_pairs={{0,96},{16,112},{32,0},{48,16},{64,32},{80,48},{96,64},{112,80},{1... | collective-permute-start | bytes 983048 | tf_op jit(solution)/shard_map/ppermute | solution.py:375
  54.9 14.4 %collective-permute-start.2 = (bf16[128,1280]{1,0:T(8,128)(2,1)}, bf16[128,1280]{1,0:T(8,128)(2,1)}, u32[]{:S(2)}, u32[]{:S(2)}) collective-permute-start(bf16[128,1280]{1,0:T(8,128)(2,1)} %once.10), channel_id=1, source_target_pairs={{0,32},{16,48},{32,64},{48,80},{64,96},{80,112},{96,0},{112,16},{1... | collective-permute-start | bytes 983048 | tf_op jit(solution)/shard_map/ppermute | solution.py:374
  66.6 8.8 %collective-permute-start.6 = (bf16[128,1280]{1,0:T(8,128)(2,1)}, bf16[128,1280]{1,0:T(8,128)(2,1)}, u32[]{:S(2)}, u32[]{:S(2)}) collective-permute-start(bf16[128,1280]{1,0:T(8,128)(2,1)} %once.12.refs_4_.refs_5_), channel_id=1, source_target_pairs={{0,96},{16,112},{32,0},{48,16},{64,32},{80,48},{96,64},{112,80},{1... | collective-permute-start | bytes 983048 | tf_op jit(solution)/shard_map/ppermute | solution.py:381
  69.3 7.5 %collective-permute-start.7 = (bf16[128,1280]{1,0:T(8,128)(2,1)}, bf16[128,1280]{1,0:T(8,128)(2,1)}, u32[]{:S(2)}, u32[]{:S(2)}) collective-permute-start(bf16[128,1280]{1,0:T(8,128)(2,1)} %once.11.refs_3_.refs_10_), channel_id=1, source_target_pairs={{0,32},{16,48},{32,64},{48,80},{64,96},{80,112},{96,0},{112,16},{1... | collective-permute-start | bytes 983048 | tf_op jit(solution)/shard_map/ppermute | solution.py:381
  69.3 6.1 %collective-permute-start.5 = (bf16[80,1024]{1,0:T(8,128)(2,1)}, bf16[80,1024]{1,0:T(8,128)(2,1)}, u32[]{:S(2)}, u32[]{:S(2)}) collective-permute-start(bf16[80,1024]{1,0:T(8,128)(2,1)} %once.13), channel_id=1, source_target_pairs={{0,16},{16,0},{32,48},{48,32},{64,80},{80,64},{96,112},{112,96},{1... | collective-permute-start | bytes 491528 | tf_op jit(solution)/shard_map/ppermute | solution.py:383
  76.7 33.4 %all-to-all-start.2 = ((bf16[8,2,3,160,128]{4,3,2,1,0:T(8,128)(2,1)}), bf16[8,2,3,160,128]{4,3,2,1,0:T(8,128)(2,1)}, u32[]{:S(2)}, u32[]{:S(2)}) async-start(bf16[8,2,3,160,128]{4,3,2,1,0:T(8,128)(2,1)} %bitcast.54), calls=%async_computation.2 | async-start | bytes 3932160 | tf_op jit(solution)/shard_map/all_to_all | solution.py:385
  85.2 6.3 %collective-permute-start.8 = (bf16[4,4,104,128]{3,2,1,0:T(8,128)(2,1)}, bf16[4,4,104,128]{3,2,1,0:T(8,128)(2,1)S(1)}, u32[]{:S(2)}, u32[]{:S(2)}) collective-permute-start(bf16[4,4,104,128]{3,2,1,0:T(8,128)(2,1)} %get-tuple-element.31), channel_id=1, source_target_pairs={{0,1},{1,0},{2,3},{3,2},{4,5},{5,4},{6,7},{7,6},{8,9},{9,8},{10,11... | collective-permute-start | bytes 1277960 | tf_op jit(solution)/shard_map/ppermute | solution.py:390
  92.7 8.3 %collective-permute-start.11 = (bf16[4,104,128]{2,1,0:T(8,128)(2,1)S(1)}, bf16[4,104,128]{2,1,0:T(8,128)(2,1)S(1)}, u32[]{:S(2)}, u32[]{:S(2)}) collective-permute-start(bf16[4,104,128]{2,1,0:T(8,128)(2,1)S(1)} %get-tuple-element.33), channel_id=1, source_target_pairs={{0,12},{1,13},{2,14},{3,15},{4,8},{5,9},{6,10},{7,11},{8,4},{9,5},... | collective-permute-start | bytes 319496 | tf_op jit(solution)/shard_map/ppermute | solution.py:393
  96.6 5.4 %collective-permute-start.10 = (bf16[4,104,128]{2,1,0:T(8,128)(2,1)S(1)}, bf16[4,104,128]{2,1,0:T(8,128)(2,1)S(1)}, u32[]{:S(2)}, u32[]{:S(2)}) collective-permute-start(bf16[4,104,128]{2,1,0:T(8,128)(2,1)S(1)} %get-tuple-element.34), channel_id=1, source_target_pairs={{0,8},{1,9},{2,10},{3,11},{4,12},{5,13},{6,14},{7,15},{8,0},{9,1},... | collective-permute-start | bytes 319496 | tf_op jit(solution)/shard_map/ppermute | solution.py:393
  96.6 5.8 %collective-permute-start.9 = (bf16[4,104,128]{2,1,0:T(8,128)(2,1)S(1)}, bf16[4,104,128]{2,1,0:T(8,128)(2,1)S(1)}, u32[]{:S(2)}, u32[]{:S(2)}) collective-permute-start(bf16[4,104,128]{2,1,0:T(8,128)(2,1)S(1)} %get-tuple-element.35), channel_id=1, source_target_pairs={{0,4},{1,5},{2,6},{3,7},{4,0},{5,1},{6,2},{7,3},{8,12},{9,13},{10,... | collective-permute-start | bytes 319496 | tf_op jit(solution)/shard_map/ppermute | solution.py:393
  102.4 4.2 %collective-permute-start.12 = (bf16[104,128]{1,0:T(8,128)(2,1)S(1)}, bf16[104,128]{1,0:T(8,128)(2,1)S(1)}, u32[]{:S(2)}, u32[]{:S(2)}) collective-permute-start(bf16[104,128]{1,0:T(8,128)(2,1)S(1)} %get-tuple-element.36), channel_id=1, source_target_pairs={{0,2},{1,3},{2,0},{3,1},{4,6},{5,7},{6,4},{7,5},{8,10},{9,11},{10,... | collective-permute-start | bytes 79880 | tf_op jit(solution)/shard_map/ppermute | solution.py:397
  102.9 5.1 %collective-permute-start.14 = (bf16[104,128]{1,0:T(8,128)(2,1)S(1)}, bf16[104,128]{1,0:T(8,128)(2,1)S(1)}, u32[]{:S(2)}, u32[]{:S(2)}) collective-permute-start(bf16[104,128]{1,0:T(8,128)(2,1)S(1)} %get-tuple-element.37), channel_id=1, source_target_pairs={{0,18},{1,19},{2,16},{3,17},{4,22},{5,23},{6,20},{7,21},{8,26},{9,... | collective-permute-start | bytes 79880 | tf_op jit(solution)/shard_map/ppermute | solution.py:397
  105.9 4.2 %collective-permute-start.13 = (bf16[104,128]{1,0:T(8,128)(2,1)S(1)}, bf16[104,128]{1,0:T(8,128)(2,1)S(1)}, u32[]{:S(2)}, u32[]{:S(2)}) collective-permute-start(bf16[104,128]{1,0:T(8,128)(2,1)S(1)} %get-tuple-element.38), channel_id=1, source_target_pairs={{0,16},{1,17},{2,18},{3,19},{4,20},{5,21},{6,22},{7,23},{8,24},{9,... | collective-permute-start | bytes 79880 | tf_op jit(solution)/shard_map/ppermute | solution.py:397
  111.6 30.5 %all-to-all-start.3 = ((bf16[64,104,128]{2,1,0:T(8,128)(2,1)}), bf16[64,104,128]{2,1,0:T(8,128)(2,1)}, u32[]{:S(2)}, u32[]{:S(2)}) async-start(bf16[64,104,128]{2,1,0:T(8,128)(2,1)} %broadcast_in_dim.18), calls=%async_computation.3 | async-start | bytes 3407872 | tf_op jit(solution)/shard_map/all_to_all | solution.py:403
  142.1 7.2 %collective-permute-start.15 = (bf16[8,832,128]{2,1,0:T(8,128)(2,1)}, bf16[8,832,128]{2,1,0:T(8,128)(2,1)S(1)}, u32[]{:S(2)}, u32[]{:S(2)}) collective-permute-start(bf16[8,832,128]{2,1,0:T(8,128)(2,1)} %bitcast.24.in_ref), channel_id=1, source_target_pairs={{0,1},{1,0},{2,3},{3,2},{4,5},{5,4},{6,7},{7,6},{8,9},{9,8},{10,11... | collective-permute-start | bytes 5111816 | tf_op jit(solution)/shard_map/ppermute | solution.py:406
